TPU v7x, 32 devices: a whole 2x2x4 slice. The times are simulated.
32 devices in a mesh: leaf: 8 (over z, x), front: 4 (over y, core).
Axes of the slice: x: 2, y: 2, z: 4, core: 2. Of those that a mesh axis runs over, the one named last changes fastest.
Arguments:
- child_update: bfloat16 [8, 4, 1, 3, 256, 3072], P('leaf', 'front'), may hold values from -60 to 60, as said below
- sep_one: bfloat16 [8, 4, 1, 4, 256, 512], P('leaf', 'front'), may hold values from -60 to 60, as said below
- sep_two: bfloat16 [8, 4, 1, 4, 256, 256], P('leaf', 'front'), may hold values from -60 to 60, as said below
- map_one: int32 [8, 1, 4, 3], replicated, may hold values from 0 to 3, as said below
- map_two: int32 [4, 1, 4, 3], replicated, may hold values from 0 to 3, as said below
- mask_one: int32 [4, 1, 12, 4], replicated, may hold values 0 or 1
- mask_two: int32 [2, 1, 12, 4], replicated, may hold values 0 or 1
Outputs:
- factor_one: float32 [8, 4, 1, 4, 256, 512], P('leaf', 'front')
- factor_two: float32 [8, 4, 1, 4, 256, 256], P('leaf', 'front')
- update_two: bfloat16 [8, 4, 1, 3, 256, 768], P('leaf', 'front')
Inputs may be any that keep to these rules, and one draw needn't show every extreme that they name: `child_update`: every child[l,b] is symmetric positive definite. `sep_one`: the top 1024 rows of each front's initial entries form a symmetric positive definite block, and every assembled front is positive definite. `sep_two`: the top 1024 rows of each front's initial entries form a symmetric positive definite block, and every assembled front is positive definite. `map_one`: for each child, batch and j the 3 entries are distinct; the two children 2p and 2p + 1 leave out different slots, so every parent tile receives one or two child tiles. `map_two`: for each first-level front, batch and j the 3 entries are distinct; fronts 2q and 2q + 1 leave out different slots, so every parent tile receives one or two child tiles.
All inputs are finite; a program needn't handle non-finite values.
Results may differ from a plain program's by a relative error of at most 0.0047.
Values may be sent and summed in bfloat16 or wider, within the bound.
No kernel may reach another device: no remote copies, remote signals or barrier semaphores. Data moves between devices by JAX's collectives and lax.ppermute only.
A program may use at most 192 MiB of HBM per device.

v0:
```python
import functools

import jax
import jax.numpy as jnp
from jax import lax
from jax.experimental import pallas as pl
from jax.experimental.pallas import tpu as pltpu
from jax.sharding import PartitionSpec as P

VMEM = pl.BlockSpec(memory_space=pltpu.VMEM)
SMEM = pl.BlockSpec(memory_space=pltpu.SMEM)
ANY = pl.BlockSpec(memory_space=pl.ANY)
GROUPS = 4
PARAMS = pltpu.CompilerParams(vmem_limit_bytes=32 * 2**20)
BLK = 128
GRP = 8
TILE = 256
NT = (((1,), (1,)), ((), ()))


def halves(x):
    high = x.astype(jnp.bfloat16)
    low = (x - high.astype(jnp.float32)).astype(jnp.bfloat16)
    return high, low


def left_parts(x):
    high, low = halves(x)
    return jnp.concatenate([high, low, high], axis=1)


def right_rows(x):
    high, low = halves(x)
    return jnp.concatenate([high, high, low], axis=0)


def right_lanes(x):
    high, low = halves(x)
    return jnp.concatenate([high, high, low], axis=1)


def dot_rows(left, right):
    return jnp.dot(left, right, preferred_element_type=jnp.float32)


def dot_lanes(left, right):
    return lax.dot_general(left, right, NT, preferred_element_type=jnp.float32)


def spread_row(ref, index):
    return jnp.broadcast_to(ref[index], (GRP, BLK))


def factor_diagonal(block, done_ref, pivot_ref, rows_ref):
    steps = BLK // GRP
    row_id = lax.broadcasted_iota(jnp.int32, (GRP, BLK), 0)
    lane_id = lax.broadcasted_iota(jnp.int32, (GRP, BLK), 1)
    matrix = [block[GRP * g : GRP * (g + 1), :] for g in range(steps)]
    inverse = [jnp.where(lane_id == row_id + GRP * g, 1.0, 0.0).astype(jnp.float32) for g in range(steps)]
    for g in range(steps):
        first = GRP * g
        slot = g % 2
        current = matrix[g]
        rows_ref[slot, :, 0:BLK] = current
        rows_ref[slot, :, BLK:] = inverse[g]
        for i in range(GRP):
            pivot_ref[slot, i] = jnp.broadcast_to(current[:, first + i : first + i + 1], (GRP, BLK))
        entry = {}
        for m in range(GRP):
            for i in range(m + 1):
                entry[m, i] = jnp.broadcast_to(pivot_ref[slot, i, m : m + 1, :], (GRP, BLK))
                entry[i, m] = entry[m, i]
        left = [jnp.broadcast_to(rows_ref[slot, m : m + 1, 0:BLK], (GRP, BLK)) for m in range(GRP)]
        right = [jnp.broadcast_to(rows_ref[slot, m : m + 1, BLK:], (GRP, BLK)) for m in range(GRP)]
        for i in range(GRP):
            root = lax.rsqrt(entry[i, i])
            scale = root * root
            done_ref[first + i : first + i + 1, 0:BLK] = (left[i] * root)[0:1]
            done_ref[first + i : first + i + 1, BLK:] = (right[i] * root)[0:1]
            left[i] = left[i] * scale
            right[i] = right[i] * scale
            scaled = {c: entry[i, c] * scale for c in range(i + 1, GRP)}
            for m in range(GRP):
                if m == i:
                    continue
                weight = entry[m, i]
                left[m] = left[m] - weight * left[i]
                right[m] = right[m] - weight * right[i]
                for c in range(i + 1, GRP):
                    if m > c:
                        continue
                    entry[m, c] = entry[m, c] - weight * scaled[c]
            for m in range(i + 1, GRP):
                for c in range(i + 1, m):
                    entry[m, c] = entry[c, m]
            for c in range(i + 1, GRP):
                entry[i, c] = scaled[c]
        for later in range(g + 1, steps):
            rows = matrix[later]
            total_left, total_right = None, None
            for i in range(GRP):
                weight = jnp.broadcast_to(rows[:, first + i : first + i + 1], (GRP, BLK))
                part_left, part_right = weight * left[i], weight * right[i]
                total_left = part_left if total_left is None else total_left + part_left
                total_right = part_right if total_right is None else total_right + part_right
            matrix[later] = rows - total_left
            inverse[later] = inverse[later] - total_right


def fill_one(ids_ref, packs, work):
    leaf, column = ids_ref[0], ids_ref[1]
    half = leaf & 1
    order = work.shape[1]
    own, core, y, y_core, x, x_core = packs[:6]
    for apart, mine, peers in (
        (0, own, (x,)),
        (1, core, (x_core,)),
        (2, y, packs[6:8]),
        (3, y_core, packs[8:10]),
    ):
        base = (column ^ apart) * TILE
        height = TILE // len(peers)
        for part, peer in enumerate(peers):
            rows = pl.ds(pl.multiple_of(base + part * height, height), height)
            piece = slice(part * height, (part + 1) * height)
            work[rows, :] = mine[piece, 0:order].astype(jnp.float32) + peer[:, 0:order].astype(jnp.float32)
            for place, ref, span in ((half, mine, piece), (1 - half, peer, slice(None))):
                columns = pl.ds(pl.multiple_of(place * (order // 2), order // 2), order // 2)
                work[rows, columns] = work[rows, columns] + ref[span, order:].astype(jnp.float32)


def fill_two(ids_ref, packs, work):
    leaf, column = ids_ref[0], ids_ref[1]
    half, side = leaf & 1, (leaf >> 1) & 1
    own, core, y, y_core, x, x_core = packs[:6]
    for apart, mine, peers in (
        (0, own, (x,)),
        (1, core, (x_core,)),
        (2, y, packs[6:8]),
        (3, y_core, packs[8:10]),
    ):
        base = (column ^ apart) * TILE
        for refs, last in (((mine,), 1 - half), (peers, half)):
            height = TILE // len(refs)
            for part, ref in enumerate(refs):
                rows = pl.ds(pl.multiple_of(base + part * height, height), height)
                for position, place in ((0, 2 * side + last), (1, 2 * (1 - side) + last)):
                    columns = pl.ds(pl.multiple_of(place * TILE, TILE), TILE)
                    work[rows, columns] = ref[:, position * TILE : (position + 1) * TILE]


def cholesky_kernel(fill, ids_ref, *refs):
    packs = refs[:10]
    lower_ref, inverse_ref, work, done, block_inverse, entries, rows = refs[10:]
    order = work.shape[0]
    blocks = order // BLK
    fill(ids_ref, packs, work)
    lower_ref[...] = jnp.zeros_like(lower_ref)
    row_id = lax.broadcasted_iota(jnp.int32, (BLK, BLK), 0)
    lane_id = lax.broadcasted_iota(jnp.int32, (BLK, BLK), 1)

    def step(k, carry):
        start = pl.multiple_of(k * BLK, BLK)
        span = pl.ds(start, BLK)
        factor_diagonal(work[span, span], done, entries, rows)
        upper = jnp.where(lane_id >= row_id, done[:, 0:BLK], 0.0)
        lower_ref[span, span] = upper.T
        block_inverse[k] = done[:, BLK:]
        for fixed in range(blocks - 1):
            after = (fixed + 1) * BLK

            @pl.when(k == fixed)
            def _():
                strip = dot_rows(
                    left_parts(done[:, BLK:]), right_rows(work[after - BLK : after, after:])
                )
                column = strip.T
                lower_ref[after:, after - BLK : after] = column
                left = left_parts(column)
                right = right_rows(strip)
                width = order - after
                for top in range(0, width, TILE):
                    high = min(TILE, width - top)
                    work[after + top : after + top + high, after + top :] = work[
                        after + top : after + top + high, after + top :
                    ] - dot_rows(left[top : top + high], right[:, top:])

        return carry

    lax.fori_loop(0, blocks, step, 0)
    for tile in range(order // TILE):
        base = tile * TILE
        first, second = block_inverse[2 * tile], block_inverse[2 * tile + 1]
        corner = lower_ref[base + BLK : base + TILE, base : base + BLK]
        mixed = dot_rows(left_parts(corner), right_rows(first))
        mixed = -dot_rows(left_parts(second), right_rows(mixed))
        inverse_ref[tile, 0:BLK, 0:BLK] = first
        inverse_ref[tile, 0:BLK, BLK:] = jnp.zeros((BLK, BLK), jnp.float32)
        inverse_ref[tile, BLK:, 0:BLK] = mixed
        inverse_ref[tile, BLK:, BLK:] = second


def cholesky(ids, packs, fill, order):
    return pl.pallas_call(
        functools.partial(cholesky_kernel, fill),
        out_shape=(
            jax.ShapeDtypeStruct((order, order), jnp.float32),
            jax.ShapeDtypeStruct((order // TILE, TILE, TILE), jnp.float32),
        ),
        in_specs=[SMEM] + [VMEM] * len(packs),
        out_specs=(VMEM, VMEM),
        scratch_shapes=[
            pltpu.VMEM((order, order), jnp.float32),
            pltpu.VMEM((BLK, 2 * BLK), jnp.float32),
            pltpu.VMEM((order // BLK, BLK, BLK), jnp.float32),
            pltpu.VMEM((2, GRP, GRP, BLK), jnp.float32),
            pltpu.VMEM((2, GRP, 2 * BLK), jnp.float32),
        ],
        compiler_params=pltpu.CompilerParams(vmem_limit_bytes=32 * 2**20),
        cost_estimate=pl.CostEstimate(flops=4 * 10**10, bytes_accessed=10**8, transcendentals=0),
        name="cholesky",
    )(ids, *packs)


def swapped(value, axis, apart):
    mask = 2**apart
    pairs = [(source, source ^ mask) for source in range(lax.axis_size(axis))]
    return lax.ppermute(value, axis, pairs)


def find_tile(map_ref, owner, group, slot, count):
    found = jnp.int32(-1)
    for s in range(count):
        found = jnp.where(map_ref[owner, group, s] == slot, jnp.int32(s), found)
    return found


def column_targets(half, side):
    targets = []
    for part in (side, 1 - side):
        targets.append(2 * part + 1 - half)
        targets += [4 + 3 * (2 * part + half) + i for i in range(3)]
    return targets


def share_place(target, half):
    place = jnp.int32(0)
    for other in column_targets(half, 0):
        earlier = jnp.logical_and((other & 3) == (target & 3), other < target)
        place = place + earlier.astype(jnp.int32)
    return place


def move_tile(live, source, target, sem):
    @pl.when(live)
    def _():
        pltpu.make_async_copy(source, target, sem).start()

    @pl.when(jnp.logical_not(live))
    def _():
        target[...] = jnp.zeros(target.shape, target.dtype)

    def wait():
        @pl.when(live)
        def _():
            pltpu.make_async_copy(source, target, sem).wait()

    return wait


def move_separator(leaf, column, map_ref, child_ref, slots, target_of, sems):
    count = child_ref.shape[0]
    waits = []
    for slot in slots:
        row = find_tile(map_ref, leaf, column, slot, count)
        for group in range(GROUPS):
            place = find_tile(map_ref, leaf, group, 0, count)
            live = jnp.logical_and(row >= 0, place >= 0)
            span = pl.ds(pl.multiple_of((jnp.maximum(place, 0) * GROUPS + group) * TILE, TILE), TILE)
            source = child_ref.at[jnp.maximum(row, 0), :, span]
            target = target_of(slot).at[:, pl.ds(group * TILE, TILE)]
            waits.append(move_tile(live, source, target, sems.at[len(waits)]))
    return waits


def pick_pivot_kernel(ids_ref, map_ref, child_ref, entries_ref, pivot_ref, sems, entry_sem):
    width = GROUPS * TILE
    entries = pltpu.make_async_copy(entries_ref.at[0], pivot_ref.at[:, pl.ds(width, width // 2)], entry_sem.at[0])
    entries.start()
    waits = move_separator(ids_ref[0], ids_ref[1], map_ref, child_ref, (0,), lambda slot: pivot_ref, sems)
    for wait in waits:
        wait()
    entries.wait()


def pick_pivot(ids, child_map, child, entries):
    width = GROUPS * TILE + entries.shape[-1]
    return pl.pallas_call(
        pick_pivot_kernel,
        out_shape=jax.ShapeDtypeStruct((TILE, width), child.dtype),
        in_specs=[SMEM, SMEM, ANY, ANY],
        out_specs=VMEM,
        scratch_shapes=[pltpu.SemaphoreType.DMA((GROUPS,)), pltpu.SemaphoreType.DMA((1,))],
        compiler_params=pltpu.CompilerParams(vmem_limit_bytes=56 * 2**20),
        name="pick_pivot",
    )(ids, child_map, child, entries)


def pick_rest_kernel(ids_ref, map_ref, next_ref, child_ref, entries_ref, coupling_ref, *refs):
    outs, (first_sems, sems, entry_sem) = refs[:6], refs[6:]
    count = child_ref.shape[0]
    width = GROUPS * TILE
    leaf, column = ids_ref[0], ids_ref[1]
    pair = leaf >> 1
    entries = pltpu.make_async_copy(
        entries_ref.at[pl.ds(1, count)], coupling_ref.at[:, :, pl.ds(width, width // 2)], entry_sem.at[0]
    )
    entries.start()
    slots = range(1, count + 1)
    waits = move_separator(
        leaf, column, map_ref, child_ref, slots, lambda slot: coupling_ref.at[slot - 1], first_sems
    )
    rows = [find_tile(map_ref, leaf, column, slot, count) for slot in slots]
    used = 0
    for which, device in enumerate((leaf ^ 1, leaf)):
        for position, target in enumerate(column_targets(device & 1, (device >> 1) & 1)):
            group = target & 3
            update = find_tile(next_ref, pair, group, target >> 2, count)
            place = find_tile(map_ref, leaf, group, update + 1, count)
            column_live = jnp.logical_and(update >= 0, place >= 0)
            source_span = pl.ds(pl.multiple_of((jnp.maximum(place, 0) * GROUPS + group) * TILE, TILE), TILE)
            for slot, row in enumerate(rows):
                live = jnp.logical_and(column_live, row >= 0)
                source = child_ref.at[jnp.maximum(row, 0), :, source_span]
                if position % 4 == 0:
                    goal = outs[3 * which].at[slot, :, pl.ds(position // 4 * TILE, TILE)]
                else:
                    goal = outs[3 * which + 1 + position // 4].at[slot, :, pl.ds((position % 4 - 1) * TILE, TILE)]
                waits.append(move_tile(live, source, goal, sems.at[used]))
                used += 1
    for wait in waits:
        wait()
    entries.wait()


def pick_rest(ids, child_map, next_map, child, entries):
    count = child.shape[0]
    wide = GROUPS * TILE + entries.shape[-1]
    widths = (wide,) + (2 * TILE, 3 * TILE, 3 * TILE) * 2
    return pl.pallas_call(
        pick_rest_kernel,
        out_shape=tuple(jax.ShapeDtypeStruct((count, TILE, width), child.dtype) for width in widths),
        in_specs=[SMEM, SMEM, SMEM, ANY, ANY],
        out_specs=(VMEM,) * 7,
        scratch_shapes=[
            pltpu.SemaphoreType.DMA((GROUPS * count,)),
            pltpu.SemaphoreType.DMA((16 * count,)),
            pltpu.SemaphoreType.DMA((1,)),
        ],
        compiler_params=pltpu.CompilerParams(vmem_limit_bytes=56 * 2**20),
        cost_estimate=pl.CostEstimate(flops=0, bytes_accessed=2 * 10**7, transcendentals=0),
        name="pick_rest",
    )(ids, child_map, next_map, child, entries)


def solve_blocks(coupling_ref, lower_ref, inverse_ref, panel_ref):
    order = lower_ref.shape[0]
    solved = []
    for k in range(order // TILE):
        span = slice(k * TILE, (k + 1) * TILE)
        rest = coupling_ref[:, span]
        if k:
            left = jnp.concatenate([part[0] for part in solved], axis=1)
            low = jnp.concatenate([part[1] for part in solved], axis=1)
            high_lower, low_lower = halves(lower_ref[span, 0 : k * TILE])
            rest = rest - dot_lanes(
                jnp.concatenate([left, low, left], axis=1),
                jnp.concatenate([high_lower, high_lower, low_lower], axis=1),
            )
        block = dot_lanes(left_parts(rest), right_lanes(inverse_ref[k]))
        panel_ref[:, span] = block
        solved.append(halves(block))
    return jnp.concatenate([part[0] for part in solved], axis=1)


def write_factor(column, offset, lower_ref, panel, factor_ref):
    width = factor_ref.shape[-1]
    rows = pl.ds(pl.multiple_of(column * TILE, TILE), TILE)
    span = pl.ds(pl.multiple_of(offset * width, width), width)
    factor_ref[0] = lower_ref[rows, span]
    for s in range(factor_ref.shape[0] - 1):
        factor_ref[s + 1] = panel[s * TILE : (s + 1) * TILE, span]


def panel_one_kernel(
    ids_ref, mask_ref, next_ref, mine_ref, peer_ref, lower_ref, inverse_ref, factor_ref, round_ref, share_ref, coupling, panel
):
    leaf, column = ids_ref[0], ids_ref[1]
    half, pair = leaf & 1, leaf >> 1
    count = mine_ref.shape[0]
    order = lower_ref.shape[0]
    for s in range(count):
        for tile in range(order // TILE):
            span = slice(tile * TILE, (tile + 1) * TILE)
            where = order + (tile % 2) * TILE
            weight = mask_ref[((pair * count + s) * GROUPS + column) * GROUPS + tile].astype(jnp.float32)
            mine = mine_ref[s, :, where : where + TILE].astype(jnp.float32)
            peer = peer_ref[s, :, where : where + TILE].astype(jnp.float32)
            own_first = half == tile // 2
            entry = jnp.where(own_first, mine, peer)
            coupling[s * TILE : (s + 1) * TILE, span] = (
                mine_ref[s, :, span].astype(jnp.float32) + peer_ref[s, :, span].astype(jnp.float32) + entry * weight
            )
    rounded = solve_blocks(coupling, lower_ref, inverse_ref, panel)
    for s in range(count):
        round_ref[s] = rounded[s * TILE : (s + 1) * TILE]
    write_factor(column, half, lower_ref, panel, factor_ref)
    for a in range(2):
        slot = jnp.int32(0)
        for target in column_targets(half, 0):
            hit = jnp.logical_and((target & 3) == column, share_place(target, half) == a)
            slot = jnp.where(hit, target >> 2, slot)
        tile = find_tile(next_ref, pair, column, slot, count)
        share_ref[a] = round_ref[jnp.maximum(tile, 0)]


def panel_one(ids, mask, next_map, mine, peer, lower, inverse):
    count = mine.shape[0]
    order = lower.shape[0]
    return pl.pallas_call(
        panel_one_kernel,
        out_shape=(
            jax.ShapeDtypeStruct((count + 1, TILE, order // 2), jnp.float32),
            jax.ShapeDtypeStruct((count, TILE, order), jnp.bfloat16),
            jax.ShapeDtypeStruct((2, TILE, order), jnp.bfloat16),
        ),
        in_specs=[SMEM, SMEM, SMEM, VMEM, VMEM, VMEM, VMEM],
        out_specs=(VMEM, VMEM, VMEM),
        scratch_shapes=[
            pltpu.VMEM((count * TILE, order), jnp.float32),
            pltpu.VMEM((count * TILE, order), jnp.float32),
        ],
        compiler_params=PARAMS,
        cost_estimate=pl.CostEstimate(flops=10**10, bytes_accessed=2 * 10**7, transcendentals=0),
        name="panel_one",
    )(ids, mask, next_map, mine, peer, lower, inverse)


def panel_two_kernel(ids_ref, own_ref, x_ref, z_ref, both_ref, lower_ref, inverse_ref, factor_ref, round_ref, share_ref, coupling, panel):
    leaf, column = ids_ref[0], ids_ref[1]
    half, side = leaf & 1, (leaf >> 1) & 1
    quarter = leaf & 3
    count = round_ref.shape[0]
    for place, ref in (
        (2 * side + 1 - half, own_ref),
        (2 * side + half, x_ref),
        (2 * (1 - side) + 1 - half, z_ref),
        (2 * (1 - side) + half, both_ref),
    ):
        coupling[:, pl.ds(pl.multiple_of(place * TILE, TILE), TILE)] = ref[...]
    rounded = solve_blocks(coupling, lower_ref, inverse_ref, panel)
    for s in range(count):
        round_ref[s] = rounded[s * TILE : (s + 1) * TILE]
    write_factor(column, quarter, lower_ref, panel, factor_ref)
    chosen = jnp.int32(0)
    for i in range(3):
        tile = 3 * quarter + i
        chosen = jnp.where((tile & 3) == column, tile >> 2, chosen)
    share_ref[...] = round_ref[chosen]


def panel_two(ids, parts, lower, inverse):
    rows = parts[0].shape[0]
    count = rows // TILE
    order = lower.shape[0]
    return pl.pallas_call(
        panel_two_kernel,
        out_shape=(
            jax.ShapeDtypeStruct((count + 1, TILE, order // 4), jnp.float32),
            jax.ShapeDtypeStruct((count, TILE, order), jnp.bfloat16),
            jax.ShapeDtypeStruct((TILE, order), jnp.bfloat16),
        ),
        in_specs=[SMEM] + [VMEM] * 6,
        out_specs=(VMEM, VMEM, VMEM),
        scratch_shapes=[pltpu.VMEM((rows, order), jnp.float32), pltpu.VMEM((rows, order), jnp.float32)],
        compiler_params=PARAMS,
        cost_estimate=pl.CostEstimate(flops=10**10, bytes_accessed=2 * 10**7, transcendentals=0),
        name="panel_two",
    )(ids, *parts, lower, inverse)


def start_shared(ids_ref, positions, shared_ref, taken, sems):
    leaf = ids_ref[0]
    half, side = leaf & 1, (leaf >> 1) & 1
    targets = column_targets(half, side)
    copies = []
    for i, position in enumerate(positions):
        target = targets[position]
        source = shared_ref.at[(target & 3) * 2 + share_place(target, half)]
        copies.append(pltpu.make_async_copy(source, taken.at[i], sems.at[i]))
        copies[-1].start()
    return copies


def update_columns(ids_ref, next_ref, positions, copies, keep_ref, peer_ref, round_ref, taken, tiles, write):
    leaf, column = ids_ref[0], ids_ref[1]
    half, side, pair = leaf & 1, (leaf >> 1) & 1, leaf >> 1
    count = keep_ref.shape[0]
    targets = column_targets(half, side)
    rows = [find_tile(next_ref, pair, column, slot, count) for slot in range(count + 1)]
    tiles[:, count] = jnp.zeros_like(tiles[:, count])
    for i, position in enumerate(positions):
        target = targets[position]
        live = find_tile(next_ref, pair, target & 3, target >> 2, count) >= 0
        span = slice(i * TILE, (i + 1) * TILE)
        copies[i].wait()
        for s in range(count):
            value = keep_ref[s, :, span].astype(jnp.float32) + peer_ref[s, :, span].astype(jnp.float32)
            value = value - dot_lanes(round_ref[s], taken[i])
            tiles[i, s] = jnp.where(live, value, 0.0).astype(jnp.bfloat16)
        for slot, row in enumerate(rows):
            write(i, slot, lambda row=row: tiles[i, jnp.where(row < 0, count, row)])


def update_separator_kernel(
    ids_ref, next_ref, keep_ref, peer_ref, round_ref, shared_ref, pivot_ref, near_ref, far_ref, taken, tiles, sems
):
    def write(i, slot, tile):
        if slot == 0:
            pivot_ref[:, i * TILE : (i + 1) * TILE] = tile()
        else:
            (near_ref, far_ref)[i][slot - 1] = tile()

    copies = start_shared(ids_ref, (0, 4), shared_ref, taken, sems)
    update_columns(ids_ref, next_ref, (0, 4), copies, keep_ref, peer_ref, round_ref, taken, tiles, write)


def update_separator(ids, next_map, keep, peer, rounded, shared):
    count, _, order = rounded.shape
    tile = jax.ShapeDtypeStruct((count, TILE, TILE), jnp.bfloat16)
    return pl.pallas_call(
        update_separator_kernel,
        out_shape=(jax.ShapeDtypeStruct((TILE, 2 * TILE), jnp.bfloat16), tile, tile),
        in_specs=[SMEM, SMEM, VMEM, VMEM, VMEM, ANY],
        out_specs=(VMEM, VMEM, VMEM),
        scratch_shapes=[
            pltpu.VMEM((2, TILE, order), jnp.bfloat16),
            pltpu.VMEM((2, count + 1, TILE, TILE), jnp.bfloat16),
            pltpu.SemaphoreType.DMA((2,)),
        ],
        compiler_params=pltpu.CompilerParams(vmem_limit_bytes=56 * 2**20),
        cost_estimate=pl.CostEstimate(flops=3 * 10**9, bytes_accessed=10**7, transcendentals=0),
        name="update_separator",
    )(ids, next_map, keep, peer, rounded, shared)


def update_trailing_kernel(
    positions, ids_ref, next_ref, keep_ref, peer_ref, round_ref, shared_ref, out_ref, taken, tiles, sems
):
    def write(i, slot, tile):
        if slot:
            out_ref[slot - 1, :, i * TILE : (i + 1) * TILE] = tile()

    copies = start_shared(ids_ref, positions, shared_ref, taken, sems)
    update_columns(ids_ref, next_ref, positions, copies, keep_ref, peer_ref, round_ref, taken, tiles, write)


def update_trailing(ids, next_map, keep, peer, rounded, shared, positions):
    count, _, order = rounded.shape
    width = len(positions)
    return pl.pallas_call(
        functools.partial(update_trailing_kernel, positions),
        out_shape=jax.ShapeDtypeStruct((count, TILE, width * TILE), jnp.bfloat16),
        in_specs=[SMEM, SMEM, VMEM, VMEM, VMEM, ANY],
        out_specs=VMEM,
        scratch_shapes=[
            pltpu.VMEM((width, TILE, order), jnp.bfloat16),
            pltpu.VMEM((width, count + 1, TILE, TILE), jnp.bfloat16),
            pltpu.SemaphoreType.DMA((width,)),
        ],
        compiler_params=pltpu.CompilerParams(vmem_limit_bytes=56 * 2**20),
        cost_estimate=pl.CostEstimate(flops=4 * 10**9, bytes_accessed=12 * 10**6, transcendentals=0),
        name="update_trailing",
    )(ids, next_map, keep, peer, rounded, shared)


def update_two_kernel(ids_ref, near_ref, far_ref, round_ref, shared_ref, out_ref):
    quarter = ids_ref[0] & 3
    for i in range(3):
        shared = shared_ref[(3 * quarter + i) & 3]
        span = slice(i * TILE, (i + 1) * TILE)
        for s in range(near_ref.shape[0]):
            total = near_ref[s, :, span].astype(jnp.float32) + far_ref[s, :, span].astype(jnp.float32)
            out_ref[s, :, span] = (total - dot_lanes(round_ref[s], shared)).astype(jnp.bfloat16)


def update_two(ids, near, far, rounded, shared):
    return pl.pallas_call(
        update_two_kernel,
        out_shape=jax.ShapeDtypeStruct(near.shape, jnp.bfloat16),
        in_specs=[SMEM, VMEM, VMEM, VMEM, VMEM],
        out_specs=VMEM,
        compiler_params=PARAMS,
        cost_estimate=pl.CostEstimate(flops=2 * 10**9, bytes_accessed=10**7, transcendentals=0),
        name="update_two",
    )(ids, near, far, rounded, shared)


def over_square(pack):
    half = pack.shape[0] // 2
    x, y, core = swapped(pack, "leaf", 0), swapped(pack, "front", 1), swapped(pack, "front", 0)
    top = swapped(y[:half], "leaf", 0)
    low = swapped(x[half:], "front", 1)
    x_core, y_core = swapped(x, "front", 0), swapped(y, "front", 0)
    top_core, low_core = swapped(top, "front", 0), swapped(low, "front", 0)
    return (pack, core, y, y_core, x, x_core, top, low, top_core, low_core)


def after(value, *earlier):
    return lax.optimization_barrier((value, *earlier))[0]


def body(child_update, sep_one, sep_two, map_one, map_two, mask_one, mask_two):
    column = lax.axis_index("front")
    leaf = lax.axis_index("leaf")
    half, side, quad = leaf & 1, (leaf >> 1) & 1, leaf >> 2
    ids = jnp.stack([leaf, column]).astype(jnp.int32)
    child = child_update[0, 0, 0]
    entries_one = sep_one[0, 0, 0]
    entries_two = sep_two[0, 0, 0]
    count = child.shape[0]
    order = GROUPS * TILE
    maps_one = map_one[:, 0]
    maps_two = map_two[:, 0]

    packs = over_square(pick_pivot(ids, maps_one, child, entries_one))
    coupling_mine, sep_send, near_send, far_send, sep_keep, near_keep, far_keep = pick_rest(
        ids, maps_one, maps_two, child, entries_one
    )
    coupling_peer = swapped(after(coupling_mine, packs[4]), "leaf", 0)
    sep_peer = swapped(after(sep_send, packs[6]), "leaf", 0)
    far_peer = swapped(after(far_send, packs[6]), "leaf", 0)
    entries_near = swapped(after(entries_two, packs[6]), "leaf", 0)
    entries_far = swapped(entries_near[0], "leaf", 1)

    lower, inverse = cholesky(ids, packs, fill_one, order)
    factor_one, rounded, share = panel_one(
        ids, mask_one.reshape(-1), maps_two, coupling_mine, coupling_peer, lower, inverse
    )
    shared = lax.all_gather(after(share, sep_peer), "front", axis=0, tiled=True)
    pivot_own, near_coupling, far_coupling = update_separator(
        ids, maps_two, after(sep_keep, far_peer), sep_peer, rounded, shared
    )

    pivot_far = swapped(pivot_own, "leaf", 1)
    pivot_tile = (
        pivot_own.astype(jnp.float32)
        + jnp.concatenate([pivot_far[:, TILE:], pivot_far[:, :TILE]], axis=1).astype(jnp.float32)
        + jnp.concatenate([entries_near[0], entries_far], axis=1).astype(jnp.float32)
    )
    packs = over_square(pivot_tile)
    far_trailing = update_trailing(
        ids, maps_two, far_keep, far_peer, after(rounded, pivot_far), shared, (5, 6, 7)
    )
    coupling_far = swapped(after(far_coupling, pivot_far), "leaf", 1)
    mask_second = lax.dynamic_index_in_dim(mask_two, quad, 0, keepdims=False).reshape(count, GROUPS, -1)
    mask_second = lax.dynamic_index_in_dim(mask_second, column, 1, keepdims=False)
    mask_second = lax.dynamic_index_in_dim(mask_second, 2 * side + 1 - half, 1, keepdims=False)
    coupling = (
        near_coupling.astype(jnp.float32)
        + coupling_far.astype(jnp.float32)
        + entries_near[1:].astype(jnp.float32) * mask_second.astype(jnp.float32)[:, None, None]
    ).reshape(count * TILE, TILE)
    coupling_x = swapped(after(coupling, packs[6]), "leaf", 0)
    coupling_z = swapped(coupling, "leaf", 1)
    coupling_xz = swapped(coupling_x, "leaf", 1)
    trailing_far = swapped(after(far_trailing, coupling_x), "leaf", 1)
    near_peer = swapped(after(near_send, coupling_x), "leaf", 0)
    lower, inverse = cholesky(ids, packs, fill_two, order)
    factor_two, rounded_two, share = panel_two(
        ids, (after(coupling, near_peer), coupling_x, coupling_z, coupling_xz), lower, inverse
    )
    near_trailing = update_trailing(ids, maps_two, near_keep, near_peer, rounded, shared, (1, 2, 3))
    shared = lax.all_gather(after(share, trailing_far)[None], "front", axis=0, tiled=True)
    update = update_two(ids, near_trailing, trailing_far, rounded_two, shared)
    return (factor_one[None, None, None], factor_two[None, None, None], update[None, None, None])


def solution(mesh):
    split = P("leaf", "front", None, None, None, None)
    return jax.shard_map(
        body,
        mesh=mesh,
        in_specs=(split, split, split, P(), P(), P(), P()),
        out_specs=(split, split, split),
        check_vma=False,
    )
```

profile of v0, /device:TPU:0, one launch (start us, length us, event | category | flops | bytes accessed | tf_op | source)
XLA Modules:
  0.0 333.0 jit_solution(5665368787515131324)
XLA Ops:
  7.2 1.4 copy.29.map_ref
  9.3 3.0 pick_pivot.1.refs_0_
  12.3 3.0 collective-permute-start.3
  15.3 1.3 collective-permute-start
  16.6 16.5 %collective-permute-done.3.refs_2_ = bf16[256,1536]{1,0:T(8,128)(2,1)S(1)} collective-permute-done((bf16[256,1536]{1,0:T(8,128)(2,1)}, bf16[256,1536]{1,0:T(8,128)(2,1)S(1)}, u32[]{:S(2)}, u32[]{:S(2)}) %collective-permute-start.3) | collective-permute-done | bytes 786464 | tf_op jit(solution)/shard_map/ppermute | solution.py:228
  33.1 1.6 collective-permute-start.6
  34.7 1.7 collective-permute-start.7
  36.9 6.6 %collective-permute-done.6.refs_6_ = bf16[128,1536]{1,0:T(8,128)(2,1)S(1)} collective-permute-done((bf16[128,1536]{1,0:T(8,128)(2,1)S(1)}, bf16[128,1536]{1,0:T(8,128)(2,1)S(1)}, u32[]{:S(2)}, u32[]{:S(2)}) %collective-permute-start.6) | collective-permute-done | bytes 393248 | tf_op jit(solution)/shard_map/ppermute | solution.py:228
  43.5 1.1 collective-permute-done.7.refs_7_
  45.3 7.5 %pick_rest.1 = (bf16[3,256,1536]{2,1,0:T(8,128)(2,1)}, bf16[3,256,512]{2,1,0:T(8,128)(2,1)}, bf16[3,256,768]{2,1,0:T(8,128)(2,1)}, bf16[3,256,768]{2,1,0:T(8,128...) custom-call(s32[2]{0:T(128)} %pad_add_fusion.ids_ref, ...), custom_call_target="tpu_custom_call" | custom-call | bytes 20000000 | tf_op jit(solution)/shard_map/pick_rest/pallas_call | solution.py:350
  52.8 1.4 copy.27
  54.3 0.9 reshape.18.mask_ref
  55.1 1.4 collective-permute-start.1
  57.3 40.6 %cholesky.2 = (f32[1024,1024]{1,0:T(8,128)S(1)}, f32[4,256,256]{2,1,0:T(8,128)S(1)}) custom-call(s32[2]{0:T(128)S(1)} %copy-done.4, bf16[256,1536]{1,0:T(8,128)(2,1)S(1)} %copy-done.2, bf16[256,1536]{1,0:T(8,128)(2,1)S(1)} %collective-permute-done.2.refs_1_, bf16[256,1536]{1,0:T(8,128)(2,1)S(1)} %collective-permute-done.3.refs_2_, ...), custom_call_target="tpu_custom_call" | custom-call | flops 40000000000 | bytes 100000000 | tf_op jit(solution)/shard_map/cholesky/pallas_call | solution.py:204
  97.9 11.5 %collective-permute-done.1.peer_ref = bf16[3,256,1536]{2,1,0:T(8,128)(2,1)S(1)} collective-permute-done((bf16[3,256,1536]{2,1,0:T(8,128)(2,1)}, bf16[3,256,1536]{2,1,0:T(8,128)(2,1)S(1)}, u32[]{:S(2)}, u32[]{:S(2)}) %collective-permute-start.1) | collective-permute-done | bytes 2359328 | tf_op jit(solution)/shard_map/ppermute | solution.py:228
  109.5 8.7 %panel_one.1 = (f32[4,256,512]{2,1,0:T(8,128)}, bf16[3,256,1024]{2,1,0:T(8,128)(2,1)S(1)}, bf16[2,256,1024]{2,1,0:T(8,128)(2,1)}) custom-call(s32[2]{0:T(128)S(1)} %copy-done.4, s32[192]{0:T(256)S(1)} %reshape.18.mask_ref, s32[4,4,3]{2,1,0:T(4,128)S(1)} %bitcast.26, bf16[3,256,1536]{2,1,0:T(8,128)(2,1)S(1)} %copy-done.7, ...), custom_call_target="tpu_custom_call" | custom-call | flops 10000000000 | bytes 20000000 | tf_op jit(solution)/shard_map/panel_one/pallas_call | solution.py:430
  118.2 1.2 copy-done.12
  119.5 6.7 %collective-permute-done.11.peer_ref = bf16[3,256,512]{2,1,0:T(8,128)(2,1)} collective-permute-done((bf16[3,256,512]{2,1,0:T(8,128)(2,1)}, bf16[3,256,512]{2,1,0:T(8,128)(2,1)}, u32[]{:S(2)}, u32[]{:S(2)}) %collective-permute-start.11) | collective-permute-done | bytes 786464 | tf_op jit(solution)/shard_map/ppermute | solution.py:228
  126.4 1.7 collective-permute-start.10
  128.5 26.9 %collective-permute-done.10.peer_ref = bf16[3,256,768]{2,1,0:T(8,128)(2,1)} collective-permute-done((bf16[3,256,768]{2,1,0:T(8,128)(2,1)S(1)}, bf16[3,256,768]{2,1,0:T(8,128)(2,1)}, u32[]{:S(2)}, u32[]{:S(2)}) %collective-permute-start.10) | collective-permute-done | bytes 1179680 | tf_op jit(solution)/shard_map/ppermute | solution.py:228
  155.4 5.8 %all-gather.4.cloned.1.call-done.shared_ref = bf16[8,256,1024]{2,1,0:T(8,128)(2,1)} async-done(((bf16[2,256,1024]{2,1,0:T(8,128)(2,1)}), bf16[8,256,1024]{2,1,0:T(8,128)(2,1)}) %all-gather.4.cloned.1.call-update) | async-done | bytes 4194320 | tf_op jit(solution)/shard_map/all_gather | solution.py:650
  161.2 5.5 %update_separator.1 = (bf16[256,512]{1,0:T(8,128)(2,1)}, bf16[3,256,256]{2,1,0:T(8,128)(2,1)}, bf16[3,256,256]{2,1,0:T(8,128)(2,1)}) custom-call(s32[2]{0:T(128)} %pad_add_fusion.ids_ref, s32[4,4,3]{2,1,0:T(4,128)} %bitcast.23, bf16[3,256,512]{2,1,0:T(8,128)(2,1)} %get-tuple-element.44.keep_ref, bf16[3,256,512]{2,1,0:T(8,128)(2,1)} %collective-permute-done.11.peer_ref, ...), custom_call_target="tpu_custom_call" | custom-call | flops 3000000000 | bytes 10000000 | tf_op jit(solution)/shard_map/update_separator/pallas_call | solution.py:541
  166.7 1.6 collective-permute-start.12
  168.9 7.2 %collective-permute-done.12 = bf16[256,512]{1,0:T(8,128)(2,1)S(1)} collective-permute-done((bf16[256,512]{1,0:T(8,128)(2,1)}, bf16[256,512]{1,0:T(8,128)(2,1)S(1)}, u32[]{:S(2)}, u32[]{:S(2)}) %collective-permute-start.12) | collective-permute-done | bytes 262176 | tf_op jit(solution)/shard_map/ppermute | solution.py:228
  176.1 2.1 collective-permute-done.15
  178.2 1.0 convert_add_fusion.refs_0_
  179.7 1.7 collective-permute-start.13
  181.7 1.5 collective-permute-start.24
  183.2 9.4 %collective-permute-done.16.refs_2_ = f32[256,512]{1,0:T(8,128)S(1)} collective-permute-done((f32[256,512]{1,0:T(8,128)S(1)}, f32[256,512]{1,0:T(8,128)S(1)}, u32[]{:S(2)}, u32[]{:S(2)}) %collective-permute-start.16) | collective-permute-done | bytes 524320 | tf_op jit(solution)/shard_map/ppermute | solution.py:228
  192.6 1.5 collective-permute-start.17
  194.4 5.7 %collective-permute-done.17.refs_6_ = f32[128,512]{1,0:T(8,128)S(1)} collective-permute-done((f32[128,512]{1,0:T(8,128)S(1)}, f32[128,512]{1,0:T(8,128)S(1)}, u32[]{:S(2)}, u32[]{:S(2)}) %collective-permute-start.17) | collective-permute-done | bytes 262176 | tf_op jit(solution)/shard_map/ppermute | solution.py:228
  200.1 1.5 collective-permute-start.18
  201.6 1.5 collective-permute-start.26
  203.6 4.4 %collective-permute-done.26.refs_7_ = f32[128,512]{1,0:T(8,128)S(1)} collective-permute-done((f32[128,512]{1,0:T(8,128)S(1)}, f32[128,512]{1,0:T(8,128)S(1)}, u32[]{:S(2)}, u32[]{:S(2)}) %collective-permute-start.26) | collective-permute-done | bytes 262176 | tf_op jit(solution)/shard_map/ppermute | solution.py:228
  208.0 9.7 %collective-permute-done.18.x_ref = f32[768,256]{1,0:T(8,128)S(1)} collective-permute-done((f32[768,256]{1,0:T(8,128)S(1)}, f32[768,256]{1,0:T(8,128)S(1)}, u32[]{:S(2)}, u32[]{:S(2)}) %collective-permute-start.18) | collective-permute-done | bytes 786464 | tf_op jit(solution)/shard_map/ppermute | solution.py:228
  217.7 6.7 %update_trailing.3 = bf16[3,256,768]{2,1,0:T(8,128)(2,1)} custom-call(s32[2]{0:T(128)} %pad_add_fusion.ids_ref, s32[4,4,3]{2,1,0:T(4,128)} %bitcast.24, bf16[3,256,768]{2,1,0:T(8,128)(2,1)} %get-tuple-element.63.keep_ref, bf16[3,256,768]{2,1,0:T(8,128)(2,1)} %collective-permute-done.10.peer_ref, bf16[3,256,1024]{2,1,0:T(8,128)(2,1)} %copy-done.12, ...), custom_call_target="tpu_custom_call" | custom-call | flops 4000000000 | bytes 12000000 | tf_op jit(solution)/shard_map/update_trailing/pallas_call | solution.py:571
  224.7 1.8 collective-permute-start.29
  226.5 1.6 collective-permute-start.19
  228.2 38.8 %cholesky.3 = (f32[1024,1024]{1,0:T(8,128)S(1)}, f32[4,256,256]{2,1,0:T(8,128)S(1)}) custom-call(s32[2]{0:T(128)S(1)} %copy-done.5, f32[256,512]{1,0:T(8,128)S(1)} %convert_add_fusion.refs_0_, f32[256,512]{1,0:T(8,128)S(1)} %collective-permute-done.22.refs_1_, f32[256,512]{1,0:T(8,128)S(1)} %collective-permute-done.16.refs_2_, ...), custom_call_target="tpu_custom_call" | custom-call | flops 40000000000 | bytes 100000000 | tf_op jit(solution)/shard_map/cholesky/pallas_call | solution.py:204
  267.0 19.5 %collective-permute-done.21.both_ref = f32[768,256]{1,0:T(8,128)S(1)} collective-permute-done((f32[768,256]{1,0:T(8,128)S(1)}, f32[768,256]{1,0:T(8,128)S(1)}, u32[]{:S(2)}, u32[]{:S(2)}) %collective-permute-start.21) | collective-permute-done | bytes 786464 | tf_op jit(solution)/shard_map/ppermute | solution.py:228
  286.6 7.8 %panel_two.1 = (f32[4,256,256]{2,1,0:T(8,128)}, bf16[3,256,1024]{2,1,0:T(8,128)(2,1)S(1)}, bf16[256,1024]{1,0:T(8,128)(2,1)}) custom-call(s32[2]{0:T(128)S(1)} %copy-done.5, f32[768,256]{1,0:T(8,128)S(1)} %bitcast.21, f32[768,256]{1,0:T(8,128)S(1)} %collective-permute-done.18.x_ref, f32[768,256]{1,0:T(8,128)S(1)} %collective-permute-done.20.z_ref, ...), custom_call_target="tpu_custom_call" | custom-call | flops 10000000000 | bytes 20000000 | tf_op jit(solution)/shard_map/panel_two/pallas_call | solution.py:476
  294.4 1.2 copy-done.9
  295.6 6.6 %update_trailing.2.near_ref = bf16[3,256,768]{2,1,0:T(8,128)(2,1)} custom-call(s32[2]{0:T(128)} %pad_add_fusion.ids_ref, s32[4,4,3]{2,1,0:T(4,128)} %bitcast.25, bf16[3,256,768]{2,1,0:T(8,128)(2,1)} %get-tuple-element.62.keep_ref, bf16[3,256,768]{2,1,0:T(8,128)(2,1)} %copy-done.17, bf16[3,256,1024]{2,1,0:T(8,128)(2,1)} %copy-done.12, ...), custom_call_target="tpu_custom_call" | custom-call | flops 4000000000 | bytes 12000000 | tf_op jit(solution)/shard_map/update_trailing/pallas_call | solution.py:571
  302.3 16.6 %all-gather.6.cloned.1.call-done = bf16[1024,1024]{1,0:T(8,128)(2,1)} async-done(((bf16[256,1024]{1,0:T(8,128)(2,1)}), bf16[1024,1024]{1,0:T(8,128)(2,1)}) %all-gather.6.cloned.1.call-update) | async-done | bytes 2097168 | tf_op jit(solution)/shard_map/all_gather | solution.py:684
  318.9 1.6 copy-done.8
  320.5 1.4 copy-done.10
  321.9 1.3 copy-done.11
  323.2 3.0 update_two.1
  (84 shorter events, 5.9 us)
Async XLA Ops:
  7.2 174.2 %copy-start = (s32[2,1,12,4]{2,3,1,0:T(4,128)S(1)}, s32[2,1,12,4]{2,3,1,0:T(4,128)}, u32[]{:S(2)}) copy-start(s32[2,1,12,4]{2,3,1,0:T(4,128)} %param.13) | copy-start | bytes 1156
  7.2 154.0 %all-gather.4.cloned.1.call-start = ((), (), s32[]{:S(2)}) async-start(), calls=%async_computation | async-start | bytes 5242880 | tf_op jit(solution)/shard_map/all_gather | solution.py:650
  12.3 32.3 %copy-start.14 = (s32[4,1,4,3]{2,1,3,0:T(1,128)S(1)}, s32[4,1,4,3]{2,1,3,0:T(1,128)}, u32[]{:S(2)}) copy-start(s32[4,1,4,3]{2,1,3,0:T(1,128)} %param.11) | copy-start | bytes 580
  12.3 20.8 %collective-permute-start.3 = (bf16[256,1536]{1,0:T(8,128)(2,1)}, bf16[256,1536]{1,0:T(8,128)(2,1)S(1)}, u32[]{:S(2)}, u32[]{:S(2)}) collective-permute-start(bf16[256,1536]{1,0:T(8,128)(2,1)} %pick_pivot.1.refs_0_), channel_id=1, source_target_pairs={{0,2},{1,3},{2,0},{3,1},{4,6},{5,7},{6,4},{7,5},{8,10},{9,11},{10,... | collective-permute-start | bytes 2359304 | tf_op jit(solution)/shard_map/ppermute | solution.py:228
  15.3 19.3 %collective-permute-start = (bf16[256,1536]{1,0:T(8,128)(2,1)}, bf16[256,1536]{1,0:T(8,128)(2,1)S(1)}, u32[]{:S(2)}, u32[]{:S(2)}) collective-permute-start(bf16[256,1536]{1,0:T(8,128)(2,1)} %pick_pivot.1.refs_0_), channel_id=1, source_target_pairs={{0,4},{4,0},{8,12},{12,8},{16,20},{20,16},{24,28},{28,24},{1,5},{5... | collective-permute-start | bytes 2359304 | tf_op jit(solution)/shard_map/ppermute | solution.py:228
  16.6 38.5 %collective-permute-start.2 = (bf16[256,1536]{1,0:T(8,128)(2,1)}, bf16[256,1536]{1,0:T(8,128)(2,1)S(1)}, u32[]{:S(2)}, u32[]{:S(2)}) collective-permute-start(bf16[256,1536]{1,0:T(8,128)(2,1)} %pick_pivot.1.refs_0_), channel_id=1, source_target_pairs={{0,1},{1,0},{2,3},{3,2},{4,5},{5,4},{6,7},{7,6},{8,9},{9,8},{10,11... | collective-permute-start | bytes 2359304 | tf_op jit(solution)/shard_map/ppermute | solution.py:228
  33.1 10.4 %collective-permute-start.6 = (bf16[128,1536]{1,0:T(8,128)(2,1)S(1)}, bf16[128,1536]{1,0:T(8,128)(2,1)S(1)}, u32[]{:S(2)}, u32[]{:S(2)}) collective-permute-start(bf16[128,1536]{1,0:T(8,128)(2,1)S(1)} %slice.33), channel_id=1, source_target_pairs={{0,4},{4,0},{8,12},{12,8},{16,20},{20,16},{24,28},{28,24},{1,5},{5... | collective-permute-start | bytes 1179656 | tf_op jit(solution)/shard_map/ppermute | solution.py:228
  34.7 9.9 %collective-permute-start.7 = (bf16[128,1536]{1,0:T(8,128)(2,1)S(1)}, bf16[128,1536]{1,0:T(8,128)(2,1)}, u32[]{:S(2)}, u32[]{:S(2)}) collective-permute-start(bf16[128,1536]{1,0:T(8,128)(2,1)S(1)} %slice.34), channel_id=1, source_target_pairs={{0,2},{1,3},{2,0},{3,1},{4,6},{5,7},{6,4},{7,5},{8,10},{9,11},{10,... | collective-permute-start | bytes 1179656 | tf_op jit(solution)/shard_map/ppermute | solution.py:228
  36.4 20.9 %collective-permute-start.5 = (bf16[256,1536]{1,0:T(8,128)(2,1)S(1)}, bf16[256,1536]{1,0:T(8,128)(2,1)}, u32[]{:S(2)}, u32[]{:S(2)}) collective-permute-start(bf16[256,1536]{1,0:T(8,128)(2,1)S(1)} %collective-permute-done.refs_4_), channel_id=1, source_target_pairs={{0,1},{1,0},{2,3},{3,2},{4,5},{5,4},{6,7},{7,6},{8,9},{9,8},{10,11... | collective-permute-start | bytes 2359304 | tf_op jit(solution)/shard_map/ppermute | solution.py:228
  36.4 20.9 %collective-permute-start.4 = (bf16[256,1536]{1,0:T(8,128)(2,1)S(1)}, bf16[256,1536]{1,0:T(8,128)(2,1)}, u32[]{:S(2)}, u32[]{:S(2)}) collective-permute-start(bf16[256,1536]{1,0:T(8,128)(2,1)S(1)} %collective-permute-done.3.refs_2_), channel_id=1, source_target_pairs={{0,1},{1,0},{2,3},{3,2},{4,5},{5,4},{6,7},{7,6},{8,9},{9,8},{10,11... | collective-permute-start | bytes 2359304 | tf_op jit(solution)/shard_map/ppermute | solution.py:228
  43.5 13.0 %collective-permute-start.8 = (bf16[128,1536]{1,0:T(8,128)(2,1)S(1)}, bf16[128,1536]{1,0:T(8,128)(2,1)}, u32[]{:S(2)}, u32[]{:S(2)}) collective-permute-start(bf16[128,1536]{1,0:T(8,128)(2,1)S(1)} %collective-permute-done.6.refs_6_), channel_id=1, source_target_pairs={{0,1},{1,0},{2,3},{3,2},{4,5},{5,4},{6,7},{7,6},{8,9},{9,8},{10,11... | collective-permute-start | bytes 1179656 | tf_op jit(solution)/shard_map/ppermute | solution.py:228
  44.6 12.7 %collective-permute-start.9 = (bf16[128,1536]{1,0:T(8,128)(2,1)}, bf16[128,1536]{1,0:T(8,128)(2,1)}, u32[]{:S(2)}, u32[]{:S(2)}) collective-permute-start(bf16[128,1536]{1,0:T(8,128)(2,1)} %collective-permute-done.7.refs_7_), channel_id=1, source_target_pairs={{0,1},{1,0},{2,3},{3,2},{4,5},{5,4},{6,7},{7,6},{8,9},{9,8},{10,11... | collective-permute-start | bytes 1179656 | tf_op jit(solution)/shard_map/ppermute | solution.py:228
  45.3 12.0 %copy-start.2 = (bf16[256,1536]{1,0:T(8,128)(2,1)S(1)}, bf16[256,1536]{1,0:T(8,128)(2,1)}, u32[]{:S(2)}) copy-start(bf16[256,1536]{1,0:T(8,128)(2,1)} %pick_pivot.1.refs_0_) | copy-start | bytes 2359300
  45.3 12.0 %copy-start.4 = (s32[2]{0:T(128)S(1)}, s32[2]{0:T(128)}, u32[]{:S(2)}) copy-start(s32[2]{0:T(128)} %pad_add_fusion.ids_ref) | copy-start | bytes 28
  55.1 54.3 %copy-start.3 = (s32[4,1,4,3]{3,2,0,1:T(4,128)S(1)}, s32[4,1,4,3]{3,2,0,1:T(4,128)}, u32[]{:S(2)}) copy-start(s32[4,1,4,3]{3,2,0,1:T(4,128)} %copy.36) | copy-start | bytes 580
  55.1 54.3 %copy-start.7 = (bf16[3,256,1536]{2,1,0:T(8,128)(2,1)S(1)}, bf16[3,256,1536]{2,1,0:T(8,128)(2,1)}, u32[]{:S(2)}) copy-start(bf16[3,256,1536]{2,1,0:T(8,128)(2,1)} %get-tuple-element.37.mine_ref) | copy-start | bytes 7077892
  55.1 54.3 %collective-permute-start.1 = (bf16[3,256,1536]{2,1,0:T(8,128)(2,1)}, bf16[3,256,1536]{2,1,0:T(8,128)(2,1)S(1)}, u32[]{:S(2)}, u32[]{:S(2)}) collective-permute-start(bf16[3,256,1536]{2,1,0:T(8,128)(2,1)} %get-tuple-element.37.mine_ref), channel_id=1, source_target_pairs={{0,4},{4,0},{8,12},{12,8},{16,20},{20,16},{24,28},{28,24},{1,5},{5... | collective-permute-start | bytes 7077896 | tf_op jit(solution)/shard_map/ppermute | solution.py:228
  56.5 69.6 %collective-permute-start.11 = (bf16[3,256,512]{2,1,0:T(8,128)(2,1)}, bf16[3,256,512]{2,1,0:T(8,128)(2,1)}, u32[]{:S(2)}, u32[]{:S(2)}) collective-permute-start(bf16[3,256,512]{2,1,0:T(8,128)(2,1)} %get-tuple-element.46), channel_id=1, source_target_pairs={{0,4},{4,0},{8,12},{12,8},{16,20},{20,16},{24,28},{28,24},{1,5},{5... | collective-permute-start | bytes 2359304 | tf_op jit(solution)/shard_map/ppermute | solution.py:228
  109.5 17.0 %copy-start.16 = (bf16[3,256,768]{2,1,0:T(8,128)(2,1)S(1)}, bf16[3,256,768]{2,1,0:T(8,128)(2,1)}, u32[]{:S(2)}) copy-start(bf16[3,256,768]{2,1,0:T(8,128)(2,1)} %get-tuple-element.43) | copy-start | bytes 3538948
  109.5 18.7 %copy-start.18 = (bf16[1,1,1,4,256,256]{5,4,3,2,1,0:T(8,128)(2,1)S(1)}, bf16[1,1,1,4,256,256]{5,4,3,2,1,0:T(8,128)(2,1)}, u32[]{:S(2)}) copy-start(bf16[1,1,1,4,256,256]{5,4,3,2,1,0:T(8,128)(2,1)} %param.9) | copy-start | bytes 1572868
  126.2 192.7 %all-gather.6.cloned.1.call-start = ((), (), s32[]{:S(2)}) async-start(), calls=%async_computation.1 | async-start | bytes 2621440 | tf_op jit(solution)/shard_map/all_gather | solution.py:684
  126.4 29.0 %collective-permute-start.10 = (bf16[3,256,768]{2,1,0:T(8,128)(2,1)S(1)}, bf16[3,256,768]{2,1,0:T(8,128)(2,1)}, u32[]{:S(2)}, u32[]{:S(2)}) collective-permute-start(bf16[3,256,768]{2,1,0:T(8,128)(2,1)S(1)} %copy-done.16), channel_id=1, source_target_pairs={{0,4},{4,0},{8,12},{12,8},{16,20},{20,16},{24,28},{28,24},{1,5},{5... | collective-permute-start | bytes 3538952 | tf_op jit(solution)/shard_map/ppermute | solution.py:228
  128.1 40.1 %collective-permute-start.14 = (bf16[4,256,256]{2,1,0:T(8,128)(2,1)S(1)}, bf16[4,256,256]{2,1,0:T(8,128)(2,1)S(1)}, u32[]{:S(2)}, u32[]{:S(2)}) collective-permute-start(bf16[4,256,256]{2,1,0:T(8,128)(2,1)S(1)} %bitcast.33), channel_id=1, source_target_pairs={{0,4},{4,0},{8,12},{12,8},{16,20},{20,16},{24,28},{28,24},{1,5},{5... | collective-permute-start | bytes 1572872 | tf_op jit(solution)/shard_map/ppermute | solution.py:228
  166.7 13.0 %copy-start.19 = (bf16[3,256,256]{2,1,0:T(8,128)(2,1)S(1)}, bf16[3,256,256]{2,1,0:T(8,128)(2,1)}, u32[]{:S(2)}) copy-start(bf16[3,256,256]{2,1,0:T(8,128)(2,1)} %get-tuple-element.53) | copy-start | bytes 1179652
  166.7 27.5 %copy-start.13 = (bf16[3,256,256]{2,1,0:T(8,128)(2,1)S(1)}, bf16[3,256,256]{2,1,0:T(8,128)(2,1)}, u32[]{:S(2)}) copy-start(bf16[3,256,256]{2,1,0:T(8,128)(2,1)} %get-tuple-element.50) | copy-start | bytes 1179652
  166.7 9.4 %collective-permute-start.12 = (bf16[256,512]{1,0:T(8,128)(2,1)}, bf16[256,512]{1,0:T(8,128)(2,1)S(1)}, u32[]{:S(2)}, u32[]{:S(2)}) collective-permute-start(bf16[256,512]{1,0:T(8,128)(2,1)} %get-tuple-element.52), channel_id=1, source_target_pairs={{0,8},{4,12},{8,0},{12,4},{16,24},{20,28},{24,16},{28,20},{1,9},{5... | collective-permute-start | bytes 786440 | tf_op jit(solution)/shard_map/ppermute | solution.py:228
  168.3 10.0 %collective-permute-start.15 = (bf16[256,256]{1,0:T(8,128)(2,1)S(1)}, bf16[256,256]{1,0:T(8,128)(2,1)S(1)}, u32[]{:S(2)}, u32[]{:S(2)}) collective-permute-start(bf16[256,256]{1,0:T(8,128)(2,1)S(1)} %slice_bitcast_fusion), channel_id=1, source_target_pairs={{0,8},{4,12},{8,0},{12,4},{16,24},{20,28},{24,16},{28,20},{1,9},{5... | collective-permute-start | bytes 393224 | tf_op jit(solution)/shard_map/ppermute | solution.py:228
  179.3 13.3 %collective-permute-start.16 = (f32[256,512]{1,0:T(8,128)S(1)}, f32[256,512]{1,0:T(8,128)S(1)}, u32[]{:S(2)}, u32[]{:S(2)}) collective-permute-start(f32[256,512]{1,0:T(8,128)S(1)} %convert_add_fusion.refs_0_), channel_id=1, source_target_pairs={{0,2},{1,3},{2,0},{3,1},{4,6},{5,7},{6,4},{7,5},{8,10},{9,11},{10,... | collective-permute-start | bytes 1572872 | tf_op jit(solution)/shard_map/ppermute | solution.py:228
  179.7 14.5 %collective-permute-start.13 = (bf16[3,256,256]{2,1,0:T(8,128)(2,1)S(1)}, bf16[3,256,256]{2,1,0:T(8,128)(2,1)S(1)}, u32[]{:S(2)}, u32[]{:S(2)}) collective-permute-start(bf16[3,256,256]{2,1,0:T(8,128)(2,1)S(1)} %copy-done.19), channel_id=1, source_target_pairs={{0,8},{4,12},{8,0},{12,4},{16,24},{20,28},{24,16},{28,20},{1,9},{5... | collective-permute-start | bytes 1179656 | tf_op jit(solution)/shard_map/ppermute | solution.py:228
  181.7 19.9 %collective-permute-start.24 = (f32[256,512]{1,0:T(8,128)S(1)}, f32[256,512]{1,0:T(8,128)S(1)}, u32[]{:S(2)}, u32[]{:S(2)}) collective-permute-start(f32[256,512]{1,0:T(8,128)S(1)} %convert_add_fusion.refs_0_), channel_id=1, source_target_pairs={{0,4},{4,0},{8,12},{12,8},{16,20},{20,16},{24,28},{28,24},{1,5},{5... | collective-permute-start | bytes 1572872 | tf_op jit(solution)/shard_map/ppermute | solution.py:228
  192.6 7.4 %collective-permute-start.17 = (f32[128,512]{1,0:T(8,128)S(1)}, f32[128,512]{1,0:T(8,128)S(1)}, u32[]{:S(2)}, u32[]{:S(2)}) collective-permute-start(f32[128,512]{1,0:T(8,128)S(1)} %slice.39), channel_id=1, source_target_pairs={{0,4},{4,0},{8,12},{12,8},{16,20},{20,16},{24,28},{28,24},{1,5},{5... | collective-permute-start | bytes 786440 | tf_op jit(solution)/shard_map/ppermute | solution.py:228
  200.1 17.7 %collective-permute-start.18 = (f32[768,256]{1,0:T(8,128)S(1)}, f32[768,256]{1,0:T(8,128)S(1)}, u32[]{:S(2)}, u32[]{:S(2)}) collective-permute-start(f32[768,256]{1,0:T(8,128)S(1)} %bitcast.19), channel_id=1, source_target_pairs={{0,4},{4,0},{8,12},{12,8},{16,20},{20,16},{24,28},{28,24},{1,5},{5... | collective-permute-start | bytes 2359304 | tf_op jit(solution)/shard_map/ppermute | solution.py:228
  201.6 6.4 %collective-permute-start.26 = (f32[128,512]{1,0:T(8,128)S(1)}, f32[128,512]{1,0:T(8,128)S(1)}, u32[]{:S(2)}, u32[]{:S(2)}) collective-permute-start(f32[128,512]{1,0:T(8,128)S(1)} %slice.40), channel_id=1, source_target_pairs={{0,2},{1,3},{2,0},{3,1},{4,6},{5,7},{6,4},{7,5},{8,10},{9,11},{10,... | collective-permute-start | bytes 786440 | tf_op jit(solution)/shard_map/ppermute | solution.py:228
  203.1 21.3 %collective-permute-start.22 = (f32[256,512]{1,0:T(8,128)S(1)}, f32[256,512]{1,0:T(8,128)S(1)}, u32[]{:S(2)}, u32[]{:S(2)}) collective-permute-start(f32[256,512]{1,0:T(8,128)S(1)} %convert_add_fusion.refs_0_), channel_id=1, source_target_pairs={{0,1},{1,0},{2,3},{3,2},{4,5},{5,4},{6,7},{7,6},{8,9},{9,8},{10,11... | collective-permute-start | bytes 1572872 | tf_op jit(solution)/shard_map/ppermute | solution.py:228
  203.1 25.0 %collective-permute-start.23 = (f32[256,512]{1,0:T(8,128)S(1)}, f32[256,512]{1,0:T(8,128)S(1)}, u32[]{:S(2)}, u32[]{:S(2)}) collective-permute-start(f32[256,512]{1,0:T(8,128)S(1)} %collective-permute-done.16.refs_2_), channel_id=1, source_target_pairs={{0,1},{1,0},{2,3},{3,2},{4,5},{5,4},{6,7},{7,6},{8,9},{9,8},{10,11... | collective-permute-start | bytes 1572872 | tf_op jit(solution)/shard_map/ppermute | solution.py:228
  203.6 24.6 %collective-permute-start.25 = (f32[256,512]{1,0:T(8,128)S(1)}, f32[256,512]{1,0:T(8,128)S(1)}, u32[]{:S(2)}, u32[]{:S(2)}) collective-permute-start(f32[256,512]{1,0:T(8,128)S(1)} %collective-permute-done.24.refs_4_), channel_id=1, source_target_pairs={{0,1},{1,0},{2,3},{3,2},{4,5},{5,4},{6,7},{7,6},{8,9},{9,8},{10,11... | collective-permute-start | bytes 1572872 | tf_op jit(solution)/shard_map/ppermute | solution.py:228
  208.0 16.6 %collective-permute-start.27 = (f32[128,512]{1,0:T(8,128)S(1)}, f32[128,512]{1,0:T(8,128)S(1)}, u32[]{:S(2)}, u32[]{:S(2)}) collective-permute-start(f32[128,512]{1,0:T(8,128)S(1)} %collective-permute-done.17.refs_6_), channel_id=1, source_target_pairs={{0,1},{1,0},{2,3},{3,2},{4,5},{5,4},{6,7},{7,6},{8,9},{9,8},{10,11... | collective-permute-start | bytes 786440 | tf_op jit(solution)/shard_map/ppermute | solution.py:228
  217.7 8.8 %collective-permute-start.28 = (f32[128,512]{1,0:T(8,128)S(1)}, f32[128,512]{1,0:T(8,128)S(1)}, u32[]{:S(2)}, u32[]{:S(2)}) collective-permute-start(f32[128,512]{1,0:T(8,128)S(1)} %collective-permute-done.26.refs_7_), channel_id=1, source_target_pairs={{0,1},{1,0},{2,3},{3,2},{4,5},{5,4},{6,7},{7,6},{8,9},{9,8},{10,11... | collective-permute-start | bytes 786440 | tf_op jit(solution)/shard_map/ppermute | solution.py:228
  217.7 8.8 %copy-start.15 = (bf16[3,256,768]{2,1,0:T(8,128)(2,1)S(1)}, bf16[3,256,768]{2,1,0:T(8,128)(2,1)}, u32[]{:S(2)}) copy-start(bf16[3,256,768]{2,1,0:T(8,128)(2,1)} %get-tuple-element.57) | copy-start | bytes 3538948
  217.7 10.5 %copy-start.5 = (s32[2]{0:T(128)S(1)}, s32[2]{0:T(128)}, u32[]{:S(2)}) copy-start(s32[2]{0:T(128)} %pad_add_fusion.ids_ref) | copy-start | bytes 28
  224.4 42.6 %collective-permute-start.20 = (f32[768,256]{1,0:T(8,128)S(1)}, f32[768,256]{1,0:T(8,128)S(1)}, u32[]{:S(2)}, u32[]{:S(2)}) collective-permute-start(f32[768,256]{1,0:T(8,128)S(1)} %bitcast.20), channel_id=1, source_target_pairs={{0,8},{4,12},{8,0},{12,4},{16,24},{20,28},{24,16},{28,20},{1,9},{5... | collective-permute-start | bytes 2359304 | tf_op jit(solution)/shard_map/ppermute | solution.py:228
  224.7 70.9 %collective-permute-start.29 = (bf16[3,256,768]{2,1,0:T(8,128)(2,1)}, bf16[3,256,768]{2,1,0:T(8,128)(2,1)S(1)}, u32[]{:S(2)}, u32[]{:S(2)}) collective-permute-start(bf16[3,256,768]{2,1,0:T(8,128)(2,1)} %update_trailing.3), channel_id=1, source_target_pairs={{0,8},{4,12},{8,0},{12,4},{16,24},{20,28},{24,16},{28,20},{1,9},{5... | collective-permute-start | bytes 3538952 | tf_op jit(solution)/shard_map/ppermute | solution.py:228
  226.5 40.5 %collective-permute-start.19 = (bf16[3,256,768]{2,1,0:T(8,128)(2,1)S(1)}, bf16[3,256,768]{2,1,0:T(8,128)(2,1)S(1)}, u32[]{:S(2)}, u32[]{:S(2)}) collective-permute-start(bf16[3,256,768]{2,1,0:T(8,128)(2,1)S(1)} %copy-done.15), channel_id=1, source_target_pairs={{0,4},{4,0},{8,12},{12,8},{16,20},{20,16},{24,28},{28,24},{1,5},{5... | collective-permute-start | bytes 3538952 | tf_op jit(solution)/shard_map/ppermute | solution.py:228
  228.1 58.5 %collective-permute-start.21 = (f32[768,256]{1,0:T(8,128)S(1)}, f32[768,256]{1,0:T(8,128)S(1)}, u32[]{:S(2)}, u32[]{:S(2)}) collective-permute-start(f32[768,256]{1,0:T(8,128)S(1)} %collective-permute-done.18.x_ref), channel_id=1, source_target_pairs={{0,8},{4,12},{8,0},{12,4},{16,24},{20,28},{24,16},{28,20},{1,9},{5... | collective-permute-start | bytes 2359304 | tf_op jit(solution)/shard_map/ppermute | solution.py:228
  267.0 27.4 %copy-start.17 = (bf16[3,256,768]{2,1,0:T(8,128)(2,1)}, bf16[3,256,768]{2,1,0:T(8,128)(2,1)S(1)}, u32[]{:S(2)}) copy-start(bf16[3,256,768]{2,1,0:T(8,128)(2,1)S(1)} %collective-permute-done.19.peer_ref) | copy-start | bytes 3538948
  295.6 23.2 %copy-start.6 = (s32[2]{0:T(128)S(1)}, s32[2]{0:T(128)}, u32[]{:S(2)}) copy-start(s32[2]{0:T(128)} %pad_add_fusion.ids_ref) | copy-start | bytes 28
  318.9 1.6 copy-start.8
  323.2 3.1 copy-start.1
  (4 other events, 5.1 us)
Sparse Core Ops, SparseCore 0:
  126.3 34.8 all-gather.3
  295.8 23.0 all-gather.5
where the time goes:
time: 334 us; the launch traced here: 333 us
  waiting for transfers between devices  150 us (45%)
  Pallas kernels  128 us (38%)
  starting transfers between devices  27.2 us (8%)
  between operations  14.3 us (4%)
  local copies, waits for them, and re-layouts  11.4 us (3%)
    ppermute x30, waiting for transfers between devices, swapped(): return lax.ppermute(value, axis, pairs)  127 us
    pallas_call x2, Pallas kernels, cholesky(): pl.pallas_call(functools.partial(cholesky_kernel, fill), out_shape=(jax.S...  79.4 us
    ppermute x30, starting transfers between devices, swapped(): return lax.ppermute(value, axis, pairs)  26.9 us
    all_gather x1, waiting for transfers between devices, body(): lax.all_gather(after(share, trailing_far)[None], 'front', axis=0, tiled=T...  16.6 us
    pallas_call x2, Pallas kernels, update_trailing(): pl.pallas_call(functools.partial(update_trailing_kernel, positions), out_...  13.3 us
    pallas_call x1, Pallas kernels, panel_one(): pl.pallas_call(panel_one_kernel, out_shape=(jax.ShapeDtypeStruct((count +...  8.74 us
    unnamed x41, local copies, waits for them, and re-layouts  8.21 us
    pallas_call x1, Pallas kernels, panel_two(): pl.pallas_call(panel_two_kernel, out_shape=(jax.ShapeDtypeStruct((count +...  7.83 us
  transfers between devices with their start and end apart: 32, of which 15 were waited for; matrix products, arithmetic and copies ran while one was open for 1% of the time, Pallas kernels for 37%

commit v1 on v0

--- a/solution.py
+++ b/solution.py
@@ -140,7 +140,7 @@
         (3, y_core, packs[8:10]),
     ):
         base = (column ^ apart) * TILE
-        for refs, last in (((mine,), 1 - half), (peers, half)):
+        for refs, last in (((mine,), half), (peers, 1 - half)):
             height = TILE // len(refs)
             for part, ref in enumerate(refs):
                 rows = pl.ds(pl.multiple_of(base + part * height, height), height)
@@ -222,8 +222,7 @@
     )(ids, *packs)
 
 
-def swapped(value, axis, apart):
-    mask = 2**apart
+def swapped(value, axis, mask):
     pairs = [(source, source ^ mask) for source in range(lax.axis_size(axis))]
     return lax.ppermute(value, axis, pairs)
 
@@ -238,7 +237,7 @@
 def column_targets(half, side):
     targets = []
     for part in (side, 1 - side):
-        targets.append(2 * part + 1 - half)
+        targets.append(2 * part + half)
         targets += [4 + 3 * (2 * part + half) + i for i in range(3)]
     return targets
 
@@ -393,7 +392,7 @@
 
 
 def panel_one_kernel(
-    ids_ref, mask_ref, next_ref, mine_ref, peer_ref, lower_ref, inverse_ref, factor_ref, round_ref, share_ref, coupling, panel
+    ids_ref, mask_ref, next_ref, mine_ref, peer_ref, lower_ref, inverse_ref, factor_ref, round_ref, first_ref, second_ref, third_ref, coupling, panel
 ):
     leaf, column = ids_ref[0], ids_ref[1]
     half, pair = leaf & 1, leaf >> 1
@@ -415,13 +414,13 @@
     for s in range(count):
         round_ref[s] = rounded[s * TILE : (s + 1) * TILE]
     write_factor(column, half, lower_ref, panel, factor_ref)
-    for a in range(2):
+    for a, share_ref in enumerate((first_ref, second_ref, third_ref)):
         slot = jnp.int32(0)
         for target in column_targets(half, 0):
             hit = jnp.logical_and((target & 3) == column, share_place(target, half) == a)
             slot = jnp.where(hit, target >> 2, slot)
         tile = find_tile(next_ref, pair, column, slot, count)
-        share_ref[a] = round_ref[jnp.maximum(tile, 0)]
+        share_ref[...] = round_ref[jnp.maximum(tile, 0)]
 
 
 def panel_one(ids, mask, next_map, mine, peer, lower, inverse):
@@ -432,16 +431,16 @@
         out_shape=(
             jax.ShapeDtypeStruct((count + 1, TILE, order // 2), jnp.float32),
             jax.ShapeDtypeStruct((count, TILE, order), jnp.bfloat16),
-            jax.ShapeDtypeStruct((2, TILE, order), jnp.bfloat16),
-        ),
+        )
+        + (jax.ShapeDtypeStruct((TILE, order), jnp.bfloat16),) * 3,
         in_specs=[SMEM, SMEM, SMEM, VMEM, VMEM, VMEM, VMEM],
-        out_specs=(VMEM, VMEM, VMEM),
+        out_specs=(VMEM,) * 5,
         scratch_shapes=[
             pltpu.VMEM((count * TILE, order), jnp.float32),
             pltpu.VMEM((count * TILE, order), jnp.float32),
         ],
         compiler_params=PARAMS,
-        cost_estimate=pl.CostEstimate(flops=10**10, bytes_accessed=2 * 10**7, transcendentals=0),
+        cost_estimate=pl.CostEstimate(flops=10**9, bytes_accessed=10**6, transcendentals=0),
         name="panel_one",
     )(ids, mask, next_map, mine, peer, lower, inverse)
 
@@ -452,10 +451,10 @@
     quarter = leaf & 3
     count = round_ref.shape[0]
     for place, ref in (
-        (2 * side + 1 - half, own_ref),
-        (2 * side + half, x_ref),
-        (2 * (1 - side) + 1 - half, z_ref),
-        (2 * (1 - side) + half, both_ref),
+        (2 * side + half, own_ref),
+        (2 * side + 1 - half, x_ref),
+        (2 * (1 - side) + half, z_ref),
+        (2 * (1 - side) + 1 - half, both_ref),
     ):
         coupling[:, pl.ds(pl.multiple_of(place * TILE, TILE), TILE)] = ref[...]
     rounded = solve_blocks(coupling, lower_ref, inverse_ref, panel)
@@ -484,21 +483,32 @@
         out_specs=(VMEM, VMEM, VMEM),
         scratch_shapes=[pltpu.VMEM((rows, order), jnp.float32), pltpu.VMEM((rows, order), jnp.float32)],
         compiler_params=PARAMS,
-        cost_estimate=pl.CostEstimate(flops=10**10, bytes_accessed=2 * 10**7, transcendentals=0),
+        cost_estimate=pl.CostEstimate(flops=10**9, bytes_accessed=10**6, transcendentals=0),
         name="panel_two",
     )(ids, *parts, lower, inverse)
 
 
-def start_shared(ids_ref, positions, shared_ref, taken, sems):
-    leaf = ids_ref[0]
+def take_tile(owner, column, refs, live, target, sem):
+    for apart, ref in enumerate(refs):
+
+        @pl.when(jnp.logical_and(live, (owner ^ column) == apart))
+        def _():
+            pltpu.make_async_copy(ref, target, sem).start()
+
+
+def start_shared(ids_ref, positions, firsts, seconds, taken, sems):
+    leaf, column = ids_ref[0], ids_ref[1]
     half, side = leaf & 1, (leaf >> 1) & 1
     targets = column_targets(half, side)
     copies = []
     for i, position in enumerate(positions):
         target = targets[position]
-        source = shared_ref.at[(target & 3) * 2 + share_place(target, half)]
-        copies.append(pltpu.make_async_copy(source, taken.at[i], sems.at[i]))
-        copies[-1].start()
+        group = target & 3
+        place = share_place(target, half)
+        take_tile(group, column, firsts, place == 0, taken.at[i], sems.at[i])
+        if seconds:
+            take_tile(jnp.where(place == 2, group ^ 1, group), column, seconds, place > 0, taken.at[i], sems.at[i])
+        copies.append(pltpu.make_async_copy(firsts[0], taken.at[i], sems.at[i]))
     return copies
 
 
@@ -523,25 +533,27 @@
 
 
 def update_separator_kernel(
-    ids_ref, next_ref, keep_ref, peer_ref, round_ref, shared_ref, pivot_ref, near_ref, far_ref, taken, tiles, sems
+    ids_ref, next_ref, keep_ref, peer_ref, round_ref, *refs
 ):
+    firsts, (pivot_ref, near_ref, far_ref, taken, tiles, sems) = refs[:4], refs[4:]
+
     def write(i, slot, tile):
         if slot == 0:
             pivot_ref[:, i * TILE : (i + 1) * TILE] = tile()
         else:
             (near_ref, far_ref)[i][slot - 1] = tile()
 
-    copies = start_shared(ids_ref, (0, 4), shared_ref, taken, sems)
+    copies = start_shared(ids_ref, (0, 4), firsts, (), taken, sems)
     update_columns(ids_ref, next_ref, (0, 4), copies, keep_ref, peer_ref, round_ref, taken, tiles, write)
 
 
-def update_separator(ids, next_map, keep, peer, rounded, shared):
+def update_separator(ids, next_map, keep, peer, rounded, firsts):
     count, _, order = rounded.shape
     tile = jax.ShapeDtypeStruct((count, TILE, TILE), jnp.bfloat16)
     return pl.pallas_call(
         update_separator_kernel,
         out_shape=(jax.ShapeDtypeStruct((TILE, 2 * TILE), jnp.bfloat16), tile, tile),
-        in_specs=[SMEM, SMEM, VMEM, VMEM, VMEM, ANY],
+        in_specs=[SMEM, SMEM, VMEM, VMEM, VMEM] + [ANY] * 4,
         out_specs=(VMEM, VMEM, VMEM),
         scratch_shapes=[
             pltpu.VMEM((2, TILE, order), jnp.bfloat16),
@@ -551,27 +563,29 @@
         compiler_params=pltpu.CompilerParams(vmem_limit_bytes=56 * 2**20),
         cost_estimate=pl.CostEstimate(flops=3 * 10**9, bytes_accessed=10**7, transcendentals=0),
         name="update_separator",
-    )(ids, next_map, keep, peer, rounded, shared)
+    )(ids, next_map, keep, peer, rounded, *firsts)
 
 
 def update_trailing_kernel(
-    positions, ids_ref, next_ref, keep_ref, peer_ref, round_ref, shared_ref, out_ref, taken, tiles, sems
+    positions, ids_ref, next_ref, keep_ref, peer_ref, round_ref, *refs
 ):
+    firsts, seconds, (out_ref, taken, tiles, sems) = refs[:4], refs[4:8], refs[8:]
+
     def write(i, slot, tile):
         if slot:
             out_ref[slot - 1, :, i * TILE : (i + 1) * TILE] = tile()
 
-    copies = start_shared(ids_ref, positions, shared_ref, taken, sems)
+    copies = start_shared(ids_ref, positions, firsts, seconds, taken, sems)
     update_columns(ids_ref, next_ref, positions, copies, keep_ref, peer_ref, round_ref, taken, tiles, write)
 
 
-def update_trailing(ids, next_map, keep, peer, rounded, shared, positions):
+def update_trailing(ids, next_map, keep, peer, rounded, firsts, seconds, positions):
     count, _, order = rounded.shape
     width = len(positions)
     return pl.pallas_call(
         functools.partial(update_trailing_kernel, positions),
         out_shape=jax.ShapeDtypeStruct((count, TILE, width * TILE), jnp.bfloat16),
-        in_specs=[SMEM, SMEM, VMEM, VMEM, VMEM, ANY],
+        in_specs=[SMEM, SMEM, VMEM, VMEM, VMEM] + [ANY] * 8,
         out_specs=VMEM,
         scratch_shapes=[
             pltpu.VMEM((width, TILE, order), jnp.bfloat16),
@@ -581,39 +595,49 @@
         compiler_params=pltpu.CompilerParams(vmem_limit_bytes=56 * 2**20),
         cost_estimate=pl.CostEstimate(flops=4 * 10**9, bytes_accessed=12 * 10**6, transcendentals=0),
         name="update_trailing",
-    )(ids, next_map, keep, peer, rounded, shared)
-
-
-def update_two_kernel(ids_ref, near_ref, far_ref, round_ref, shared_ref, out_ref):
-    quarter = ids_ref[0] & 3
+    )(ids, next_map, keep, peer, rounded, *firsts, *seconds)
+
+
+def update_two_kernel(ids_ref, near_ref, far_ref, round_ref, *refs):
+    firsts, (out_ref, taken, sems) = refs[:4], refs[4:]
+    quarter, column = ids_ref[0] & 3, ids_ref[1]
     for i in range(3):
-        shared = shared_ref[(3 * quarter + i) & 3]
+        take_tile((3 * quarter + i) & 3, column, firsts, True, taken.at[i], sems.at[i])
+    for i in range(3):
         span = slice(i * TILE, (i + 1) * TILE)
+        pltpu.make_async_copy(firsts[0], taken.at[i], sems.at[i]).wait()
         for s in range(near_ref.shape[0]):
             total = near_ref[s, :, span].astype(jnp.float32) + far_ref[s, :, span].astype(jnp.float32)
-            out_ref[s, :, span] = (total - dot_lanes(round_ref[s], shared)).astype(jnp.bfloat16)
-
-
-def update_two(ids, near, far, rounded, shared):
+            out_ref[s, :, span] = (total - dot_lanes(round_ref[s], taken[i])).astype(jnp.bfloat16)
+
+
+def update_two(ids, near, far, rounded, firsts):
+    order = rounded.shape[-1]
     return pl.pallas_call(
         update_two_kernel,
         out_shape=jax.ShapeDtypeStruct(near.shape, jnp.bfloat16),
-        in_specs=[SMEM, VMEM, VMEM, VMEM, VMEM],
+        in_specs=[SMEM, VMEM, VMEM, VMEM] + [ANY] * 4,
         out_specs=VMEM,
-        compiler_params=PARAMS,
+        scratch_shapes=[pltpu.VMEM((3, TILE, order), jnp.bfloat16), pltpu.SemaphoreType.DMA((3,))],
+        compiler_params=pltpu.CompilerParams(vmem_limit_bytes=56 * 2**20),
         cost_estimate=pl.CostEstimate(flops=2 * 10**9, bytes_accessed=10**7, transcendentals=0),
         name="update_two",
-    )(ids, near, far, rounded, shared)
-
-
-def over_square(pack):
+    )(ids, near, far, rounded, *firsts)
+
+
+def over_square(pack, beside):
     half = pack.shape[0] // 2
-    x, y, core = swapped(pack, "leaf", 0), swapped(pack, "front", 1), swapped(pack, "front", 0)
-    top = swapped(y[:half], "leaf", 0)
-    low = swapped(x[half:], "front", 1)
-    x_core, y_core = swapped(x, "front", 0), swapped(y, "front", 0)
-    top_core, low_core = swapped(top, "front", 0), swapped(low, "front", 0)
+    x, y, core = swapped(pack, "leaf", 1), swapped(pack, "front", 2), swapped(pack, "front", 1)
+    x, y = lax.optimization_barrier((x, y, beside))[:2]
+    top = swapped(y[:half], "leaf", 1)
+    low = swapped(x[half:], "front", 2)
+    x_core, y_core = swapped(x, "front", 1), swapped(y, "front", 1)
+    top_core, low_core = swapped(top, "front", 1), swapped(low, "front", 1)
     return (pack, core, y, y_core, x, x_core, top, low, top_core, low_core)
+
+
+def over_front(tile, y, *earlier):
+    return (tile, swapped(tile, "front", 1), y, swapped(after(y, *earlier), "front", 1))
 
 
 def after(value, *earlier):
@@ -623,7 +647,7 @@
 def body(child_update, sep_one, sep_two, map_one, map_two, mask_one, mask_two):
     column = lax.axis_index("front")
     leaf = lax.axis_index("leaf")
-    half, side, quad = leaf & 1, (leaf >> 1) & 1, leaf >> 2
+    quad, quarter = leaf >> 2, leaf & 3
     ids = jnp.stack([leaf, column]).astype(jnp.int32)
     child = child_update[0, 0, 0]
     entries_one = sep_one[0, 0, 0]
@@ -633,56 +657,57 @@
     maps_one = map_one[:, 0]
     maps_two = map_two[:, 0]
 
-    packs = over_square(pick_pivot(ids, maps_one, child, entries_one))
+    pivot_mine = pick_pivot(ids, maps_one, child, entries_one)
     coupling_mine, sep_send, near_send, far_send, sep_keep, near_keep, far_keep = pick_rest(
         ids, maps_one, maps_two, child, entries_one
     )
-    coupling_peer = swapped(after(coupling_mine, packs[4]), "leaf", 0)
-    sep_peer = swapped(after(sep_send, packs[6]), "leaf", 0)
-    far_peer = swapped(after(far_send, packs[6]), "leaf", 0)
-    entries_near = swapped(after(entries_two, packs[6]), "leaf", 0)
-    entries_far = swapped(entries_near[0], "leaf", 1)
+    packs = over_square(pivot_mine, coupling_mine)
+    coupling_peer = swapped(after(coupling_mine, packs[4]), "leaf", 1)
+    sep_peer = swapped(after(sep_send, packs[6]), "leaf", 1)
+    far_peer = swapped(after(far_send, packs[6]), "leaf", 1)
+    entries_far = swapped(entries_two[0], "leaf", 2)
 
     lower, inverse = cholesky(ids, packs, fill_one, order)
-    factor_one, rounded, share = panel_one(
+    factor_one, rounded, first, second, third = panel_one(
         ids, mask_one.reshape(-1), maps_two, coupling_mine, coupling_peer, lower, inverse
     )
-    shared = lax.all_gather(after(share, sep_peer), "front", axis=0, tiled=True)
-    pivot_own, near_coupling, far_coupling = update_separator(
-        ids, maps_two, after(sep_keep, far_peer), sep_peer, rounded, shared
-    )
-
-    pivot_far = swapped(pivot_own, "leaf", 1)
+    first_y = swapped(first, "front", 2)
+    firsts = over_front(first, first_y, sep_peer)
+    pivot_own, near_coupling, far_coupling = update_separator(ids, maps_two, sep_keep, sep_peer, rounded, firsts)
+    second = jnp.where((leaf & 1) == (column & 1), second, swapped(third, "front", 1))
+    second_y = swapped(after(second, first_y), "front", 2)
+    seconds = over_front(second, second_y)
+
+    pivot_far = swapped(pivot_own, "leaf", 2)
     pivot_tile = (
         pivot_own.astype(jnp.float32)
         + jnp.concatenate([pivot_far[:, TILE:], pivot_far[:, :TILE]], axis=1).astype(jnp.float32)
-        + jnp.concatenate([entries_near[0], entries_far], axis=1).astype(jnp.float32)
+        + jnp.concatenate([entries_two[0], entries_far], axis=1).astype(jnp.float32)
     )
-    packs = over_square(pivot_tile)
     far_trailing = update_trailing(
-        ids, maps_two, far_keep, far_peer, after(rounded, pivot_far), shared, (5, 6, 7)
+        ids, maps_two, far_keep, far_peer, after(rounded, pivot_far), firsts, seconds, (5, 6, 7)
     )
-    coupling_far = swapped(after(far_coupling, pivot_far), "leaf", 1)
+    packs = over_square(after(pivot_tile, far_peer), far_trailing)
+    coupling_far = swapped(after(far_coupling, pivot_far), "leaf", 2)
     mask_second = lax.dynamic_index_in_dim(mask_two, quad, 0, keepdims=False).reshape(count, GROUPS, -1)
     mask_second = lax.dynamic_index_in_dim(mask_second, column, 1, keepdims=False)
-    mask_second = lax.dynamic_index_in_dim(mask_second, 2 * side + 1 - half, 1, keepdims=False)
+    mask_second = lax.dynamic_index_in_dim(mask_second, quarter, 1, keepdims=False)
     coupling = (
         near_coupling.astype(jnp.float32)
         + coupling_far.astype(jnp.float32)
-        + entries_near[1:].astype(jnp.float32) * mask_second.astype(jnp.float32)[:, None, None]
+        + entries_two[1:].astype(jnp.float32) * mask_second.astype(jnp.float32)[:, None, None]
     ).reshape(count * TILE, TILE)
-    coupling_x = swapped(after(coupling, packs[6]), "leaf", 0)
-    coupling_z = swapped(coupling, "leaf", 1)
-    coupling_xz = swapped(coupling_x, "leaf", 1)
-    trailing_far = swapped(after(far_trailing, coupling_x), "leaf", 1)
-    near_peer = swapped(after(near_send, coupling_x), "leaf", 0)
+    coupling = after(coupling, packs[4])
+    coupling_x, coupling_z, coupling_xz = (swapped(coupling, "leaf", mask) for mask in (1, 2, 3))
+    trailing_far = swapped(after(far_trailing, packs[4]), "leaf", 2)
+    near_peer = swapped(after(near_send, packs[6]), "leaf", 1)
     lower, inverse = cholesky(ids, packs, fill_two, order)
     factor_two, rounded_two, share = panel_two(
-        ids, (after(coupling, near_peer), coupling_x, coupling_z, coupling_xz), lower, inverse
+        ids, (coupling, coupling_x, coupling_z, coupling_xz), lower, inverse
     )
-    near_trailing = update_trailing(ids, maps_two, near_keep, near_peer, rounded, shared, (1, 2, 3))
-    shared = lax.all_gather(after(share, trailing_far)[None], "front", axis=0, tiled=True)
-    update = update_two(ids, near_trailing, trailing_far, rounded_two, shared)
+    near_trailing = update_trailing(ids, maps_two, near_keep, near_peer, rounded, firsts, seconds, (1, 2, 3))
+    shares = over_front(share, swapped(share, "front", 2), near_peer, trailing_far)
+    update = update_two(ids, near_trailing, trailing_far, rounded_two, shares)
     return (factor_one[None, None, None], factor_two[None, None, None], update[None, None, None])
 
 

time: 334 us -> 253 us (0.76)
  waiting for transfers between devices: 150 us -> 72.9 us
  between operations: 14.3 us -> 1.24 us
  starting transfers between devices: 27.2 us -> 31.9 us
  Pallas kernels: 128 us -> 132 us
    ppermute x30 -> x39, waiting for transfers between devices: 127 us -> 72.9 us  [swapped(): return lax.ppermute(value, axis, pairs)]
    all_gather x2 -> x0, waiting for transfers between devices: 22.4 us -> none  [the longest x1 16.6 us: body(): lax.all_gather(after(share, trailing_far)[None], 'front', axis=0, tiled=T...]
    ppermute x30 -> x39, starting transfers between devices: 26.9 us -> 31.9 us  [swapped(): return lax.ppermute(value, axis, pairs)]
    unnamed x41 -> x57, local copies, waits for them, and re-layouts: 8.21 us -> 6.2 us
  transfers between devices with their start and end apart: 32 -> 39, of which waited for: 15 -> 17; matrix products, arithmetic and copies ran while one was open for 1% -> 2% of each run, Pallas kernels for 37% -> 49%
where the time goes in v1:
time: 253 us; the launch traced here: 252 us
  Pallas kernels  132 us (52%)
  waiting for transfers between devices  72.9 us (29%)
  starting transfers between devices  31.9 us (13%)
  local copies, waits for them, and re-layouts  10.9 us (4%)
  other arithmetic  3.27 us (1%)
    pallas_call x2, Pallas kernels, cholesky(): pl.pallas_call(functools.partial(cholesky_kernel, fill), out_shape=(jax.S...  80.3 us
    ppermute x39, waiting for transfers between devices, swapped(): return lax.ppermute(value, axis, pairs)  72.9 us
    ppermute x39, starting transfers between devices, swapped(): return lax.ppermute(value, axis, pairs)  31.9 us
    pallas_call x2, Pallas kernels, update_trailing(): pl.pallas_call(functools.partial(update_trailing_kernel, positions), out_...  13.1 us
    pallas_call x1, Pallas kernels, panel_one(): pl.pallas_call(panel_one_kernel, out_shape=(jax.ShapeDtypeStruct((count +...  8.36 us
    pallas_call x1, Pallas kernels, pick_rest(): pl.pallas_call(pick_rest_kernel, out_shape=tuple((jax.ShapeDtypeStruct((c...  7.8 us
    pallas_call x1, Pallas kernels, panel_two(): pl.pallas_call(panel_two_kernel, out_shape=(jax.ShapeDtypeStruct((count +...  7.67 us
    pallas_call x1, Pallas kernels, update_two(): pl.pallas_call(update_two_kernel, out_shape=jax.ShapeDtypeStruct(near.sha...  6.34 us
  transfers between devices with their start and end apart: 39, of which 17 were waited for; matrix products, arithmetic and copies ran while one was open for 2% of the time, Pallas kernels for 49%

profile of v1, /device:TPU:0, one launch (start us, length us, event | category | flops | bytes accessed | tf_op | source)
XLA Modules:
  0.0 252.2 jit_solution(16136366323904267098)
XLA Ops:
  0.7 1.4 copy.20.map_ref
  2.6 2.9 %pick_pivot.1.refs_0_ = bf16[256,1536]{1,0:T(8,128)(2,1)} custom-call(s32[2]{0:T(128)} %pad_add_fusion.ids_ref, s32[8,4,3]{2,1,0:T(4,128)} %copy.20.map_ref, bf16[3,256,3072]{2,1,0:T(8,128)(2,1)} %bitcast.29, bf16[4,256,512]{2,1,0:T(8,128)(2,1)} %bitcast.31), custom_call_target="tpu_custom_call" | custom-call | tf_op jit(solution)/shard_map/pick_pivot/pallas_call | solution.py:297
  5.6 3.2 %collective-permute-start = (bf16[256,1536]{1,0:T(8,128)(2,1)}, bf16[256,1536]{1,0:T(8,128)(2,1)S(1)}, u32[]{:S(2)}, u32[]{:S(2)}) collective-permute-start(bf16[256,1536]{1,0:T(8,128)(2,1)} %pick_pivot.1.refs_0_), channel_id=1, source_target_pairs={{0,4},{4,0},{8,12},{12,8},{16,20},{20,16},{24,28},{28,24},{1,5},{5... | collective-permute-start | bytes 2359304 | tf_op jit(solution)/shard_map/ppermute | solution.py:227
  8.8 1.5 collective-permute-start.1
  11.0 7.8 %pick_rest.1 = (bf16[3,256,1536]{2,1,0:T(8,128)(2,1)}, bf16[3,256,512]{2,1,0:T(8,128)(2,1)}, bf16[3,256,768]{2,1,0:T(8,128)(2,1)}, bf16[3,256,768]{2,1,0:T(8,128...) custom-call(s32[2]{0:T(128)} %pad_add_fusion.ids_ref, ...), custom_call_target="tpu_custom_call" | custom-call | bytes 20000000 | tf_op jit(solution)/shard_map/pick_rest/pallas_call | solution.py:349
  18.8 7.7 %collective-permute-done.refs_4_ = bf16[256,1536]{1,0:T(8,128)(2,1)S(1)} collective-permute-done((bf16[256,1536]{1,0:T(8,128)(2,1)}, bf16[256,1536]{1,0:T(8,128)(2,1)S(1)}, u32[]{:S(2)}, u32[]{:S(2)}) %collective-permute-start) | collective-permute-done | bytes 786464 | tf_op jit(solution)/shard_map/ppermute | solution.py:227
  26.5 1.5 collective-permute-done.1.refs_2_
  28.5 1.7 collective-permute-start.7
  30.6 7.2 %collective-permute-done.6.refs_6_ = bf16[128,1536]{1,0:T(8,128)(2,1)} collective-permute-done((bf16[128,1536]{1,0:T(8,128)(2,1)S(1)}, bf16[128,1536]{1,0:T(8,128)(2,1)}, u32[]{:S(2)}, u32[]{:S(2)}) %collective-permute-start.6) | collective-permute-done | bytes 393248 | tf_op jit(solution)/shard_map/ppermute | solution.py:227
  38.6 1.4 collective-permute-start.2
  40.8 40.9 %cholesky.2 = (f32[1024,1024]{1,0:T(8,128)S(1)}, f32[4,256,256]{2,1,0:T(8,128)S(1)}) custom-call(s32[2]{0:T(128)S(1)} %copy-done.5, bf16[256,1536]{1,0:T(8,128)(2,1)S(1)} %copy-done.3, bf16[256,1536]{1,0:T(8,128)(2,1)S(1)} %collective-permute-done.3.refs_1_, bf16[256,1536]{1,0:T(8,128)(2,1)S(1)} %collective-permute-done.1.refs_2_, ...), custom_call_target="tpu_custom_call" | custom-call | flops 40000000000 | bytes 100000000 | tf_op jit(solution)/shard_map/cholesky/pallas_call | solution.py:204
  81.6 11.3 %collective-permute-done.2.peer_ref = bf16[3,256,1536]{2,1,0:T(8,128)(2,1)S(1)} collective-permute-done((bf16[3,256,1536]{2,1,0:T(8,128)(2,1)}, bf16[3,256,1536]{2,1,0:T(8,128)(2,1)S(1)}, u32[]{:S(2)}, u32[]{:S(2)}) %collective-permute-start.2) | collective-permute-done | bytes 2359328 | tf_op jit(solution)/shard_map/ppermute | solution.py:227
  92.9 8.4 %panel_one.1 = (f32[4,256,512]{2,1,0:T(8,128)}, bf16[3,256,1024]{2,1,0:T(8,128)(2,1)S(1)}, bf16[256,1024]{1,0:T(8,128)(2,1)S(1)}, bf16[256,1024]{1,0:T(8,128)(2,1)S(1)}, bf16[256,1024]{1,0:T(8,128)(2,1)S(1)}) custom-call(s32[2]{0:T(128)S(1)} %copy-done.5, s32[192]{0:T(256)S(1)} %reshape.23.mask_ref, s32[4,4,3]{2,1,0:T(4,128)S(1)} %bitcast.28, ...), custom_call_target="tpu_custom_call" | custom-call | flops 1000000000 | bytes 1000000 | tf_op jit(solution)/shard_map/panel_one/pallas_call | solution.py:429
  101.3 1.2 copy-done.7
  102.5 1.5 collective-permute-start.12
  104.5 4.9 %collective-permute-done.10.peer_ref = bf16[3,256,512]{2,1,0:T(8,128)(2,1)S(1)} collective-permute-done((bf16[3,256,512]{2,1,0:T(8,128)(2,1)}, bf16[3,256,512]{2,1,0:T(8,128)(2,1)S(1)}, u32[]{:S(2)}, u32[]{:S(2)}) %collective-permute-start.10) | collective-permute-done | bytes 786464 | tf_op jit(solution)/shard_map/ppermute | solution.py:227
  109.4 6.2 %collective-permute-done.12.refs_2_ = bf16[256,1024]{1,0:T(8,128)(2,1)S(1)} collective-permute-done((bf16[256,1024]{1,0:T(8,128)(2,1)S(1)}, bf16[256,1024]{1,0:T(8,128)(2,1)S(1)}, u32[]{:S(2)}, u32[]{:S(2)}) %collective-permute-start.12) | collective-permute-done | bytes 524320 | tf_op jit(solution)/shard_map/ppermute | solution.py:227
  115.6 1.5 collective-permute-start.17
  117.2 1.6 collective-permute-start.22
  119.7 5.5 %update_separator.1 = (bf16[256,512]{1,0:T(8,128)(2,1)}, bf16[3,256,256]{2,1,0:T(8,128)(2,1)}, bf16[3,256,256]{2,1,0:T(8,128)(2,1)}) custom-call(s32[2]{0:T(128)} %pad_add_fusion.ids_ref, s32[4,4,3]{2,1,0:T(4,128)} %bitcast.25, bf16[3,256,512]{2,1,0:T(8,128)(2,1)} %get-tuple-element.48.keep_ref, bf16[3,256,512]{2,1,0:T(8,128)(2,1)} %copy-done.18, ...), custom_call_target="tpu_custom_call" | custom-call | flops 3000000000 | bytes 10000000 | tf_op jit(solution)/shard_map/update_separator/pallas_call | solution.py:553
  125.2 1.6 collective-permute-start.14
  128.3 3.0 %collective-permute-done.22.refs_6_ = bf16[256,1024]{1,0:T(8,128)(2,1)S(1)} collective-permute-done((bf16[256,1024]{1,0:T(8,128)(2,1)S(1)}, bf16[256,1024]{1,0:T(8,128)(2,1)S(1)}, u32[]{:S(2)}, u32[]{:S(2)}) %collective-permute-start.22) | collective-permute-done | bytes 524320 | tf_op jit(solution)/shard_map/ppermute | solution.py:227
  131.3 3.3 %collective-permute-done.14 = bf16[256,512]{1,0:T(8,128)(2,1)S(1)} collective-permute-done((bf16[256,512]{1,0:T(8,128)(2,1)}, bf16[256,512]{1,0:T(8,128)(2,1)S(1)}, u32[]{:S(2)}, u32[]{:S(2)}) %collective-permute-start.14) | collective-permute-done | bytes 262176 | tf_op jit(solution)/shard_map/ppermute | solution.py:227
  134.7 1.7 collective-permute-done.16
  136.3 1.0 convert_add_fusion.refs_0_
  137.4 6.9 %collective-permute-done.17.peer_ref = bf16[3,256,768]{2,1,0:T(8,128)(2,1)S(1)} collective-permute-done((bf16[3,256,768]{2,1,0:T(8,128)(2,1)}, bf16[3,256,768]{2,1,0:T(8,128)(2,1)S(1)}, u32[]{:S(2)}, u32[]{:S(2)}) %collective-permute-start.17) | collective-permute-done | bytes 1179680 | tf_op jit(solution)/shard_map/ppermute | solution.py:227
  144.2 1.5 collective-permute-start.18
  145.7 1.5 collective-permute-start.19
  147.2 1.6 collective-permute-start.15
  149.8 6.5 %update_trailing.2 = bf16[3,256,768]{2,1,0:T(8,128)(2,1)} custom-call(s32[2]{0:T(128)} %pad_add_fusion.ids_ref, s32[4,4,3]{2,1,0:T(4,128)} %bitcast.26, bf16[3,256,768]{2,1,0:T(8,128)(2,1)} %get-tuple-element.61.keep_ref, bf16[3,256,768]{2,1,0:T(8,128)(2,1)} %copy-done.15, bf16[3,256,1024]{2,1,0:T(8,128)(2,1)} %copy-done.7, bf16[256,1024]{1,0:T(8,128)(2,1)} %copy-done.9, ...), custom_call_target="tpu_custom_call" | custom-call | flops 4000000000 | bytes 12000000 | tf_op jit(solution)/shard_map/update_trailing/pallas_call | solution.py:585
  156.3 1.4 collective-permute-done.18.refs_4_
  157.7 1.2 collective-permute-done.19.refs_2_
  160.9 1.4 collective-permute-start.31
  163.1 3.5 %collective-permute-done.30.refs_6_ = f32[128,512]{1,0:T(8,128)S(1)} collective-permute-done((f32[128,512]{1,0:T(8,128)}, f32[128,512]{1,0:T(8,128)S(1)}, u32[]{:S(2)}, u32[]{:S(2)}) %collective-permute-start.30) | collective-permute-done | bytes 262176 | tf_op jit(solution)/shard_map/ppermute | solution.py:227
  166.6 1.1 collective-permute-done.31.refs_7_
  167.7 1.4 fusion
  169.1 1.6 collective-permute-start.24
  170.7 1.6 collective-permute-start.25
  172.7 1.6 collective-permute-start.35
  174.3 1.5 collective-permute-start.34
  175.8 39.4 %cholesky.3 = (f32[1024,1024]{1,0:T(8,128)S(1)}, f32[4,256,256]{2,1,0:T(8,128)S(1)}) custom-call(s32[2]{0:T(128)S(1)} %copy-done.6, f32[256,512]{1,0:T(8,128)S(1)} %convert_add_fusion.refs_0_, f32[256,512]{1,0:T(8,128)S(1)} %collective-permute-done.27.refs_1_, f32[256,512]{1,0:T(8,128)S(1)} %collective-permute-done.19.refs_2_, ...), custom_call_target="tpu_custom_call" | custom-call | flops 40000000000 | bytes 100000000 | tf_op jit(solution)/shard_map/cholesky/pallas_call | solution.py:204
  215.3 7.7 %panel_two.1 = (f32[4,256,256]{2,1,0:T(8,128)}, bf16[3,256,1024]{2,1,0:T(8,128)(2,1)S(1)}, bf16[256,1024]{1,0:T(8,128)(2,1)S(1)}) custom-call(s32[2]{0:T(128)S(1)} %copy-done.6, f32[768,256]{1,0:T(8,128)S(1)} %bitcast.23, f32[768,256]{1,0:T(8,128)S(1)} %collective-permute-done.24.x_ref, f32[768,256]{1,0:T(8,128)S(1)} %collective-permute-done.25.z_ref, ...), custom_call_target="tpu_custom_call" | custom-call | flops 1000000000 | bytes 1000000 | tf_op jit(solution)/shard_map/panel_two/pallas_call | solution.py:475
  222.9 1.1 copy-done.8
  224.1 1.4 collective-permute-start.37
  225.5 7.0 %collective-permute-done.35.far_ref = bf16[3,256,768]{2,1,0:T(8,128)(2,1)S(1)} collective-permute-done((bf16[3,256,768]{2,1,0:T(8,128)(2,1)}, bf16[3,256,768]{2,1,0:T(8,128)(2,1)S(1)}, u32[]{:S(2)}, u32[]{:S(2)}) %collective-permute-start.35) | collective-permute-done | bytes 1179680 | tf_op jit(solution)/shard_map/ppermute | solution.py:227
  232.5 4.5 %collective-permute-done.37.refs_2_ = bf16[256,1024]{1,0:T(8,128)(2,1)S(1)} collective-permute-done((bf16[256,1024]{1,0:T(8,128)(2,1)S(1)}, bf16[256,1024]{1,0:T(8,128)(2,1)S(1)}, u32[]{:S(2)}, u32[]{:S(2)}) %collective-permute-start.37) | collective-permute-done | bytes 524320 | tf_op jit(solution)/shard_map/ppermute | solution.py:227
  238.1 6.6 %update_trailing.3.near_ref = bf16[3,256,768]{2,1,0:T(8,128)(2,1)} custom-call(s32[2]{0:T(128)} %pad_add_fusion.ids_ref, s32[4,4,3]{2,1,0:T(4,128)} %bitcast.27, bf16[3,256,768]{2,1,0:T(8,128)(2,1)} %get-tuple-element.72.keep_ref, bf16[3,256,768]{2,1,0:T(8,128)(2,1)} %copy-done.17, bf16[3,256,1024]{2,1,0:T(8,128)(2,1)} %copy-done.7, ...), custom_call_target="tpu_custom_call" | custom-call | flops 4000000000 | bytes 12000000 | tf_op jit(solution)/shard_map/update_trailing/pallas_call | solution.py:585
  245.7 6.3 %update_two.1 = bf16[3,256,768]{2,1,0:T(8,128)(2,1)} custom-call(s32[2]{0:T(128)} %pad_add_fusion.ids_ref, bf16[3,256,768]{2,1,0:T(8,128)(2,1)} %update_trailing.3.near_ref, bf16[3,256,768]{2,1,0:T(8,128)(2,1)} %copy-done.16, bf16[3,256,1024]{2,1,0:T(8,128)(2,1)} %copy-done.8, bf16[256,1024]{1,0:T(8,128)(2,1)} %copy-done.10, bf16[256,1024]{1,0:T(8,128)(2,1)} %copy-done.25, ...), custom_call_target="tpu_custom_call" | custom-call | flops 2000000000 | bytes 10000000 | tf_op jit(solution)/shard_map/update_two/pallas_call | solution.py:616
  (113 shorter events, 12.8 us)
Async XLA Ops:
  0.6 162.2 %copy-start = (s32[2,1,12,4]{2,3,1,0:T(4,128)S(1)}, s32[2,1,12,4]{2,3,1,0:T(4,128)}, u32[]{:S(2)}) copy-start(s32[2,1,12,4]{2,3,1,0:T(4,128)} %param.13) | copy-start | bytes 1156
  5.6 21.0 %collective-permute-start = (bf16[256,1536]{1,0:T(8,128)(2,1)}, bf16[256,1536]{1,0:T(8,128)(2,1)S(1)}, u32[]{:S(2)}, u32[]{:S(2)}) collective-permute-start(bf16[256,1536]{1,0:T(8,128)(2,1)} %pick_pivot.1.refs_0_), channel_id=1, source_target_pairs={{0,4},{4,0},{8,12},{12,8},{16,20},{20,16},{24,28},{28,24},{1,5},{5... | collective-permute-start | bytes 2359304 | tf_op jit(solution)/shard_map/ppermute | solution.py:227
  8.8 19.2 %collective-permute-start.1 = (bf16[256,1536]{1,0:T(8,128)(2,1)}, bf16[256,1536]{1,0:T(8,128)(2,1)S(1)}, u32[]{:S(2)}, u32[]{:S(2)}) collective-permute-start(bf16[256,1536]{1,0:T(8,128)(2,1)} %pick_pivot.1.refs_0_), channel_id=1, source_target_pairs={{0,2},{1,3},{2,0},{3,1},{4,6},{5,7},{6,4},{7,5},{8,10},{9,11},{10,... | collective-permute-start | bytes 2359304 | tf_op jit(solution)/shard_map/ppermute | solution.py:227
  10.3 28.3 %collective-permute-start.3 = (bf16[256,1536]{1,0:T(8,128)(2,1)}, bf16[256,1536]{1,0:T(8,128)(2,1)S(1)}, u32[]{:S(2)}, u32[]{:S(2)}) collective-permute-start(bf16[256,1536]{1,0:T(8,128)(2,1)} %pick_pivot.1.refs_0_), channel_id=1, source_target_pairs={{0,1},{1,0},{2,3},{3,2},{4,5},{5,4},{6,7},{7,6},{8,9},{9,8},{10,11... | collective-permute-start | bytes 2359304 | tf_op jit(solution)/shard_map/ppermute | solution.py:227
  18.8 19.6 %copy-start.12 = (s32[4,1,12,4]{2,3,1,0:T(4,128)S(1)}, s32[4,1,12,4]{2,3,1,0:T(4,128)}, u32[]{:S(2)}) copy-start(s32[4,1,12,4]{2,3,1,0:T(4,128)} %param.12) | copy-start | bytes 2308
  18.8 21.9 %copy-start.3 = (bf16[256,1536]{1,0:T(8,128)(2,1)S(1)}, bf16[256,1536]{1,0:T(8,128)(2,1)}, u32[]{:S(2)}) copy-start(bf16[256,1536]{1,0:T(8,128)(2,1)} %pick_pivot.1.refs_0_) | copy-start | bytes 2359300
  18.8 21.9 %copy-start.5 = (s32[2]{0:T(128)S(1)}, s32[2]{0:T(128)}, u32[]{:S(2)}) copy-start(s32[2]{0:T(128)} %pad_add_fusion.ids_ref) | copy-start | bytes 28
  28.0 9.8 %collective-permute-start.6 = (bf16[128,1536]{1,0:T(8,128)(2,1)S(1)}, bf16[128,1536]{1,0:T(8,128)(2,1)}, u32[]{:S(2)}, u32[]{:S(2)}) collective-permute-start(bf16[128,1536]{1,0:T(8,128)(2,1)S(1)} %slice.27), channel_id=1, source_target_pairs={{0,4},{4,0},{8,12},{12,8},{16,20},{20,16},{24,28},{28,24},{1,5},{5... | collective-permute-start | bytes 1179656 | tf_op jit(solution)/shard_map/ppermute | solution.py:227
  28.5 9.9 %collective-permute-start.7 = (bf16[128,1536]{1,0:T(8,128)(2,1)S(1)}, bf16[128,1536]{1,0:T(8,128)(2,1)}, u32[]{:S(2)}, u32[]{:S(2)}) collective-permute-start(bf16[128,1536]{1,0:T(8,128)(2,1)S(1)} %slice.28), channel_id=1, source_target_pairs={{0,2},{1,3},{2,0},{3,1},{4,6},{5,7},{6,4},{7,5},{8,10},{9,11},{10,... | collective-permute-start | bytes 1179656 | tf_op jit(solution)/shard_map/ppermute | solution.py:227
  30.1 10.6 %collective-permute-start.5 = (bf16[256,1536]{1,0:T(8,128)(2,1)S(1)}, bf16[256,1536]{1,0:T(8,128)(2,1)}, u32[]{:S(2)}, u32[]{:S(2)}) collective-permute-start(bf16[256,1536]{1,0:T(8,128)(2,1)S(1)} %collective-permute-done.refs_4_), channel_id=1, source_target_pairs={{0,1},{1,0},{2,3},{3,2},{4,5},{5,4},{6,7},{7,6},{8,9},{9,8},{10,11... | collective-permute-start | bytes 2359304 | tf_op jit(solution)/shard_map/ppermute | solution.py:227
  30.1 10.6 %collective-permute-start.4 = (bf16[256,1536]{1,0:T(8,128)(2,1)S(1)}, bf16[256,1536]{1,0:T(8,128)(2,1)}, u32[]{:S(2)}, u32[]{:S(2)}) collective-permute-start(bf16[256,1536]{1,0:T(8,128)(2,1)S(1)} %collective-permute-done.1.refs_2_), channel_id=1, source_target_pairs={{0,1},{1,0},{2,3},{3,2},{4,5},{5,4},{6,7},{7,6},{8,9},{9,8},{10,11... | collective-permute-start | bytes 2359304 | tf_op jit(solution)/shard_map/ppermute | solution.py:227
  37.9 2.2 collective-permute-start.8
  38.4 2.4 collective-permute-start.9
  38.6 54.3 %copy-start.4 = (s32[4,1,4,3]{3,2,0,1:T(4,128)S(1)}, s32[4,1,4,3]{3,2,0,1:T(4,128)}, u32[]{:S(2)}) copy-start(s32[4,1,4,3]{3,2,0,1:T(4,128)} %copy.27) | copy-start | bytes 580
  38.6 54.3 %collective-permute-start.2 = (bf16[3,256,1536]{2,1,0:T(8,128)(2,1)}, bf16[3,256,1536]{2,1,0:T(8,128)(2,1)S(1)}, u32[]{:S(2)}, u32[]{:S(2)}) collective-permute-start(bf16[3,256,1536]{2,1,0:T(8,128)(2,1)} %get-tuple-element.43.mine_ref), channel_id=1, source_target_pairs={{0,4},{4,0},{8,12},{12,8},{16,20},{20,16},{24,28},{28,24},{1,5},{5... | collective-permute-start | bytes 7077896 | tf_op jit(solution)/shard_map/ppermute | solution.py:227
  40.0 69.4 %collective-permute-start.10 = (bf16[3,256,512]{2,1,0:T(8,128)(2,1)}, bf16[3,256,512]{2,1,0:T(8,128)(2,1)S(1)}, u32[]{:S(2)}, u32[]{:S(2)}) collective-permute-start(bf16[3,256,512]{2,1,0:T(8,128)(2,1)} %get-tuple-element.50), channel_id=1, source_target_pairs={{0,4},{4,0},{8,12},{12,8},{16,20},{20,16},{24,28},{28,24},{1,5},{5... | collective-permute-start | bytes 2359304 | tf_op jit(solution)/shard_map/ppermute | solution.py:227
  40.7 52.2 %copy-start.2 = (bf16[3,256,1536]{2,1,0:T(8,128)(2,1)S(1)}, bf16[3,256,1536]{2,1,0:T(8,128)(2,1)}, u32[]{:S(2)}) copy-start(bf16[3,256,1536]{2,1,0:T(8,128)(2,1)} %get-tuple-element.43.mine_ref) | copy-start | bytes 7077892
  102.5 13.1 %collective-permute-start.12 = (bf16[256,1024]{1,0:T(8,128)(2,1)S(1)}, bf16[256,1024]{1,0:T(8,128)(2,1)S(1)}, u32[]{:S(2)}, u32[]{:S(2)}) collective-permute-start(bf16[256,1024]{1,0:T(8,128)(2,1)S(1)} %get-tuple-element.52.refs_0_), channel_id=1, source_target_pairs={{0,2},{1,3},{2,0},{3,1},{4,6},{5,7},{6,4},{7,5},{8,10},{9,11},{10,... | collective-permute-start | bytes 1572872 | tf_op jit(solution)/shard_map/ppermute | solution.py:227
  104.0 13.1 %collective-permute-start.20 = (bf16[256,1024]{1,0:T(8,128)(2,1)S(1)}, bf16[256,1024]{1,0:T(8,128)(2,1)S(1)}, u32[]{:S(2)}, u32[]{:S(2)}) collective-permute-start(bf16[256,1024]{1,0:T(8,128)(2,1)S(1)} %get-tuple-element.64), channel_id=1, source_target_pairs={{0,1},{1,0},{2,3},{3,2},{4,5},{5,4},{6,7},{7,6},{8,9},{9,8},{10,11... | collective-permute-start | bytes 1572872 | tf_op jit(solution)/shard_map/ppermute | solution.py:227
  104.0 14.8 %collective-permute-start.11 = (bf16[256,1024]{1,0:T(8,128)(2,1)S(1)}, bf16[256,1024]{1,0:T(8,128)(2,1)S(1)}, u32[]{:S(2)}, u32[]{:S(2)}) collective-permute-start(bf16[256,1024]{1,0:T(8,128)(2,1)S(1)} %get-tuple-element.52.refs_0_), channel_id=1, source_target_pairs={{0,1},{1,0},{2,3},{3,2},{4,5},{5,4},{6,7},{7,6},{8,9},{9,8},{10,11... | collective-permute-start | bytes 1572872 | tf_op jit(solution)/shard_map/ppermute | solution.py:227
  115.6 3.2 %collective-permute-start.13 = (bf16[256,1024]{1,0:T(8,128)(2,1)S(1)}, bf16[256,1024]{1,0:T(8,128)(2,1)}, u32[]{:S(2)}, u32[]{:S(2)}) collective-permute-start(bf16[256,1024]{1,0:T(8,128)(2,1)S(1)} %collective-permute-done.12.refs_2_), channel_id=1, source_target_pairs={{0,1},{1,0},{2,3},{3,2},{4,5},{5,4},{6,7},{7,6},{8,9},{9,8},{10,11... | collective-permute-start | bytes 1572872 | tf_op jit(solution)/shard_map/ppermute | solution.py:227
  115.6 28.6 %collective-permute-start.17 = (bf16[3,256,768]{2,1,0:T(8,128)(2,1)}, bf16[3,256,768]{2,1,0:T(8,128)(2,1)S(1)}, u32[]{:S(2)}, u32[]{:S(2)}) collective-permute-start(bf16[3,256,768]{2,1,0:T(8,128)(2,1)} %get-tuple-element.59), channel_id=1, source_target_pairs={{0,4},{4,0},{8,12},{12,8},{16,20},{20,16},{24,28},{28,24},{1,5},{5... | collective-permute-start | bytes 3538952 | tf_op jit(solution)/shard_map/ppermute | solution.py:227
  117.2 14.1 %collective-permute-start.22 = (bf16[256,1024]{1,0:T(8,128)(2,1)S(1)}, bf16[256,1024]{1,0:T(8,128)(2,1)S(1)}, u32[]{:S(2)}, u32[]{:S(2)}) collective-permute-start(bf16[256,1024]{1,0:T(8,128)(2,1)S(1)} %broadcast_select_fusion.refs_4_), channel_id=1, source_target_pairs={{0,2},{1,3},{2,0},{3,1},{4,6},{5,7},{6,4},{7,5},{8,10},{9,11},{10,... | collective-permute-start | bytes 1572872 | tf_op jit(solution)/shard_map/ppermute | solution.py:227
  125.2 22.0 %copy-start.27 = (bf16[3,256,256]{2,1,0:T(8,128)(2,1)S(1)}, bf16[3,256,256]{2,1,0:T(8,128)(2,1)}, u32[]{:S(2)}) copy-start(bf16[3,256,256]{2,1,0:T(8,128)(2,1)} %get-tuple-element.57) | copy-start | bytes 1179652
  125.2 9.5 %collective-permute-start.14 = (bf16[256,512]{1,0:T(8,128)(2,1)}, bf16[256,512]{1,0:T(8,128)(2,1)S(1)}, u32[]{:S(2)}, u32[]{:S(2)}) collective-permute-start(bf16[256,512]{1,0:T(8,128)(2,1)} %get-tuple-element.56), channel_id=1, source_target_pairs={{0,8},{4,12},{8,0},{12,4},{16,24},{20,28},{24,16},{28,20},{1,9},{5... | collective-permute-start | bytes 786440 | tf_op jit(solution)/shard_map/ppermute | solution.py:227
  127.7 8.6 %collective-permute-start.16 = (bf16[256,256]{1,0:T(8,128)(2,1)S(1)}, bf16[256,256]{1,0:T(8,128)(2,1)S(1)}, u32[]{:S(2)}, u32[]{:S(2)}) collective-permute-start(bf16[256,256]{1,0:T(8,128)(2,1)S(1)} %slice_bitcast_fusion), channel_id=1, source_target_pairs={{0,8},{4,12},{8,0},{12,4},{16,24},{20,28},{24,16},{28,20},{1,9},{5... | collective-permute-start | bytes 393224 | tf_op jit(solution)/shard_map/ppermute | solution.py:227
  128.3 20.6 %collective-permute-start.21 = (bf16[256,1024]{1,0:T(8,128)(2,1)S(1)}, bf16[256,1024]{1,0:T(8,128)(2,1)S(1)}, u32[]{:S(2)}, u32[]{:S(2)}) collective-permute-start(bf16[256,1024]{1,0:T(8,128)(2,1)S(1)} %broadcast_select_fusion.refs_4_), channel_id=1, source_target_pairs={{0,1},{1,0},{2,3},{3,2},{4,5},{5,4},{6,7},{7,6},{8,9},{9,8},{10,11... | collective-permute-start | bytes 1572872 | tf_op jit(solution)/shard_map/ppermute | solution.py:227
  131.3 17.5 %copy-start.21 = (bf16[256,1024]{1,0:T(8,128)(2,1)}, bf16[256,1024]{1,0:T(8,128)(2,1)S(1)}, u32[]{:S(2)}) copy-start(bf16[256,1024]{1,0:T(8,128)(2,1)S(1)} %collective-permute-done.22.refs_6_) | copy-start | bytes 1572868
  131.3 17.5 %collective-permute-start.23 = (bf16[256,1024]{1,0:T(8,128)(2,1)S(1)}, bf16[256,1024]{1,0:T(8,128)(2,1)S(1)}, u32[]{:S(2)}, u32[]{:S(2)}) collective-permute-start(bf16[256,1024]{1,0:T(8,128)(2,1)S(1)} %collective-permute-done.22.refs_6_), channel_id=1, source_target_pairs={{0,1},{1,0},{2,3},{3,2},{4,5},{5,4},{6,7},{7,6},{8,9},{9,8},{10,11... | collective-permute-start | bytes 1572872 | tf_op jit(solution)/shard_map/ppermute | solution.py:227
  144.2 13.5 %collective-permute-start.18 = (f32[256,512]{1,0:T(8,128)S(1)}, f32[256,512]{1,0:T(8,128)S(1)}, u32[]{:S(2)}, u32[]{:S(2)}) collective-permute-start(f32[256,512]{1,0:T(8,128)S(1)} %convert_add_fusion.refs_0_), channel_id=1, source_target_pairs={{0,4},{4,0},{8,12},{12,8},{16,20},{20,16},{24,28},{28,24},{1,5},{5... | collective-permute-start | bytes 1572872 | tf_op jit(solution)/shard_map/ppermute | solution.py:227
  145.7 13.2 %collective-permute-start.19 = (f32[256,512]{1,0:T(8,128)S(1)}, f32[256,512]{1,0:T(8,128)S(1)}, u32[]{:S(2)}, u32[]{:S(2)}) collective-permute-start(f32[256,512]{1,0:T(8,128)S(1)} %convert_add_fusion.refs_0_), channel_id=1, source_target_pairs={{0,2},{1,3},{2,0},{3,1},{4,6},{5,7},{6,4},{7,5},{8,10},{9,11},{10,... | collective-permute-start | bytes 1572872 | tf_op jit(solution)/shard_map/ppermute | solution.py:227
  147.2 15.6 %collective-permute-start.15 = (bf16[3,256,256]{2,1,0:T(8,128)(2,1)S(1)}, bf16[3,256,256]{2,1,0:T(8,128)(2,1)}, u32[]{:S(2)}, u32[]{:S(2)}) collective-permute-start(bf16[3,256,256]{2,1,0:T(8,128)(2,1)S(1)} %copy-done.27), channel_id=1, source_target_pairs={{0,8},{4,12},{8,0},{12,4},{16,24},{20,28},{24,16},{28,20},{1,9},{5... | collective-permute-start | bytes 1179656 | tf_op jit(solution)/shard_map/ppermute | solution.py:227
  159.6 7.0 %collective-permute-start.30 = (f32[128,512]{1,0:T(8,128)}, f32[128,512]{1,0:T(8,128)S(1)}, u32[]{:S(2)}, u32[]{:S(2)}) collective-permute-start(f32[128,512]{1,0:T(8,128)} %slice.33), channel_id=1, source_target_pairs={{0,4},{4,0},{8,12},{12,8},{16,20},{20,16},{24,28},{28,24},{1,5},{5... | collective-permute-start | bytes 786440 | tf_op jit(solution)/shard_map/ppermute | solution.py:227
  160.9 6.8 %collective-permute-start.31 = (f32[128,512]{1,0:T(8,128)}, f32[128,512]{1,0:T(8,128)}, u32[]{:S(2)}, u32[]{:S(2)}) collective-permute-start(f32[128,512]{1,0:T(8,128)} %slice.34), channel_id=1, source_target_pairs={{0,2},{1,3},{2,0},{3,1},{4,6},{5,7},{6,4},{7,5},{8,10},{9,11},{10,... | collective-permute-start | bytes 786440 | tf_op jit(solution)/shard_map/ppermute | solution.py:227
  162.3 6.8 %collective-permute-start.27 = (f32[256,512]{1,0:T(8,128)S(1)}, f32[256,512]{1,0:T(8,128)S(1)}, u32[]{:S(2)}, u32[]{:S(2)}) collective-permute-start(f32[256,512]{1,0:T(8,128)S(1)} %convert_add_fusion.refs_0_), channel_id=1, source_target_pairs={{0,1},{1,0},{2,3},{3,2},{4,5},{5,4},{6,7},{7,6},{8,9},{9,8},{10,11... | collective-permute-start | bytes 1572872 | tf_op jit(solution)/shard_map/ppermute | solution.py:227
  162.3 8.4 %collective-permute-start.28 = (f32[256,512]{1,0:T(8,128)S(1)}, f32[256,512]{1,0:T(8,128)S(1)}, u32[]{:S(2)}, u32[]{:S(2)}) collective-permute-start(f32[256,512]{1,0:T(8,128)S(1)} %collective-permute-done.19.refs_2_), channel_id=1, source_target_pairs={{0,1},{1,0},{2,3},{3,2},{4,5},{5,4},{6,7},{7,6},{8,9},{9,8},{10,11... | collective-permute-start | bytes 1572872 | tf_op jit(solution)/shard_map/ppermute | solution.py:227
  162.8 9.4 %collective-permute-start.29 = (f32[256,512]{1,0:T(8,128)S(1)}, f32[256,512]{1,0:T(8,128)S(1)}, u32[]{:S(2)}, u32[]{:S(2)}) collective-permute-start(f32[256,512]{1,0:T(8,128)S(1)} %collective-permute-done.18.refs_4_), channel_id=1, source_target_pairs={{0,1},{1,0},{2,3},{3,2},{4,5},{5,4},{6,7},{7,6},{8,9},{9,8},{10,11... | collective-permute-start | bytes 1572872 | tf_op jit(solution)/shard_map/ppermute | solution.py:227
  166.6 6.1 %collective-permute-start.32 = (f32[128,512]{1,0:T(8,128)S(1)}, f32[128,512]{1,0:T(8,128)S(1)}, u32[]{:S(2)}, u32[]{:S(2)}) collective-permute-start(f32[128,512]{1,0:T(8,128)S(1)} %collective-permute-done.30.refs_6_), channel_id=1, source_target_pairs={{0,1},{1,0},{2,3},{3,2},{4,5},{5,4},{6,7},{7,6},{8,9},{9,8},{10,11... | collective-permute-start | bytes 786440 | tf_op jit(solution)/shard_map/ppermute | solution.py:227
  167.7 6.6 %collective-permute-start.33 = (f32[128,512]{1,0:T(8,128)}, f32[128,512]{1,0:T(8,128)S(1)}, u32[]{:S(2)}, u32[]{:S(2)}) collective-permute-start(f32[128,512]{1,0:T(8,128)} %collective-permute-done.31.refs_7_), channel_id=1, source_target_pairs={{0,1},{1,0},{2,3},{3,2},{4,5},{5,4},{6,7},{7,6},{8,9},{9,8},{10,11... | collective-permute-start | bytes 786440 | tf_op jit(solution)/shard_map/ppermute | solution.py:227
  169.1 46.1 %collective-permute-start.24 = (f32[768,256]{1,0:T(8,128)S(1)}, f32[768,256]{1,0:T(8,128)S(1)}, u32[]{:S(2)}, u32[]{:S(2)}) collective-permute-start(f32[768,256]{1,0:T(8,128)S(1)} %bitcast.20), channel_id=1, source_target_pairs={{0,4},{4,0},{8,12},{12,8},{16,20},{20,16},{24,28},{28,24},{1,5},{5... | collective-permute-start | bytes 2359304 | tf_op jit(solution)/shard_map/ppermute | solution.py:227
  170.7 44.6 %collective-permute-start.25 = (f32[768,256]{1,0:T(8,128)S(1)}, f32[768,256]{1,0:T(8,128)S(1)}, u32[]{:S(2)}, u32[]{:S(2)}) collective-permute-start(f32[768,256]{1,0:T(8,128)S(1)} %bitcast.21), channel_id=1, source_target_pairs={{0,8},{4,12},{8,0},{12,4},{16,24},{20,28},{24,16},{28,20},{1,9},{5... | collective-permute-start | bytes 2359304 | tf_op jit(solution)/shard_map/ppermute | solution.py:227
  172.3 43.0 %collective-permute-start.26 = (f32[768,256]{1,0:T(8,128)S(1)}, f32[768,256]{1,0:T(8,128)S(1)}, u32[]{:S(2)}, u32[]{:S(2)}) collective-permute-start(f32[768,256]{1,0:T(8,128)S(1)} %bitcast.22), channel_id=1, source_target_pairs={{0,12},{4,8},{8,4},{12,0},{16,28},{20,24},{24,20},{28,16},{1,13},{... | collective-permute-start | bytes 2359304 | tf_op jit(solution)/shard_map/ppermute | solution.py:227
  172.7 59.8 %collective-permute-start.35 = (bf16[3,256,768]{2,1,0:T(8,128)(2,1)}, bf16[3,256,768]{2,1,0:T(8,128)(2,1)S(1)}, u32[]{:S(2)}, u32[]{:S(2)}) collective-permute-start(bf16[3,256,768]{2,1,0:T(8,128)(2,1)} %update_trailing.2), channel_id=1, source_target_pairs={{0,8},{4,12},{8,0},{12,4},{16,24},{20,28},{24,16},{28,20},{1,9},{5... | collective-permute-start | bytes 3538952 | tf_op jit(solution)/shard_map/ppermute | solution.py:227
  174.3 62.7 %collective-permute-start.34 = (bf16[3,256,768]{2,1,0:T(8,128)(2,1)S(1)}, bf16[3,256,768]{2,1,0:T(8,128)(2,1)S(1)}, u32[]{:S(2)}, u32[]{:S(2)}) collective-permute-start(bf16[3,256,768]{2,1,0:T(8,128)(2,1)S(1)} %copy-done.14), channel_id=1, source_target_pairs={{0,4},{4,0},{8,12},{12,8},{16,20},{20,16},{24,28},{28,24},{1,5},{5... | collective-permute-start | bytes 3538952 | tf_op jit(solution)/shard_map/ppermute | solution.py:227
  224.1 20.6 %copy-start.10 = (bf16[256,1024]{1,0:T(8,128)(2,1)}, bf16[256,1024]{1,0:T(8,128)(2,1)S(1)}, u32[]{:S(2)}) copy-start(bf16[256,1024]{1,0:T(8,128)(2,1)S(1)} %get-tuple-element.77.refs_0_) | copy-start | bytes 1572868
  224.1 12.9 %collective-permute-start.37 = (bf16[256,1024]{1,0:T(8,128)(2,1)S(1)}, bf16[256,1024]{1,0:T(8,128)(2,1)S(1)}, u32[]{:S(2)}, u32[]{:S(2)}) collective-permute-start(bf16[256,1024]{1,0:T(8,128)(2,1)S(1)} %get-tuple-element.77.refs_0_), channel_id=1, source_target_pairs={{0,2},{1,3},{2,0},{3,1},{4,6},{5,7},{6,4},{7,5},{8,10},{9,11},{10,... | collective-permute-start | bytes 1572872 | tf_op jit(solution)/shard_map/ppermute | solution.py:227
  225.5 19.2 %collective-permute-start.36 = (bf16[256,1024]{1,0:T(8,128)(2,1)S(1)}, bf16[256,1024]{1,0:T(8,128)(2,1)S(1)}, u32[]{:S(2)}, u32[]{:S(2)}) collective-permute-start(bf16[256,1024]{1,0:T(8,128)(2,1)S(1)} %get-tuple-element.77.refs_0_), channel_id=1, source_target_pairs={{0,1},{1,0},{2,3},{3,2},{4,5},{5,4},{6,7},{7,6},{8,9},{9,8},{10,11... | collective-permute-start | bytes 1572872 | tf_op jit(solution)/shard_map/ppermute | solution.py:227
  237.1 7.7 %collective-permute-start.38 = (bf16[256,1024]{1,0:T(8,128)(2,1)S(1)}, bf16[256,1024]{1,0:T(8,128)(2,1)S(1)}, u32[]{:S(2)}, u32[]{:S(2)}) collective-permute-start(bf16[256,1024]{1,0:T(8,128)(2,1)S(1)} %collective-permute-done.37.refs_2_), channel_id=1, source_target_pairs={{0,1},{1,0},{2,3},{3,2},{4,5},{5,4},{6,7},{7,6},{8,9},{9,8},{10,11... | collective-permute-start | bytes 1572872 | tf_op jit(solution)/shard_map/ppermute | solution.py:227
  (19 other events, 102.9 us)

commit v2 on v1

--- a/solution.py
+++ b/solution.py
@@ -49,6 +49,12 @@
 
 def spread_row(ref, index):
     return jnp.broadcast_to(ref[index], (GRP, BLK))
+
+
+def tree_sum(parts):
+    while len(parts) > 1:
+        parts = [parts[k] + parts[k + 1] for k in range(0, len(parts), 2)]
+    return parts[0]
 
 
 def factor_diagonal(block, done_ref, pivot_ref, rows_ref):
@@ -72,39 +78,51 @@
                 entry[i, m] = entry[m, i]
         left = [jnp.broadcast_to(rows_ref[slot, m : m + 1, 0:BLK], (GRP, BLK)) for m in range(GRP)]
         right = [jnp.broadcast_to(rows_ref[slot, m : m + 1, BLK:], (GRP, BLK)) for m in range(GRP)]
-        for i in range(GRP):
-            root = lax.rsqrt(entry[i, i])
-            scale = root * root
-            done_ref[first + i : first + i + 1, 0:BLK] = (left[i] * root)[0:1]
-            done_ref[first + i : first + i + 1, BLK:] = (right[i] * root)[0:1]
-            left[i] = left[i] * scale
-            right[i] = right[i] * scale
-            scaled = {c: entry[i, c] * scale for c in range(i + 1, GRP)}
+        for i in range(0, GRP, 2):
+            n = i + 1
+            a, b, c = entry[i, i], entry[n, i], entry[n, n]
+            root = lax.rsqrt(a)
+            root_both = lax.rsqrt(a * c - b * b)
+            scale = root_both * root_both
+            second_root = root * root_both
+
+            def solve(x, y):
+                return c * x - b * y, a * y - b * x
+
+            solved = {}
+            for name, rows_now in (("left", left), ("right", right)):
+                raw = solve(rows_now[i], rows_now[n])
+                lanes = slice(0, BLK) if name == "left" else slice(BLK, 2 * BLK)
+                done_ref[first + i : first + i + 1, lanes] = (rows_now[i] * root)[0:1]
+                done_ref[first + n : first + n + 1, lanes] = (raw[1] * second_root)[0:1]
+                rows_now[i], rows_now[n] = raw[0] * scale, raw[1] * scale
+            for col in range(i + 2, GRP):
+                raw = solve(entry[i, col], entry[n, col])
+                solved[col] = (raw[0] * scale, raw[1] * scale)
             for m in range(GRP):
-                if m == i:
+                if m in (i, n):
                     continue
-                weight = entry[m, i]
-                left[m] = left[m] - weight * left[i]
-                right[m] = right[m] - weight * right[i]
-                for c in range(i + 1, GRP):
-                    if m > c:
+                weight, other = entry[m, i], entry[m, n]
+                for rows_now in (left, right):
+                    rows_now[m] = rows_now[m] - (weight * rows_now[i] + other * rows_now[n])
+                for col in range(i + 2, GRP):
+                    if m > col:
                         continue
-                    entry[m, c] = entry[m, c] - weight * scaled[c]
-            for m in range(i + 1, GRP):
-                for c in range(i + 1, m):
-                    entry[m, c] = entry[c, m]
-            for c in range(i + 1, GRP):
-                entry[i, c] = scaled[c]
+                    entry[m, col] = entry[m, col] - (weight * solved[col][0] + other * solved[col][1])
+            for m in range(i + 2, GRP):
+                for col in range(i + 2, m):
+                    entry[m, col] = entry[col, m]
+            for col in range(i + 2, GRP):
+                entry[i, col], entry[n, col] = solved[col]
         for later in range(g + 1, steps):
             rows = matrix[later]
-            total_left, total_right = None, None
+            parts_left, parts_right = [], []
             for i in range(GRP):
                 weight = jnp.broadcast_to(rows[:, first + i : first + i + 1], (GRP, BLK))
-                part_left, part_right = weight * left[i], weight * right[i]
-                total_left = part_left if total_left is None else total_left + part_left
-                total_right = part_right if total_right is None else total_right + part_right
-            matrix[later] = rows - total_left
-            inverse[later] = inverse[later] - total_right
+                parts_left.append(weight * left[i])
+                parts_right.append(weight * right[i])
+            matrix[later] = rows - tree_sum(parts_left)
+            inverse[later] = inverse[later] - tree_sum(parts_right)
 
 
 def fill_one(ids_ref, packs, work):
@@ -225,6 +243,17 @@
 def swapped(value, axis, mask):
     pairs = [(source, source ^ mask) for source in range(lax.axis_size(axis))]
     return lax.ppermute(value, axis, pairs)
+
+
+def swapped_heavy(value, mask):
+    groups = lax.axis_size("front")
+    pairs = [
+        (leaf * groups + column, leaf * groups + (column ^ mask))
+        for leaf in range(lax.axis_size("leaf"))
+        for column in range(groups)
+        if (leaf & 1) == (column & 1)
+    ]
+    return lax.ppermute(value, ("leaf", "front"), pairs)
 
 
 def find_tile(map_ref, owner, group, slot, count):
@@ -414,7 +443,8 @@
     for s in range(count):
         round_ref[s] = rounded[s * TILE : (s + 1) * TILE]
     write_factor(column, half, lower_ref, panel, factor_ref)
-    for a, share_ref in enumerate((first_ref, second_ref, third_ref)):
+    heavy = half == (column & 1)
+    for a, share_ref in ((0, first_ref), (jnp.where(heavy, 1, 0), second_ref), (2, third_ref)):
         slot = jnp.int32(0)
         for target in column_targets(half, 0):
             hit = jnp.logical_and((target & 3) == column, share_place(target, half) == a)
@@ -496,7 +526,7 @@
             pltpu.make_async_copy(ref, target, sem).start()
 
 
-def start_shared(ids_ref, positions, firsts, seconds, taken, sems):
+def start_shared(ids_ref, positions, firsts, thirds, taken, sems):
     leaf, column = ids_ref[0], ids_ref[1]
     half, side = leaf & 1, (leaf >> 1) & 1
     targets = column_targets(half, side)
@@ -505,9 +535,9 @@
         target = targets[position]
         group = target & 3
         place = share_place(target, half)
-        take_tile(group, column, firsts, place == 0, taken.at[i], sems.at[i])
-        if seconds:
-            take_tile(jnp.where(place == 2, group ^ 1, group), column, seconds, place > 0, taken.at[i], sems.at[i])
+        take_tile(group, column, firsts, place < 2, taken.at[i], sems.at[i])
+        if thirds:
+            take_tile(group, column, thirds, place == 2, taken.at[i], sems.at[i])
         copies.append(pltpu.make_async_copy(firsts[0], taken.at[i], sems.at[i]))
     return copies
 
@@ -561,7 +591,7 @@
             pltpu.SemaphoreType.DMA((2,)),
         ],
         compiler_params=pltpu.CompilerParams(vmem_limit_bytes=56 * 2**20),
-        cost_estimate=pl.CostEstimate(flops=3 * 10**9, bytes_accessed=10**7, transcendentals=0),
+        cost_estimate=pl.CostEstimate(flops=10**8, bytes_accessed=10**5, transcendentals=0),
         name="update_separator",
     )(ids, next_map, keep, peer, rounded, *firsts)
 
@@ -569,17 +599,17 @@
 def update_trailing_kernel(
     positions, ids_ref, next_ref, keep_ref, peer_ref, round_ref, *refs
 ):
-    firsts, seconds, (out_ref, taken, tiles, sems) = refs[:4], refs[4:8], refs[8:]
+    seconds, thirds, (out_ref, taken, tiles, sems) = refs[:4], refs[4:8], refs[8:]
 
     def write(i, slot, tile):
         if slot:
             out_ref[slot - 1, :, i * TILE : (i + 1) * TILE] = tile()
 
-    copies = start_shared(ids_ref, positions, firsts, seconds, taken, sems)
+    copies = start_shared(ids_ref, positions, seconds, thirds, taken, sems)
     update_columns(ids_ref, next_ref, positions, copies, keep_ref, peer_ref, round_ref, taken, tiles, write)
 
 
-def update_trailing(ids, next_map, keep, peer, rounded, firsts, seconds, positions):
+def update_trailing(ids, next_map, keep, peer, rounded, seconds, thirds, positions):
     count, _, order = rounded.shape
     width = len(positions)
     return pl.pallas_call(
@@ -595,7 +625,7 @@
         compiler_params=pltpu.CompilerParams(vmem_limit_bytes=56 * 2**20),
         cost_estimate=pl.CostEstimate(flops=4 * 10**9, bytes_accessed=12 * 10**6, transcendentals=0),
         name="update_trailing",
-    )(ids, next_map, keep, peer, rounded, *firsts, *seconds)
+    )(ids, next_map, keep, peer, rounded, *seconds, *thirds)
 
 
 def update_two_kernel(ids_ref, near_ref, far_ref, round_ref, *refs):
@@ -640,6 +670,10 @@
     return (tile, swapped(tile, "front", 1), y, swapped(after(y, *earlier), "front", 1))
 
 
+def over_heavy(tile, y, *earlier):
+    return (tile, swapped_heavy(tile, 1), y, swapped_heavy(after(y, *earlier), 1))
+
+
 def after(value, *earlier):
     return lax.optimization_barrier((value, *earlier))[0]
 
@@ -671,12 +705,12 @@
     factor_one, rounded, first, second, third = panel_one(
         ids, mask_one.reshape(-1), maps_two, coupling_mine, coupling_peer, lower, inverse
     )
-    first_y = swapped(first, "front", 2)
-    firsts = over_front(first, first_y, sep_peer)
+    first_y = swapped_heavy(first, 2)
+    firsts = over_heavy(first, first_y, sep_peer)
     pivot_own, near_coupling, far_coupling = update_separator(ids, maps_two, sep_keep, sep_peer, rounded, firsts)
-    second = jnp.where((leaf & 1) == (column & 1), second, swapped(third, "front", 1))
     second_y = swapped(after(second, first_y), "front", 2)
     seconds = over_front(second, second_y)
+    thirds = over_heavy(third, swapped_heavy(after(third, first_y), 2))
 
     pivot_far = swapped(pivot_own, "leaf", 2)
     pivot_tile = (
@@ -685,7 +719,7 @@
         + jnp.concatenate([entries_two[0], entries_far], axis=1).astype(jnp.float32)
     )
     far_trailing = update_trailing(
-        ids, maps_two, far_keep, far_peer, after(rounded, pivot_far), firsts, seconds, (5, 6, 7)
+        ids, maps_two, far_keep, far_peer, after(rounded, pivot_far), seconds, thirds, (5, 6, 7)
     )
     packs = over_square(after(pivot_tile, far_peer), far_trailing)
     coupling_far = swapped(after(far_coupling, pivot_far), "leaf", 2)
@@ -705,8 +739,8 @@
     factor_two, rounded_two, share = panel_two(
         ids, (coupling, coupling_x, coupling_z, coupling_xz), lower, inverse
     )
-    near_trailing = update_trailing(ids, maps_two, near_keep, near_peer, rounded, firsts, seconds, (1, 2, 3))
-    shares = over_front(share, swapped(share, "front", 2), near_peer, trailing_far)
+    near_trailing = update_trailing(ids, maps_two, near_keep, near_peer, rounded, seconds, thirds, (1, 2, 3))
+    shares = over_front(share, swapped(share, "front", 2), near_trailing, trailing_far)
     update = update_two(ids, near_trailing, trailing_far, rounded_two, shares)
     return (factor_one[None, None, None], factor_two[None, None, None], update[None, None, None])
 

time: 253 us -> 245 us (0.968)
  Pallas kernels: 132 us -> 120 us
  starting transfers between devices: 31.9 us -> 39.7 us
  waiting for transfers between devices: 72.9 us -> 69 us
    pallas_call x2, Pallas kernels: 80.3 us -> 67.9 us  [cholesky(): pl.pallas_call(functools.partial(cholesky_kernel, fill), out_shape=(jax.S...]
    ppermute x0 -> x6, starting transfers between devices: none -> 12.1 us  [swapped_heavy(): return lax.ppermute(value, ('leaf', 'front'), pairs)]
    ppermute x39 -> x35, waiting for transfers between devices: 72.9 us -> 64.5 us  [swapped(): return lax.ppermute(value, axis, pairs)]
    ppermute x0 -> x6, waiting for transfers between devices: none -> 4.52 us  [swapped_heavy(): return lax.ppermute(value, ('leaf', 'front'), pairs)]
    ppermute x39 -> x35, starting transfers between devices: 31.9 us -> 27.6 us  [swapped(): return lax.ppermute(value, axis, pairs)]
    unnamed x57 -> x65, local copies, waits for them, and re-layouts: 6.2 us -> 6.29 us
  transfers between devices with their start and end apart: 39 -> 41, of which waited for: 17 -> 15; matrix products, arithmetic and copies ran while one was open for 2% -> 2% of each run, Pallas kernels for 49% -> 45%
where the time goes in v2:
time: 245 us; the launch traced here: 244 us
  Pallas kernels  120 us (49%)
  waiting for transfers between devices  69 us (28%)
  starting transfers between devices  39.7 us (16%)
  local copies, waits for them, and re-layouts  11 us (4%)
  other arithmetic  3.29 us (1%)
    pallas_call x2, Pallas kernels, cholesky(): pl.pallas_call(functools.partial(cholesky_kernel, fill), out_shape=(jax.S...  67.9 us
    ppermute x35, waiting for transfers between devices, swapped(): return lax.ppermute(value, axis, pairs)  64.5 us
    ppermute x35, starting transfers between devices, swapped(): return lax.ppermute(value, axis, pairs)  27.6 us
    pallas_call x2, Pallas kernels, update_trailing(): pl.pallas_call(functools.partial(update_trailing_kernel, positions), out_...  13.2 us
    ppermute x6, starting transfers between devices, swapped_heavy(): return lax.ppermute(value, ('leaf', 'front'), pairs)  12.1 us
    pallas_call x1, Pallas kernels, panel_one(): pl.pallas_call(panel_one_kernel, out_shape=(jax.ShapeDtypeStruct((count +...  8.38 us
    pallas_call x1, Pallas kernels, pick_rest(): pl.pallas_call(pick_rest_kernel, out_shape=tuple((jax.ShapeDtypeStruct((c...  7.83 us
    pallas_call x1, Pallas kernels, panel_two(): pl.pallas_call(panel_two_kernel, out_shape=(jax.ShapeDtypeStruct((count +...  7.67 us
  transfers between devices with their start and end apart: 41, of which 15 were waited for; matrix products, arithmetic and copies ran while one was open for 2% of the time, Pallas kernels for 45%

profile of v2, /device:TPU:0, one launch (start us, length us, event | category | flops | bytes accessed | tf_op | source)
XLA Modules:
  0.0 244.0 jit_solution(15368396464189534448)
XLA Ops:
  0.7 1.4 copy.20.map_ref
  2.7 2.9 %pick_pivot.1.refs_0_ = bf16[256,1536]{1,0:T(8,128)(2,1)} custom-call(s32[2]{0:T(128)} %pad_add_fusion.ids_ref, s32[8,4,3]{2,1,0:T(4,128)} %copy.20.map_ref, bf16[3,256,3072]{2,1,0:T(8,128)(2,1)} %bitcast.29, bf16[4,256,512]{2,1,0:T(8,128)(2,1)} %bitcast.31), custom_call_target="tpu_custom_call" | custom-call | tf_op jit(solution)/shard_map/pick_pivot/pallas_call | solution.py:326
  5.6 3.2 %collective-permute-start = (bf16[256,1536]{1,0:T(8,128)(2,1)}, bf16[256,1536]{1,0:T(8,128)(2,1)S(1)}, u32[]{:S(2)}, u32[]{:S(2)}) collective-permute-start(bf16[256,1536]{1,0:T(8,128)(2,1)} %pick_pivot.1.refs_0_), channel_id=1, source_target_pairs={{0,4},{4,0},{8,12},{12,8},{16,20},{20,16},{24,28},{28,24},{1,5},{5... | collective-permute-start | bytes 2359304 | tf_op jit(solution)/shard_map/ppermute | solution.py:245
  8.8 1.5 collective-permute-start.1
  11.0 7.8 %pick_rest.1 = (bf16[3,256,1536]{2,1,0:T(8,128)(2,1)}, bf16[3,256,512]{2,1,0:T(8,128)(2,1)}, bf16[3,256,768]{2,1,0:T(8,128)(2,1)}, bf16[3,256,768]{2,1,0:T(8,128...) custom-call(s32[2]{0:T(128)} %pad_add_fusion.ids_ref, ...), custom_call_target="tpu_custom_call" | custom-call | bytes 20000000 | tf_op jit(solution)/shard_map/pick_rest/pallas_call | solution.py:378
  18.9 7.7 %collective-permute-done.refs_4_ = bf16[256,1536]{1,0:T(8,128)(2,1)S(1)} collective-permute-done((bf16[256,1536]{1,0:T(8,128)(2,1)}, bf16[256,1536]{1,0:T(8,128)(2,1)S(1)}, u32[]{:S(2)}, u32[]{:S(2)}) %collective-permute-start) | collective-permute-done | bytes 786464 | tf_op jit(solution)/shard_map/ppermute | solution.py:245
  26.6 1.5 collective-permute-done.1.refs_2_
  28.5 1.7 collective-permute-start.7
  30.7 7.2 %collective-permute-done.6.refs_6_ = bf16[128,1536]{1,0:T(8,128)(2,1)} collective-permute-done((bf16[128,1536]{1,0:T(8,128)(2,1)S(1)}, bf16[128,1536]{1,0:T(8,128)(2,1)}, u32[]{:S(2)}, u32[]{:S(2)}) %collective-permute-start.6) | collective-permute-done | bytes 393248 | tf_op jit(solution)/shard_map/ppermute | solution.py:245
  38.7 1.4 collective-permute-start.2
  40.8 34.8 %cholesky.2 = (f32[1024,1024]{1,0:T(8,128)S(1)}, f32[4,256,256]{2,1,0:T(8,128)S(1)}) custom-call(s32[2]{0:T(128)S(1)} %copy-done.7, bf16[256,1536]{1,0:T(8,128)(2,1)S(1)} %copy-done.4, bf16[256,1536]{1,0:T(8,128)(2,1)S(1)} %collective-permute-done.3.refs_1_, bf16[256,1536]{1,0:T(8,128)(2,1)S(1)} %collective-permute-done.1.refs_2_, ...), custom_call_target="tpu_custom_call" | custom-call | flops 40000000000 | bytes 100000000 | tf_op jit(solution)/shard_map/cholesky/pallas_call | solution.py:222
  75.6 17.4 %collective-permute-done.2.peer_ref = bf16[3,256,1536]{2,1,0:T(8,128)(2,1)S(1)} collective-permute-done((bf16[3,256,1536]{2,1,0:T(8,128)(2,1)}, bf16[3,256,1536]{2,1,0:T(8,128)(2,1)S(1)}, u32[]{:S(2)}, u32[]{:S(2)}) %collective-permute-start.2) | collective-permute-done | bytes 2359328 | tf_op jit(solution)/shard_map/ppermute | solution.py:245
  93.0 8.4 %panel_one.1 = (f32[4,256,512]{2,1,0:T(8,128)}, bf16[3,256,1024]{2,1,0:T(8,128)(2,1)S(1)}, bf16[256,1024]{1,0:T(8,128)(2,1)S(1)}, bf16[256,1024]{1,0:T(8,128)(2,1)S(1)}, bf16[256,1024]{1,0:T(8,128)(2,1)S(1)}) custom-call(s32[2]{0:T(128)S(1)} %copy-done.7, s32[192]{0:T(256)S(1)} %reshape.23.mask_ref, s32[4,4,3]{2,1,0:T(4,128)S(1)} %bitcast.28, ...), custom_call_target="tpu_custom_call" | custom-call | flops 1000000000 | bytes 1000000 | tf_op jit(solution)/shard_map/panel_one/pallas_call | solution.py:459
  101.4 1.2 copy-done.3
  102.5 3.3 %collective-permute-start.12 = (bf16[256,1024]{1,0:T(8,128)(2,1)S(1)}, bf16[256,1024]{1,0:T(8,128)(2,1)S(1)}, u32[]{:S(2)}, u32[]{:S(2)}) collective-permute-start(bf16[256,1024]{1,0:T(8,128)(2,1)S(1)} %get-tuple-element.53.refs_0_), channel_id=1, source_target_pairs={{0,2},{2,0},{5,7},{7,5},{8,10},{10,8},{13,15},{15,13},{16,18},{18,... | collective-permute-start | bytes 1572872 | tf_op jit(solution)/shard_map/ppermute | solution.py:256
  105.9 1.3 collective-permute-start.11
  107.2 2.2 collective-permute-done.10.peer_ref
  109.4 4.2 %collective-permute-done.12.refs_2_ = bf16[256,1024]{1,0:T(8,128)(2,1)S(1)} collective-permute-done((bf16[256,1024]{1,0:T(8,128)(2,1)S(1)}, bf16[256,1024]{1,0:T(8,128)(2,1)S(1)}, u32[]{:S(2)}, u32[]{:S(2)}) %collective-permute-start.12) | collective-permute-done | bytes 524320 | tf_op jit(solution)/shard_map/ppermute | solution.py:256
  113.6 1.3 collective-permute-start.13
  115.0 3.5 %collective-permute-start.24 = (bf16[256,1024]{1,0:T(8,128)(2,1)S(1)}, bf16[256,1024]{1,0:T(8,128)(2,1)S(1)}, u32[]{:S(2)}, u32[]{:S(2)}) collective-permute-start(bf16[256,1024]{1,0:T(8,128)(2,1)S(1)} %get-tuple-element.67.refs_4_), channel_id=1, source_target_pairs={{0,2},{2,0},{5,7},{7,5},{8,10},{10,8},{13,15},{15,13},{16,18},{18,... | collective-permute-start | bytes 1572872 | tf_op jit(solution)/shard_map/ppermute | solution.py:256
  120.2 5.4 %update_separator.1 = (bf16[256,512]{1,0:T(8,128)(2,1)}, bf16[3,256,256]{2,1,0:T(8,128)(2,1)}, bf16[3,256,256]{2,1,0:T(8,128)(2,1)}) custom-call(s32[2]{0:T(128)} %pad_add_fusion.ids_ref, s32[4,4,3]{2,1,0:T(4,128)} %bitcast.25, bf16[3,256,512]{2,1,0:T(8,128)(2,1)} %get-tuple-element.49.keep_ref, bf16[3,256,512]{2,1,0:T(8,128)(2,1)} %copy-done.13, ...), custom_call_target="tpu_custom_call" | custom-call | flops 100000000 | bytes 100000 | tf_op jit(solution)/shard_map/update_separator/pallas_call | solution.py:583
  125.7 1.7 collective-permute-start.14
  129.1 5.6 %collective-permute-done.21.refs_2_ = bf16[256,1024]{1,0:T(8,128)(2,1)S(1)} collective-permute-done((bf16[256,1024]{1,0:T(8,128)(2,1)S(1)}, bf16[256,1024]{1,0:T(8,128)(2,1)S(1)}, u32[]{:S(2)}, u32[]{:S(2)}) %collective-permute-start.21) | collective-permute-done | bytes 524320 | tf_op jit(solution)/shard_map/ppermute | solution.py:245
  134.7 1.3 collective-permute-start.23
  136.1 1.3 collective-permute-start.25
  137.5 1.0 convert_add_fusion.refs_0_
  138.6 2.4 collective-permute-done.17.peer_ref
  140.9 1.7 collective-permute-start.18
  142.7 1.2 collective-permute-start.19
  143.8 2.0 collective-permute-start.15
  146.9 6.5 %update_trailing.2 = bf16[3,256,768]{2,1,0:T(8,128)(2,1)} custom-call(s32[2]{0:T(128)} %pad_add_fusion.ids_ref, s32[4,4,3]{2,1,0:T(4,128)} %bitcast.26, bf16[3,256,768]{2,1,0:T(8,128)(2,1)} %get-tuple-element.62.keep_ref, bf16[3,256,768]{2,1,0:T(8,128)(2,1)} %copy-done.20, bf16[3,256,1024]{2,1,0:T(8,128)(2,1)} %copy-done.3, bf16[256,1024]{1,0:T(8,128)(2,1)} %copy-done.10, ...), custom_call_target="tpu_custom_call" | custom-call | flops 4000000000 | bytes 12000000 | tf_op jit(solution)/shard_map/update_trailing/pallas_call | solution.py:615
  153.5 1.4 collective-permute-done.19.refs_2_
  158.4 3.8 %collective-permute-done.32.refs_6_ = f32[128,512]{1,0:T(8,128)S(1)} collective-permute-done((f32[128,512]{1,0:T(8,128)}, f32[128,512]{1,0:T(8,128)S(1)}, u32[]{:S(2)}, u32[]{:S(2)}) %collective-permute-start.32) | collective-permute-done | bytes 262176 | tf_op jit(solution)/shard_map/ppermute | solution.py:245
  162.2 1.2 collective-permute-done.33.refs_7_
  163.4 1.4 fusion
  164.8 1.7 collective-permute-start.26
  166.6 1.6 collective-permute-start.27
  168.4 1.6 collective-permute-start.37
  170.0 1.7 collective-permute-start.36
  171.7 33.1 %cholesky.3 = (f32[1024,1024]{1,0:T(8,128)S(1)}, f32[4,256,256]{2,1,0:T(8,128)S(1)}) custom-call(s32[2]{0:T(128)S(1)} %copy-done.8, f32[256,512]{1,0:T(8,128)S(1)} %convert_add_fusion.refs_0_, f32[256,512]{1,0:T(8,128)S(1)} %collective-permute-done.29.refs_1_, f32[256,512]{1,0:T(8,128)S(1)} %collective-permute-done.19.refs_2_, ...), custom_call_target="tpu_custom_call" | custom-call | flops 40000000000 | bytes 100000000 | tf_op jit(solution)/shard_map/cholesky/pallas_call | solution.py:222
  204.8 7.7 %panel_two.1 = (f32[4,256,256]{2,1,0:T(8,128)}, bf16[3,256,1024]{2,1,0:T(8,128)(2,1)S(1)}, bf16[256,1024]{1,0:T(8,128)(2,1)S(1)}) custom-call(s32[2]{0:T(128)S(1)} %copy-done.8, f32[768,256]{1,0:T(8,128)S(1)} %bitcast.23, f32[768,256]{1,0:T(8,128)S(1)} %collective-permute-done.26.x_ref, f32[768,256]{1,0:T(8,128)S(1)} %collective-permute-done.27.z_ref, ...), custom_call_target="tpu_custom_call" | custom-call | flops 1000000000 | bytes 1000000 | tf_op jit(solution)/shard_map/panel_two/pallas_call | solution.py:505
  212.5 1.1 copy-done.9
  213.7 1.5 collective-permute-start.39
  215.2 11.8 %collective-permute-done.36.peer_ref = bf16[3,256,768]{2,1,0:T(8,128)(2,1)S(1)} collective-permute-done((bf16[3,256,768]{2,1,0:T(8,128)(2,1)S(1)}, bf16[3,256,768]{2,1,0:T(8,128)(2,1)S(1)}, u32[]{:S(2)}, u32[]{:S(2)}) %collective-permute-start.36) | collective-permute-done | bytes 1179680 | tf_op jit(solution)/shard_map/ppermute | solution.py:245
  227.0 1.0 copy-done.21
  228.0 6.6 %update_trailing.3.near_ref = bf16[3,256,768]{2,1,0:T(8,128)(2,1)} custom-call(s32[2]{0:T(128)} %pad_add_fusion.ids_ref, s32[4,4,3]{2,1,0:T(4,128)} %bitcast.27, bf16[3,256,768]{2,1,0:T(8,128)(2,1)} %get-tuple-element.74.keep_ref, bf16[3,256,768]{2,1,0:T(8,128)(2,1)} %copy-done.21, bf16[3,256,1024]{2,1,0:T(8,128)(2,1)} %copy-done.3, ...), custom_call_target="tpu_custom_call" | custom-call | flops 4000000000 | bytes 12000000 | tf_op jit(solution)/shard_map/update_trailing/pallas_call | solution.py:615
  234.8 1.9 collective-permute-done.40.refs_3_
  237.5 6.3 %update_two.1 = bf16[3,256,768]{2,1,0:T(8,128)(2,1)} custom-call(s32[2]{0:T(128)} %pad_add_fusion.ids_ref, bf16[3,256,768]{2,1,0:T(8,128)(2,1)} %update_trailing.3.near_ref, bf16[3,256,768]{2,1,0:T(8,128)(2,1)} %collective-permute-done.37.far_ref, bf16[3,256,1024]{2,1,0:T(8,128)(2,1)} %copy-done.9, bf16[256,1024]{1,0:T(8,128)(2,1)} %copy-done.12, ...), custom_call_target="tpu_custom_call" | custom-call | flops 2000000000 | bytes 10000000 | tf_op jit(solution)/shard_map/update_two/pallas_call | solution.py:646
  (124 shorter events, 13.0 us)
Async XLA Ops:
  0.6 157.5 %copy-start = (s32[2,1,12,4]{2,3,1,0:T(4,128)S(1)}, s32[2,1,12,4]{2,3,1,0:T(4,128)}, u32[]{:S(2)}) copy-start(s32[2,1,12,4]{2,3,1,0:T(4,128)} %param.13) | copy-start | bytes 1156
  5.6 20.9 %collective-permute-start = (bf16[256,1536]{1,0:T(8,128)(2,1)}, bf16[256,1536]{1,0:T(8,128)(2,1)S(1)}, u32[]{:S(2)}, u32[]{:S(2)}) collective-permute-start(bf16[256,1536]{1,0:T(8,128)(2,1)} %pick_pivot.1.refs_0_), channel_id=1, source_target_pairs={{0,4},{4,0},{8,12},{12,8},{16,20},{20,16},{24,28},{28,24},{1,5},{5... | collective-permute-start | bytes 2359304 | tf_op jit(solution)/shard_map/ppermute | solution.py:245
  8.8 19.2 %collective-permute-start.1 = (bf16[256,1536]{1,0:T(8,128)(2,1)}, bf16[256,1536]{1,0:T(8,128)(2,1)S(1)}, u32[]{:S(2)}, u32[]{:S(2)}) collective-permute-start(bf16[256,1536]{1,0:T(8,128)(2,1)} %pick_pivot.1.refs_0_), channel_id=1, source_target_pairs={{0,2},{1,3},{2,0},{3,1},{4,6},{5,7},{6,4},{7,5},{8,10},{9,11},{10,... | collective-permute-start | bytes 2359304 | tf_op jit(solution)/shard_map/ppermute | solution.py:245
  10.3 28.3 %collective-permute-start.3 = (bf16[256,1536]{1,0:T(8,128)(2,1)}, bf16[256,1536]{1,0:T(8,128)(2,1)S(1)}, u32[]{:S(2)}, u32[]{:S(2)}) collective-permute-start(bf16[256,1536]{1,0:T(8,128)(2,1)} %pick_pivot.1.refs_0_), channel_id=1, source_target_pairs={{0,1},{1,0},{2,3},{3,2},{4,5},{5,4},{6,7},{7,6},{8,9},{9,8},{10,11... | collective-permute-start | bytes 2359304 | tf_op jit(solution)/shard_map/ppermute | solution.py:245
  18.9 21.9 %copy-start.4 = (bf16[256,1536]{1,0:T(8,128)(2,1)S(1)}, bf16[256,1536]{1,0:T(8,128)(2,1)}, u32[]{:S(2)}) copy-start(bf16[256,1536]{1,0:T(8,128)(2,1)} %pick_pivot.1.refs_0_) | copy-start | bytes 2359300
  18.9 21.9 %copy-start.7 = (s32[2]{0:T(128)S(1)}, s32[2]{0:T(128)}, u32[]{:S(2)}) copy-start(s32[2]{0:T(128)} %pad_add_fusion.ids_ref) | copy-start | bytes 28
  28.1 9.8 %collective-permute-start.6 = (bf16[128,1536]{1,0:T(8,128)(2,1)S(1)}, bf16[128,1536]{1,0:T(8,128)(2,1)}, u32[]{:S(2)}, u32[]{:S(2)}) collective-permute-start(bf16[128,1536]{1,0:T(8,128)(2,1)S(1)} %slice.27), channel_id=1, source_target_pairs={{0,4},{4,0},{8,12},{12,8},{16,20},{20,16},{24,28},{28,24},{1,5},{5... | collective-permute-start | bytes 1179656 | tf_op jit(solution)/shard_map/ppermute | solution.py:245
  28.5 9.9 %collective-permute-start.7 = (bf16[128,1536]{1,0:T(8,128)(2,1)S(1)}, bf16[128,1536]{1,0:T(8,128)(2,1)}, u32[]{:S(2)}, u32[]{:S(2)}) collective-permute-start(bf16[128,1536]{1,0:T(8,128)(2,1)S(1)} %slice.28), channel_id=1, source_target_pairs={{0,2},{1,3},{2,0},{3,1},{4,6},{5,7},{6,4},{7,5},{8,10},{9,11},{10,... | collective-permute-start | bytes 1179656 | tf_op jit(solution)/shard_map/ppermute | solution.py:245
  30.2 10.5 %collective-permute-start.5 = (bf16[256,1536]{1,0:T(8,128)(2,1)S(1)}, bf16[256,1536]{1,0:T(8,128)(2,1)}, u32[]{:S(2)}, u32[]{:S(2)}) collective-permute-start(bf16[256,1536]{1,0:T(8,128)(2,1)S(1)} %collective-permute-done.refs_4_), channel_id=1, source_target_pairs={{0,1},{1,0},{2,3},{3,2},{4,5},{5,4},{6,7},{7,6},{8,9},{9,8},{10,11... | collective-permute-start | bytes 2359304 | tf_op jit(solution)/shard_map/ppermute | solution.py:245
  30.2 10.5 %collective-permute-start.4 = (bf16[256,1536]{1,0:T(8,128)(2,1)S(1)}, bf16[256,1536]{1,0:T(8,128)(2,1)}, u32[]{:S(2)}, u32[]{:S(2)}) collective-permute-start(bf16[256,1536]{1,0:T(8,128)(2,1)S(1)} %collective-permute-done.1.refs_2_), channel_id=1, source_target_pairs={{0,1},{1,0},{2,3},{3,2},{4,5},{5,4},{6,7},{7,6},{8,9},{9,8},{10,11... | collective-permute-start | bytes 2359304 | tf_op jit(solution)/shard_map/ppermute | solution.py:245
  37.9 2.2 collective-permute-start.8
  38.4 2.4 collective-permute-start.9
  38.6 54.3 %copy-start.6 = (s32[4,1,4,3]{3,2,0,1:T(4,128)S(1)}, s32[4,1,4,3]{3,2,0,1:T(4,128)}, u32[]{:S(2)}) copy-start(s32[4,1,4,3]{3,2,0,1:T(4,128)} %copy.27) | copy-start | bytes 580
  38.7 54.3 %collective-permute-start.2 = (bf16[3,256,1536]{2,1,0:T(8,128)(2,1)}, bf16[3,256,1536]{2,1,0:T(8,128)(2,1)S(1)}, u32[]{:S(2)}, u32[]{:S(2)}) collective-permute-start(bf16[3,256,1536]{2,1,0:T(8,128)(2,1)} %get-tuple-element.44.mine_ref), channel_id=1, source_target_pairs={{0,4},{4,0},{8,12},{12,8},{16,20},{20,16},{24,28},{28,24},{1,5},{5... | collective-permute-start | bytes 7077896 | tf_op jit(solution)/shard_map/ppermute | solution.py:245
  40.1 69.4 %collective-permute-start.10 = (bf16[3,256,512]{2,1,0:T(8,128)(2,1)}, bf16[3,256,512]{2,1,0:T(8,128)(2,1)S(1)}, u32[]{:S(2)}, u32[]{:S(2)}) collective-permute-start(bf16[3,256,512]{2,1,0:T(8,128)(2,1)} %get-tuple-element.51), channel_id=1, source_target_pairs={{0,4},{4,0},{8,12},{12,8},{16,20},{20,16},{24,28},{28,24},{1,5},{5... | collective-permute-start | bytes 2359304 | tf_op jit(solution)/shard_map/ppermute | solution.py:245
  40.8 52.2 %copy-start.2 = (bf16[3,256,1536]{2,1,0:T(8,128)(2,1)S(1)}, bf16[3,256,1536]{2,1,0:T(8,128)(2,1)}, u32[]{:S(2)}) copy-start(bf16[3,256,1536]{2,1,0:T(8,128)(2,1)} %get-tuple-element.44.mine_ref) | copy-start | bytes 7077892
  102.5 26.6 %copy-start.10 = (bf16[256,1024]{1,0:T(8,128)(2,1)}, bf16[256,1024]{1,0:T(8,128)(2,1)S(1)}, u32[]{:S(2)}) copy-start(bf16[256,1024]{1,0:T(8,128)(2,1)S(1)} %get-tuple-element.65.refs_0_) | copy-start | bytes 1572868
  102.5 32.2 %copy-start.11 = (bf16[256,1024]{1,0:T(8,128)(2,1)}, bf16[256,1024]{1,0:T(8,128)(2,1)S(1)}, u32[]{:S(2)}) copy-start(bf16[256,1024]{1,0:T(8,128)(2,1)S(1)} %get-tuple-element.67.refs_4_) | copy-start | bytes 1572868
  102.5 11.1 %collective-permute-start.12 = (bf16[256,1024]{1,0:T(8,128)(2,1)S(1)}, bf16[256,1024]{1,0:T(8,128)(2,1)S(1)}, u32[]{:S(2)}, u32[]{:S(2)}) collective-permute-start(bf16[256,1024]{1,0:T(8,128)(2,1)S(1)} %get-tuple-element.53.refs_0_), channel_id=1, source_target_pairs={{0,2},{2,0},{5,7},{7,5},{8,10},{10,8},{13,15},{15,13},{16,18},{18,... | collective-permute-start | bytes 1572872 | tf_op jit(solution)/shard_map/ppermute | solution.py:256
  105.9 13.4 %collective-permute-start.11 = (bf16[256,1024]{1,0:T(8,128)(2,1)S(1)}, bf16[256,1024]{1,0:T(8,128)(2,1)S(1)}, u32[]{:S(2)}, u32[]{:S(2)}) collective-permute-start(bf16[256,1024]{1,0:T(8,128)(2,1)S(1)} %get-tuple-element.53.refs_0_), channel_id=1, source_target_pairs={{0,1},{2,3},{5,4},{7,6},{8,9},{10,11},{13,12},{15,14},{16,17},{18,... | collective-permute-start | bytes 1572872 | tf_op jit(solution)/shard_map/ppermute | solution.py:256
  113.6 5.6 %collective-permute-start.13 = (bf16[256,1024]{1,0:T(8,128)(2,1)S(1)}, bf16[256,1024]{1,0:T(8,128)(2,1)S(1)}, u32[]{:S(2)}, u32[]{:S(2)}) collective-permute-start(bf16[256,1024]{1,0:T(8,128)(2,1)S(1)} %collective-permute-done.12.refs_2_), channel_id=1, source_target_pairs={{0,1},{2,3},{5,4},{7,6},{8,9},{10,11},{13,12},{15,14},{16,17},{18,... | collective-permute-start | bytes 1572872 | tf_op jit(solution)/shard_map/ppermute | solution.py:256
  114.9 26.0 %collective-permute-start.17 = (bf16[3,256,768]{2,1,0:T(8,128)(2,1)}, bf16[3,256,768]{2,1,0:T(8,128)(2,1)S(1)}, u32[]{:S(2)}, u32[]{:S(2)}) collective-permute-start(bf16[3,256,768]{2,1,0:T(8,128)(2,1)} %get-tuple-element.60), channel_id=1, source_target_pairs={{0,4},{4,0},{8,12},{12,8},{16,20},{20,16},{24,28},{28,24},{1,5},{5... | collective-permute-start | bytes 3538952 | tf_op jit(solution)/shard_map/ppermute | solution.py:245
  115.0 14.1 %collective-permute-start.24 = (bf16[256,1024]{1,0:T(8,128)(2,1)S(1)}, bf16[256,1024]{1,0:T(8,128)(2,1)S(1)}, u32[]{:S(2)}, u32[]{:S(2)}) collective-permute-start(bf16[256,1024]{1,0:T(8,128)(2,1)S(1)} %get-tuple-element.67.refs_4_), channel_id=1, source_target_pairs={{0,2},{2,0},{5,7},{7,5},{8,10},{10,8},{13,15},{15,13},{16,18},{18,... | collective-permute-start | bytes 1572872 | tf_op jit(solution)/shard_map/ppermute | solution.py:256
  118.6 16.2 %collective-permute-start.21 = (bf16[256,1024]{1,0:T(8,128)(2,1)S(1)}, bf16[256,1024]{1,0:T(8,128)(2,1)S(1)}, u32[]{:S(2)}, u32[]{:S(2)}) collective-permute-start(bf16[256,1024]{1,0:T(8,128)(2,1)S(1)} %get-tuple-element.65.refs_0_), channel_id=1, source_target_pairs={{0,2},{1,3},{2,0},{3,1},{4,6},{5,7},{6,4},{7,5},{8,10},{9,11},{10,... | collective-permute-start | bytes 1572872 | tf_op jit(solution)/shard_map/ppermute | solution.py:245
  125.7 11.7 %collective-permute-start.14 = (bf16[256,512]{1,0:T(8,128)(2,1)}, bf16[256,512]{1,0:T(8,128)(2,1)S(1)}, u32[]{:S(2)}, u32[]{:S(2)}) collective-permute-start(bf16[256,512]{1,0:T(8,128)(2,1)} %get-tuple-element.57), channel_id=1, source_target_pairs={{0,8},{4,12},{8,0},{12,4},{16,24},{20,28},{24,16},{28,20},{1,9},{5... | collective-permute-start | bytes 786440 | tf_op jit(solution)/shard_map/ppermute | solution.py:245
  128.3 7.7 %collective-permute-start.16 = (bf16[256,256]{1,0:T(8,128)(2,1)S(1)}, bf16[256,256]{1,0:T(8,128)(2,1)S(1)}, u32[]{:S(2)}, u32[]{:S(2)}) collective-permute-start(bf16[256,256]{1,0:T(8,128)(2,1)S(1)} %slice_bitcast_fusion), channel_id=1, source_target_pairs={{0,8},{4,12},{8,0},{12,4},{16,24},{20,28},{24,16},{28,20},{1,9},{5... | collective-permute-start | bytes 393224 | tf_op jit(solution)/shard_map/ppermute | solution.py:245
  129.1 13.6 %collective-permute-start.20 = (bf16[256,1024]{1,0:T(8,128)(2,1)S(1)}, bf16[256,1024]{1,0:T(8,128)(2,1)S(1)}, u32[]{:S(2)}, u32[]{:S(2)}) collective-permute-start(bf16[256,1024]{1,0:T(8,128)(2,1)S(1)} %get-tuple-element.65.refs_0_), channel_id=1, source_target_pairs={{0,1},{1,0},{2,3},{3,2},{4,5},{5,4},{6,7},{7,6},{8,9},{9,8},{10,11... | collective-permute-start | bytes 1572872 | tf_op jit(solution)/shard_map/ppermute | solution.py:245
  134.7 9.1 %collective-permute-start.23 = (bf16[256,1024]{1,0:T(8,128)(2,1)S(1)}, bf16[256,1024]{1,0:T(8,128)(2,1)S(1)}, u32[]{:S(2)}, u32[]{:S(2)}) collective-permute-start(bf16[256,1024]{1,0:T(8,128)(2,1)S(1)} %get-tuple-element.67.refs_4_), channel_id=1, source_target_pairs={{0,1},{2,3},{5,4},{7,6},{8,9},{10,11},{13,12},{15,14},{16,17},{18,... | collective-permute-start | bytes 1572872 | tf_op jit(solution)/shard_map/ppermute | solution.py:256
  136.1 9.8 %collective-permute-start.25 = (bf16[256,1024]{1,0:T(8,128)(2,1)S(1)}, bf16[256,1024]{1,0:T(8,128)(2,1)S(1)}, u32[]{:S(2)}, u32[]{:S(2)}) collective-permute-start(bf16[256,1024]{1,0:T(8,128)(2,1)S(1)} %collective-permute-done.24.refs_6_), channel_id=1, source_target_pairs={{0,1},{2,3},{5,4},{7,6},{8,9},{10,11},{13,12},{15,14},{16,17},{18,... | collective-permute-start | bytes 1572872 | tf_op jit(solution)/shard_map/ppermute | solution.py:256
  137.4 8.5 %collective-permute-start.22 = (bf16[256,1024]{1,0:T(8,128)(2,1)S(1)}, bf16[256,1024]{1,0:T(8,128)(2,1)S(1)}, u32[]{:S(2)}, u32[]{:S(2)}) collective-permute-start(bf16[256,1024]{1,0:T(8,128)(2,1)S(1)} %collective-permute-done.21.refs_2_), channel_id=1, source_target_pairs={{0,1},{1,0},{2,3},{3,2},{4,5},{5,4},{6,7},{7,6},{8,9},{9,8},{10,11... | collective-permute-start | bytes 1572872 | tf_op jit(solution)/shard_map/ppermute | solution.py:245
  140.9 12.5 %collective-permute-start.18 = (f32[256,512]{1,0:T(8,128)S(1)}, f32[256,512]{1,0:T(8,128)S(1)}, u32[]{:S(2)}, u32[]{:S(2)}) collective-permute-start(f32[256,512]{1,0:T(8,128)S(1)} %convert_add_fusion.refs_0_), channel_id=1, source_target_pairs={{0,4},{4,0},{8,12},{12,8},{16,20},{20,16},{24,28},{28,24},{1,5},{5... | collective-permute-start | bytes 1572872 | tf_op jit(solution)/shard_map/ppermute | solution.py:245
  142.7 12.2 %collective-permute-start.19 = (f32[256,512]{1,0:T(8,128)S(1)}, f32[256,512]{1,0:T(8,128)S(1)}, u32[]{:S(2)}, u32[]{:S(2)}) collective-permute-start(f32[256,512]{1,0:T(8,128)S(1)} %convert_add_fusion.refs_0_), channel_id=1, source_target_pairs={{0,2},{1,3},{2,0},{3,1},{4,6},{5,7},{6,4},{7,5},{8,10},{9,11},{10,... | collective-permute-start | bytes 1572872 | tf_op jit(solution)/shard_map/ppermute | solution.py:245
  143.8 14.3 %collective-permute-start.15 = (bf16[3,256,256]{2,1,0:T(8,128)(2,1)S(1)}, bf16[3,256,256]{2,1,0:T(8,128)(2,1)}, u32[]{:S(2)}, u32[]{:S(2)}) collective-permute-start(bf16[3,256,256]{2,1,0:T(8,128)(2,1)S(1)} %copy-done.31), channel_id=1, source_target_pairs={{0,8},{4,12},{8,0},{12,4},{16,24},{20,28},{24,16},{28,20},{1,9},{5... | collective-permute-start | bytes 1179656 | tf_op jit(solution)/shard_map/ppermute | solution.py:245
  155.6 6.6 %collective-permute-start.32 = (f32[128,512]{1,0:T(8,128)}, f32[128,512]{1,0:T(8,128)S(1)}, u32[]{:S(2)}, u32[]{:S(2)}) collective-permute-start(f32[128,512]{1,0:T(8,128)} %slice.33), channel_id=1, source_target_pairs={{0,4},{4,0},{8,12},{12,8},{16,20},{20,16},{24,28},{28,24},{1,5},{5... | collective-permute-start | bytes 786440 | tf_op jit(solution)/shard_map/ppermute | solution.py:245
  156.7 6.7 %collective-permute-start.33 = (f32[128,512]{1,0:T(8,128)}, f32[128,512]{1,0:T(8,128)}, u32[]{:S(2)}, u32[]{:S(2)}) collective-permute-start(f32[128,512]{1,0:T(8,128)} %slice.34), channel_id=1, source_target_pairs={{0,2},{1,3},{2,0},{3,1},{4,6},{5,7},{6,4},{7,5},{8,10},{9,11},{10,... | collective-permute-start | bytes 786440 | tf_op jit(solution)/shard_map/ppermute | solution.py:245
  157.6 7.2 %collective-permute-start.29 = (f32[256,512]{1,0:T(8,128)S(1)}, f32[256,512]{1,0:T(8,128)S(1)}, u32[]{:S(2)}, u32[]{:S(2)}) collective-permute-start(f32[256,512]{1,0:T(8,128)S(1)} %convert_add_fusion.refs_0_), channel_id=1, source_target_pairs={{0,1},{1,0},{2,3},{3,2},{4,5},{5,4},{6,7},{7,6},{8,9},{9,8},{10,11... | collective-permute-start | bytes 1572872 | tf_op jit(solution)/shard_map/ppermute | solution.py:245
  157.6 9.0 %collective-permute-start.30 = (f32[256,512]{1,0:T(8,128)S(1)}, f32[256,512]{1,0:T(8,128)S(1)}, u32[]{:S(2)}, u32[]{:S(2)}) collective-permute-start(f32[256,512]{1,0:T(8,128)S(1)} %collective-permute-done.19.refs_2_), channel_id=1, source_target_pairs={{0,1},{1,0},{2,3},{3,2},{4,5},{5,4},{6,7},{7,6},{8,9},{9,8},{10,11... | collective-permute-start | bytes 1572872 | tf_op jit(solution)/shard_map/ppermute | solution.py:245
  158.1 10.0 %collective-permute-start.31 = (f32[256,512]{1,0:T(8,128)S(1)}, f32[256,512]{1,0:T(8,128)S(1)}, u32[]{:S(2)}, u32[]{:S(2)}) collective-permute-start(f32[256,512]{1,0:T(8,128)S(1)} %collective-permute-done.18.refs_4_), channel_id=1, source_target_pairs={{0,1},{1,0},{2,3},{3,2},{4,5},{5,4},{6,7},{7,6},{8,9},{9,8},{10,11... | collective-permute-start | bytes 1572872 | tf_op jit(solution)/shard_map/ppermute | solution.py:245
  162.2 6.2 %collective-permute-start.34 = (f32[128,512]{1,0:T(8,128)S(1)}, f32[128,512]{1,0:T(8,128)S(1)}, u32[]{:S(2)}, u32[]{:S(2)}) collective-permute-start(f32[128,512]{1,0:T(8,128)S(1)} %collective-permute-done.32.refs_6_), channel_id=1, source_target_pairs={{0,1},{1,0},{2,3},{3,2},{4,5},{5,4},{6,7},{7,6},{8,9},{9,8},{10,11... | collective-permute-start | bytes 786440 | tf_op jit(solution)/shard_map/ppermute | solution.py:245
  163.4 6.6 %collective-permute-start.35 = (f32[128,512]{1,0:T(8,128)}, f32[128,512]{1,0:T(8,128)S(1)}, u32[]{:S(2)}, u32[]{:S(2)}) collective-permute-start(f32[128,512]{1,0:T(8,128)} %collective-permute-done.33.refs_7_), channel_id=1, source_target_pairs={{0,1},{1,0},{2,3},{3,2},{4,5},{5,4},{6,7},{7,6},{8,9},{9,8},{10,11... | collective-permute-start | bytes 786440 | tf_op jit(solution)/shard_map/ppermute | solution.py:245
  164.8 40.0 %collective-permute-start.26 = (f32[768,256]{1,0:T(8,128)S(1)}, f32[768,256]{1,0:T(8,128)S(1)}, u32[]{:S(2)}, u32[]{:S(2)}) collective-permute-start(f32[768,256]{1,0:T(8,128)S(1)} %bitcast.20), channel_id=1, source_target_pairs={{0,4},{4,0},{8,12},{12,8},{16,20},{20,16},{24,28},{28,24},{1,5},{5... | collective-permute-start | bytes 2359304 | tf_op jit(solution)/shard_map/ppermute | solution.py:245
  166.6 38.3 %collective-permute-start.27 = (f32[768,256]{1,0:T(8,128)S(1)}, f32[768,256]{1,0:T(8,128)S(1)}, u32[]{:S(2)}, u32[]{:S(2)}) collective-permute-start(f32[768,256]{1,0:T(8,128)S(1)} %bitcast.21), channel_id=1, source_target_pairs={{0,8},{4,12},{8,0},{12,4},{16,24},{20,28},{24,16},{28,20},{1,9},{5... | collective-permute-start | bytes 2359304 | tf_op jit(solution)/shard_map/ppermute | solution.py:245
  168.2 36.7 %collective-permute-start.28 = (f32[768,256]{1,0:T(8,128)S(1)}, f32[768,256]{1,0:T(8,128)S(1)}, u32[]{:S(2)}, u32[]{:S(2)}) collective-permute-start(f32[768,256]{1,0:T(8,128)S(1)} %bitcast.22), channel_id=1, source_target_pairs={{0,12},{4,8},{8,4},{12,0},{16,28},{20,24},{24,20},{28,16},{1,13},{... | collective-permute-start | bytes 2359304 | tf_op jit(solution)/shard_map/ppermute | solution.py:245
  168.4 66.3 %collective-permute-start.37 = (bf16[3,256,768]{2,1,0:T(8,128)(2,1)}, bf16[3,256,768]{2,1,0:T(8,128)(2,1)}, u32[]{:S(2)}, u32[]{:S(2)}) collective-permute-start(bf16[3,256,768]{2,1,0:T(8,128)(2,1)} %update_trailing.2), channel_id=1, source_target_pairs={{0,8},{4,12},{8,0},{12,4},{16,24},{20,28},{24,16},{28,20},{1,9},{5... | collective-permute-start | bytes 3538952 | tf_op jit(solution)/shard_map/ppermute | solution.py:245
  170.0 57.0 %collective-permute-start.36 = (bf16[3,256,768]{2,1,0:T(8,128)(2,1)S(1)}, bf16[3,256,768]{2,1,0:T(8,128)(2,1)S(1)}, u32[]{:S(2)}, u32[]{:S(2)}) collective-permute-start(bf16[3,256,768]{2,1,0:T(8,128)(2,1)S(1)} %copy-done.19), channel_id=1, source_target_pairs={{0,4},{4,0},{8,12},{12,8},{16,20},{20,16},{24,28},{28,24},{1,5},{5... | collective-permute-start | bytes 3538952 | tf_op jit(solution)/shard_map/ppermute | solution.py:245
  213.7 21.0 %collective-permute-start.39 = (bf16[256,1024]{1,0:T(8,128)(2,1)S(1)}, bf16[256,1024]{1,0:T(8,128)(2,1)S(1)}, u32[]{:S(2)}, u32[]{:S(2)}) collective-permute-start(bf16[256,1024]{1,0:T(8,128)(2,1)S(1)} %get-tuple-element.79.refs_0_), channel_id=1, source_target_pairs={{0,2},{1,3},{2,0},{3,1},{4,6},{5,7},{6,4},{7,5},{8,10},{9,11},{10,... | collective-permute-start | bytes 1572872 | tf_op jit(solution)/shard_map/ppermute | solution.py:245
  215.2 19.6 %collective-permute-start.38 = (bf16[256,1024]{1,0:T(8,128)(2,1)S(1)}, bf16[256,1024]{1,0:T(8,128)(2,1)S(1)}, u32[]{:S(2)}, u32[]{:S(2)}) collective-permute-start(bf16[256,1024]{1,0:T(8,128)(2,1)S(1)} %get-tuple-element.79.refs_0_), channel_id=1, source_target_pairs={{0,1},{1,0},{2,3},{3,2},{4,5},{5,4},{6,7},{7,6},{8,9},{9,8},{10,11... | collective-permute-start | bytes 1572872 | tf_op jit(solution)/shard_map/ppermute | solution.py:245
  234.7 2.0 collective-permute-start.40
  (25 other events, 182.8 us)

commit v3 on v2

--- a/solution.py
+++ b/solution.py
@@ -167,12 +167,9 @@
                     work[rows, columns] = ref[:, position * TILE : (position + 1) * TILE]
 
 
-def cholesky_kernel(fill, ids_ref, *refs):
-    packs = refs[:10]
-    lower_ref, inverse_ref, work, done, block_inverse, entries, rows = refs[10:]
+def eliminate(work, lower_ref, inverse_ref, done, block_inverse, entries, rows):
     order = work.shape[0]
-    blocks = order // BLK
-    fill(ids_ref, packs, work)
+    blocks = lower_ref.shape[1] // BLK
     lower_ref[...] = jnp.zeros_like(lower_ref)
     row_id = lax.broadcasted_iota(jnp.int32, (BLK, BLK), 0)
     lane_id = lax.broadcasted_iota(jnp.int32, (BLK, BLK), 1)
@@ -184,8 +181,10 @@
         upper = jnp.where(lane_id >= row_id, done[:, 0:BLK], 0.0)
         lower_ref[span, span] = upper.T
         block_inverse[k] = done[:, BLK:]
-        for fixed in range(blocks - 1):
+        for fixed in range(blocks):
             after = (fixed + 1) * BLK
+            if after == order:
+                continue
 
             @pl.when(k == fixed)
             def _():
@@ -206,7 +205,7 @@
         return carry
 
     lax.fori_loop(0, blocks, step, 0)
-    for tile in range(order // TILE):
+    for tile in range(blocks * BLK // TILE):
         base = tile * TILE
         first, second = block_inverse[2 * tile], block_inverse[2 * tile + 1]
         corner = lower_ref[base + BLK : base + TILE, base : base + BLK]
@@ -218,26 +217,63 @@
         inverse_ref[tile, BLK:, BLK:] = second
 
 
-def cholesky(ids, packs, fill, order):
+def cholesky_first_kernel(fill, ids_ref, *refs):
+    packs = refs[:10]
+    lower_ref, inverse_ref, rest_ref, work, *scratch = refs[10:]
+    fill(ids_ref, packs, work)
+    eliminate(work, lower_ref, inverse_ref, *scratch)
+    done = lower_ref.shape[1]
+    rest_ref[...] = work[done:, done:]
+
+
+def cholesky_second_kernel(rest_ref, lower_ref, inverse_ref, work, *scratch):
+    work[...] = rest_ref[...]
+    eliminate(work, lower_ref, inverse_ref, *scratch)
+
+
+def elimination_scratch(order, blocks):
+    return [
+        pltpu.VMEM((order, order), jnp.float32),
+        pltpu.VMEM((BLK, 2 * BLK), jnp.float32),
+        pltpu.VMEM((blocks, BLK, BLK), jnp.float32),
+        pltpu.VMEM((2, GRP, GRP, BLK), jnp.float32),
+        pltpu.VMEM((2, GRP, 2 * BLK), jnp.float32),
+    ]
+
+
+def cholesky_first(ids, packs, fill, order):
+    done = order // 2
     return pl.pallas_call(
-        functools.partial(cholesky_kernel, fill),
+        functools.partial(cholesky_first_kernel, fill),
+        out_shape=(
+            jax.ShapeDtypeStruct((order, done), jnp.float32),
+            jax.ShapeDtypeStruct((done // TILE, TILE, TILE), jnp.float32),
+            jax.ShapeDtypeStruct((order - done, order - done), jnp.float32),
+        ),
+        in_specs=[SMEM] + [VMEM] * len(packs),
+        out_specs=(VMEM,) * 3,
+        scratch_shapes=elimination_scratch(order, done // BLK),
+        compiler_params=pltpu.CompilerParams(vmem_limit_bytes=32 * 2**20),
+        cost_estimate=pl.CostEstimate(flops=2 * 10**10, bytes_accessed=5 * 10**7, transcendentals=0),
+        name="cholesky_first",
+    )(ids, *packs)
+
+
+def cholesky_second(rest):
+    order = rest.shape[0]
+    return pl.pallas_call(
+        cholesky_second_kernel,
         out_shape=(
             jax.ShapeDtypeStruct((order, order), jnp.float32),
             jax.ShapeDtypeStruct((order // TILE, TILE, TILE), jnp.float32),
         ),
-        in_specs=[SMEM] + [VMEM] * len(packs),
-        out_specs=(VMEM, VMEM),
-        scratch_shapes=[
-            pltpu.VMEM((order, order), jnp.float32),
-            pltpu.VMEM((BLK, 2 * BLK), jnp.float32),
-            pltpu.VMEM((order // BLK, BLK, BLK), jnp.float32),
-            pltpu.VMEM((2, GRP, GRP, BLK), jnp.float32),
-            pltpu.VMEM((2, GRP, 2 * BLK), jnp.float32),
-        ],
-        compiler_params=pltpu.CompilerParams(vmem_limit_bytes=32 * 2**20),
-        cost_estimate=pl.CostEstimate(flops=4 * 10**10, bytes_accessed=10**8, transcendentals=0),
-        name="cholesky",
-    )(ids, *packs)
+        in_specs=[VMEM],
+        out_specs=(VMEM,) * 2,
+        scratch_shapes=elimination_scratch(order, order // BLK),
+        compiler_params=pltpu.CompilerParams(vmem_limit_bytes=24 * 2**20),
+        cost_estimate=pl.CostEstimate(flops=2 * 10**10, bytes_accessed=5 * 10**7, transcendentals=0),
+        name="cholesky_second",
+    )(rest)
 
 
 def swapped(value, axis, mask):
@@ -296,17 +332,17 @@
     return wait
 
 
-def move_separator(leaf, column, map_ref, child_ref, slots, target_of, sems):
+def move_separator(leaf, column, map_ref, child_ref, slots, groups, target_of, sems):
     count = child_ref.shape[0]
     waits = []
     for slot in slots:
         row = find_tile(map_ref, leaf, column, slot, count)
-        for group in range(GROUPS):
+        for position, group in enumerate(groups):
             place = find_tile(map_ref, leaf, group, 0, count)
             live = jnp.logical_and(row >= 0, place >= 0)
             span = pl.ds(pl.multiple_of((jnp.maximum(place, 0) * GROUPS + group) * TILE, TILE), TILE)
             source = child_ref.at[jnp.maximum(row, 0), :, span]
-            target = target_of(slot).at[:, pl.ds(group * TILE, TILE)]
+            target = target_of(slot, position)
             waits.append(move_tile(live, source, target, sems.at[len(waits)]))
     return waits
 
@@ -315,7 +351,10 @@
     width = GROUPS * TILE
     entries = pltpu.make_async_copy(entries_ref.at[0], pivot_ref.at[:, pl.ds(width, width // 2)], entry_sem.at[0])
     entries.start()
-    waits = move_separator(ids_ref[0], ids_ref[1], map_ref, child_ref, (0,), lambda slot: pivot_ref, sems)
+    waits = move_separator(
+        ids_ref[0], ids_ref[1], map_ref, child_ref, (0,), range(GROUPS),
+        lambda slot, position: pivot_ref.at[:, pl.ds(position * TILE, TILE)], sems,
+    )
     for wait in waits:
         wait()
     entries.wait()
@@ -334,19 +373,17 @@
     )(ids, child_map, child, entries)
 
 
-def pick_rest_kernel(ids_ref, map_ref, next_ref, child_ref, entries_ref, coupling_ref, *refs):
-    outs, (first_sems, sems, entry_sem) = refs[:6], refs[6:]
+def pick_rest_kernel(ids_ref, map_ref, next_ref, child_ref, *refs):
+    halves_out, outs, (first_sems, sems) = refs[:2], refs[2:8], refs[8:]
     count = child_ref.shape[0]
-    width = GROUPS * TILE
     leaf, column = ids_ref[0], ids_ref[1]
-    pair = leaf >> 1
-    entries = pltpu.make_async_copy(
-        entries_ref.at[pl.ds(1, count)], coupling_ref.at[:, :, pl.ds(width, width // 2)], entry_sem.at[0]
-    )
-    entries.start()
+    half, pair = leaf & 1, leaf >> 1
     slots = range(1, count + 1)
+    groups = (2 * (1 - half), 2 * (1 - half) + 1, 2 * half, 2 * half + 1)
     waits = move_separator(
-        leaf, column, map_ref, child_ref, slots, lambda slot: coupling_ref.at[slot - 1], first_sems
+        leaf, column, map_ref, child_ref, slots, groups,
+        lambda slot, position: halves_out[position // 2].at[slot - 1, :, pl.ds(position % 2 * TILE, TILE)],
+        first_sems,
     )
     rows = [find_tile(map_ref, leaf, column, slot, count) for slot in slots]
     used = 0
@@ -368,81 +405,86 @@
                 used += 1
     for wait in waits:
         wait()
-    entries.wait()
-
-
-def pick_rest(ids, child_map, next_map, child, entries):
+
+
+def pick_rest(ids, child_map, next_map, child):
     count = child.shape[0]
-    wide = GROUPS * TILE + entries.shape[-1]
-    widths = (wide,) + (2 * TILE, 3 * TILE, 3 * TILE) * 2
+    widths = (2 * TILE, 2 * TILE) + (2 * TILE, 3 * TILE, 3 * TILE) * 2
     return pl.pallas_call(
         pick_rest_kernel,
         out_shape=tuple(jax.ShapeDtypeStruct((count, TILE, width), child.dtype) for width in widths),
-        in_specs=[SMEM, SMEM, SMEM, ANY, ANY],
-        out_specs=(VMEM,) * 7,
-        scratch_shapes=[
-            pltpu.SemaphoreType.DMA((GROUPS * count,)),
-            pltpu.SemaphoreType.DMA((16 * count,)),
-            pltpu.SemaphoreType.DMA((1,)),
-        ],
+        in_specs=[SMEM, SMEM, SMEM, ANY],
+        out_specs=(VMEM,) * 8,
+        scratch_shapes=[pltpu.SemaphoreType.DMA((GROUPS * count,)), pltpu.SemaphoreType.DMA((16 * count,))],
         compiler_params=pltpu.CompilerParams(vmem_limit_bytes=56 * 2**20),
         cost_estimate=pl.CostEstimate(flops=0, bytes_accessed=2 * 10**7, transcendentals=0),
         name="pick_rest",
-    )(ids, child_map, next_map, child, entries)
-
-
-def solve_blocks(coupling_ref, lower_ref, inverse_ref, panel_ref):
-    order = lower_ref.shape[0]
+    )(ids, child_map, next_map, child)
+
+
+def solve_blocks(coupling_ref, lowers, inverses, panel_ref):
+    split = lowers[0].shape[1]
     solved = []
-    for k in range(order // TILE):
+    for k in range(panel_ref.shape[1] // TILE):
         span = slice(k * TILE, (k + 1) * TILE)
         rest = coupling_ref[:, span]
         if k:
             left = jnp.concatenate([part[0] for part in solved], axis=1)
             low = jnp.concatenate([part[1] for part in solved], axis=1)
-            high_lower, low_lower = halves(lower_ref[span, 0 : k * TILE])
+            strip = lowers[0][span, 0 : min(k * TILE, split)]
+            if k * TILE > split:
+                inner = slice(k * TILE - split, (k + 1) * TILE - split)
+                strip = jnp.concatenate([strip, lowers[1][inner, 0 : k * TILE - split]], axis=1)
+            high_lower, low_lower = halves(strip)
             rest = rest - dot_lanes(
                 jnp.concatenate([left, low, left], axis=1),
                 jnp.concatenate([high_lower, high_lower, low_lower], axis=1),
             )
-        block = dot_lanes(left_parts(rest), right_lanes(inverse_ref[k]))
+        tiles = split // TILE
+        inverse = inverses[0][k] if k < tiles else inverses[1][k - tiles]
+        block = dot_lanes(left_parts(rest), right_lanes(inverse))
         panel_ref[:, span] = block
         solved.append(halves(block))
     return jnp.concatenate([part[0] for part in solved], axis=1)
 
 
-def write_factor(column, offset, lower_ref, panel, factor_ref):
+def write_factor(column, offset, lowers, panel, factor_ref):
     width = factor_ref.shape[-1]
-    rows = pl.ds(pl.multiple_of(column * TILE, TILE), TILE)
+    split = lowers[0].shape[1]
+    per = split // width
+    tiles = split // TILE
     span = pl.ds(pl.multiple_of(offset * width, width), width)
-    factor_ref[0] = lower_ref[rows, span]
+    factor_ref[0] = jnp.zeros(factor_ref.shape[1:], factor_ref.dtype)
+
+    @pl.when(offset < per)
+    def _():
+        inner = pl.ds(pl.multiple_of(jnp.minimum(offset, per - 1) * width, width), width)
+        factor_ref[0] = lowers[0][pl.ds(pl.multiple_of(column * TILE, TILE), TILE), inner]
+
+    @pl.when(jnp.logical_and(offset >= per, column >= tiles))
+    def _():
+        inner = pl.ds(pl.multiple_of(jnp.maximum(offset - per, 0) * width, width), width)
+        rows = pl.ds(pl.multiple_of(jnp.maximum(column - tiles, 0) * TILE, TILE), TILE)
+        factor_ref[0] = lowers[1][rows, inner]
+
     for s in range(factor_ref.shape[0] - 1):
         factor_ref[s + 1] = panel[s * TILE : (s + 1) * TILE, span]
 
 
-def panel_one_kernel(
-    ids_ref, mask_ref, next_ref, mine_ref, peer_ref, lower_ref, inverse_ref, factor_ref, round_ref, first_ref, second_ref, third_ref, coupling, panel
-):
+def panel_one_kernel(ids_ref, next_ref, mine_ref, peer_ref, *refs):
+    lowers, inverses = refs[:2], refs[2:4]
+    factor_ref, round_ref, first_ref, second_ref, third_ref, coupling, panel = refs[4:]
     leaf, column = ids_ref[0], ids_ref[1]
     half, pair = leaf & 1, leaf >> 1
-    count = mine_ref.shape[0]
-    order = lower_ref.shape[0]
-    for s in range(count):
-        for tile in range(order // TILE):
-            span = slice(tile * TILE, (tile + 1) * TILE)
-            where = order + (tile % 2) * TILE
-            weight = mask_ref[((pair * count + s) * GROUPS + column) * GROUPS + tile].astype(jnp.float32)
-            mine = mine_ref[s, :, where : where + TILE].astype(jnp.float32)
-            peer = peer_ref[s, :, where : where + TILE].astype(jnp.float32)
-            own_first = half == tile // 2
-            entry = jnp.where(own_first, mine, peer)
-            coupling[s * TILE : (s + 1) * TILE, span] = (
-                mine_ref[s, :, span].astype(jnp.float32) + peer_ref[s, :, span].astype(jnp.float32) + entry * weight
-            )
-    rounded = solve_blocks(coupling, lower_ref, inverse_ref, panel)
+    count, _, width = mine_ref.shape
+    for ref, place in ((mine_ref, half), (peer_ref, 1 - half)):
+        span = pl.ds(pl.multiple_of(place * width, width), width)
+        for s in range(count):
+            coupling[s * TILE : (s + 1) * TILE, span] = ref[s].astype(jnp.float32)
+    rounded = solve_blocks(coupling, lowers, inverses, panel)
     for s in range(count):
         round_ref[s] = rounded[s * TILE : (s + 1) * TILE]
-    write_factor(column, half, lower_ref, panel, factor_ref)
+    write_factor(column, half, lowers, panel, factor_ref)
     heavy = half == (column & 1)
     for a, share_ref in ((0, first_ref), (jnp.where(heavy, 1, 0), second_ref), (2, third_ref)):
         slot = jnp.int32(0)
@@ -453,9 +495,9 @@
         share_ref[...] = round_ref[jnp.maximum(tile, 0)]
 
 
-def panel_one(ids, mask, next_map, mine, peer, lower, inverse):
+def panel_one(ids, next_map, mine, peer, lowers, inverses):
     count = mine.shape[0]
-    order = lower.shape[0]
+    order = lowers[0].shape[0]
     return pl.pallas_call(
         panel_one_kernel,
         out_shape=(
@@ -463,7 +505,7 @@
             jax.ShapeDtypeStruct((count, TILE, order), jnp.bfloat16),
         )
         + (jax.ShapeDtypeStruct((TILE, order), jnp.bfloat16),) * 3,
-        in_specs=[SMEM, SMEM, SMEM, VMEM, VMEM, VMEM, VMEM],
+        in_specs=[SMEM, SMEM] + [VMEM] * 6,
         out_specs=(VMEM,) * 5,
         scratch_shapes=[
             pltpu.VMEM((count * TILE, order), jnp.float32),
@@ -472,10 +514,12 @@
         compiler_params=PARAMS,
         cost_estimate=pl.CostEstimate(flops=10**9, bytes_accessed=10**6, transcendentals=0),
         name="panel_one",
-    )(ids, mask, next_map, mine, peer, lower, inverse)
-
-
-def panel_two_kernel(ids_ref, own_ref, x_ref, z_ref, both_ref, lower_ref, inverse_ref, factor_ref, round_ref, share_ref, coupling, panel):
+    )(ids, next_map, mine, peer, *lowers, *inverses)
+
+
+def panel_two_kernel(ids_ref, own_ref, x_ref, z_ref, both_ref, *refs):
+    lowers, inverses = refs[:2], refs[2:4]
+    factor_ref, round_ref, share_ref, coupling, panel = refs[4:]
     leaf, column = ids_ref[0], ids_ref[1]
     half, side = leaf & 1, (leaf >> 1) & 1
     quarter = leaf & 3
@@ -486,11 +530,11 @@
         (2 * (1 - side) + half, z_ref),
         (2 * (1 - side) + 1 - half, both_ref),
     ):
-        coupling[:, pl.ds(pl.multiple_of(place * TILE, TILE), TILE)] = ref[...]
-    rounded = solve_blocks(coupling, lower_ref, inverse_ref, panel)
+        coupling[:, pl.ds(pl.multiple_of(place * TILE, TILE), TILE)] = ref[...].astype(jnp.float32)
+    rounded = solve_blocks(coupling, lowers, inverses, panel)
     for s in range(count):
         round_ref[s] = rounded[s * TILE : (s + 1) * TILE]
-    write_factor(column, quarter, lower_ref, panel, factor_ref)
+    write_factor(column, quarter, lowers, panel, factor_ref)
     chosen = jnp.int32(0)
     for i in range(3):
         tile = 3 * quarter + i
@@ -498,10 +542,10 @@
     share_ref[...] = round_ref[chosen]
 
 
-def panel_two(ids, parts, lower, inverse):
+def panel_two(ids, parts, lowers, inverses):
     rows = parts[0].shape[0]
     count = rows // TILE
-    order = lower.shape[0]
+    order = lowers[0].shape[0]
     return pl.pallas_call(
         panel_two_kernel,
         out_shape=(
@@ -509,13 +553,13 @@
             jax.ShapeDtypeStruct((count, TILE, order), jnp.bfloat16),
             jax.ShapeDtypeStruct((TILE, order), jnp.bfloat16),
         ),
-        in_specs=[SMEM] + [VMEM] * 6,
+        in_specs=[SMEM] + [VMEM] * 8,
         out_specs=(VMEM, VMEM, VMEM),
         scratch_shapes=[pltpu.VMEM((rows, order), jnp.float32), pltpu.VMEM((rows, order), jnp.float32)],
         compiler_params=PARAMS,
         cost_estimate=pl.CostEstimate(flops=10**9, bytes_accessed=10**6, transcendentals=0),
         name="panel_two",
-    )(ids, *parts, lower, inverse)
+    )(ids, *parts, *lowers, *inverses)
 
 
 def take_tile(owner, column, refs, live, target, sem):
@@ -678,6 +722,11 @@
     return lax.optimization_barrier((value, *earlier))[0]
 
 
+def own_mask(mask, front, column, count):
+    rows = lax.dynamic_index_in_dim(mask, front, 0, keepdims=False).reshape(count, GROUPS, -1)
+    return lax.dynamic_index_in_dim(rows, column, 1, keepdims=False).astype(jnp.float32)
+
+
 def body(child_update, sep_one, sep_two, map_one, map_two, mask_one, mask_two):
     column = lax.axis_index("front")
     leaf = lax.axis_index("leaf")
@@ -692,18 +741,28 @@
     maps_two = map_two[:, 0]
 
     pivot_mine = pick_pivot(ids, maps_one, child, entries_one)
-    coupling_mine, sep_send, near_send, far_send, sep_keep, near_keep, far_keep = pick_rest(
-        ids, maps_one, maps_two, child, entries_one
+    coupling_send, coupling_keep, sep_send, near_send, far_send, sep_keep, near_keep, far_keep = pick_rest(
+        ids, maps_one, maps_two, child
     )
-    packs = over_square(pivot_mine, coupling_mine)
-    coupling_peer = swapped(after(coupling_mine, packs[4]), "leaf", 1)
-    sep_peer = swapped(after(sep_send, packs[6]), "leaf", 1)
-    far_peer = swapped(after(far_send, packs[6]), "leaf", 1)
+    packs = over_square(pivot_mine, coupling_send)
+    coupling_got = swapped(after(coupling_send, packs[4]), "leaf", 1)
     entries_far = swapped(entries_two[0], "leaf", 2)
-
-    lower, inverse = cholesky(ids, packs, fill_one, order)
+    mask_first = own_mask(mask_one, leaf >> 1, column, count)
+    mask_first = lax.dynamic_slice_in_dim(mask_first, 2 * (leaf & 1), 2, 1)
+    mask_first = jnp.repeat(mask_first, TILE, axis=1)[:, None, :]
+
+    lower, inverse, rest = cholesky_first(ids, packs, fill_one, order)
+    coupling = (
+        coupling_keep.astype(jnp.float32)
+        + after(coupling_got, rest).astype(jnp.float32)
+        + entries_one[1:].astype(jnp.float32) * mask_first
+    )
+    coupling_peer = swapped(coupling.astype(jnp.bfloat16), "leaf", 1)
+    lower_rest, inverse_rest = cholesky_second(rest)
+    sep_peer = swapped(after(sep_send, lower_rest), "leaf", 1)
+    far_peer = swapped(after(far_send, lower_rest), "leaf", 1)
     factor_one, rounded, first, second, third = panel_one(
-        ids, mask_one.reshape(-1), maps_two, coupling_mine, coupling_peer, lower, inverse
+        ids, maps_two, coupling, coupling_peer, (lower, lower_rest), (inverse, inverse_rest)
     )
     first_y = swapped_heavy(first, 2)
     firsts = over_heavy(first, first_y, sep_peer)
@@ -723,21 +782,20 @@
     )
     packs = over_square(after(pivot_tile, far_peer), far_trailing)
     coupling_far = swapped(after(far_coupling, pivot_far), "leaf", 2)
-    mask_second = lax.dynamic_index_in_dim(mask_two, quad, 0, keepdims=False).reshape(count, GROUPS, -1)
-    mask_second = lax.dynamic_index_in_dim(mask_second, column, 1, keepdims=False)
-    mask_second = lax.dynamic_index_in_dim(mask_second, quarter, 1, keepdims=False)
+    mask_second = lax.dynamic_index_in_dim(own_mask(mask_two, quad, column, count), quarter, 1, keepdims=False)
     coupling = (
         near_coupling.astype(jnp.float32)
         + coupling_far.astype(jnp.float32)
-        + entries_two[1:].astype(jnp.float32) * mask_second.astype(jnp.float32)[:, None, None]
+        + entries_two[1:].astype(jnp.float32) * mask_second[:, None, None]
     ).reshape(count * TILE, TILE)
-    coupling = after(coupling, packs[4])
-    coupling_x, coupling_z, coupling_xz = (swapped(coupling, "leaf", mask) for mask in (1, 2, 3))
+    coupling_sent = after(coupling.astype(jnp.bfloat16), packs[4])
+    coupling_x, coupling_z, coupling_xz = (swapped(coupling_sent, "leaf", mask) for mask in (1, 2, 3))
     trailing_far = swapped(after(far_trailing, packs[4]), "leaf", 2)
     near_peer = swapped(after(near_send, packs[6]), "leaf", 1)
-    lower, inverse = cholesky(ids, packs, fill_two, order)
+    lower, inverse, rest = cholesky_first(ids, packs, fill_two, order)
+    lower_rest, inverse_rest = cholesky_second(rest)
     factor_two, rounded_two, share = panel_two(
-        ids, (coupling, coupling_x, coupling_z, coupling_xz), lower, inverse
+        ids, (coupling, coupling_x, coupling_z, coupling_xz), (lower, lower_rest), (inverse, inverse_rest)
     )
     near_trailing = update_trailing(ids, maps_two, near_keep, near_peer, rounded, seconds, thirds, (1, 2, 3))
     shares = over_front(share, swapped(share, "front", 2), near_trailing, trailing_far)

time: 245 us -> 226 us (0.922); the launches traced: 244 us -> 222 us
  waiting for transfers between devices: 69 us -> 50.5 us
  starting transfers between devices: 39.7 us -> 37.2 us
    ppermute x35 -> x36, waiting for transfers between devices: 64.5 us -> 45.8 us  [swapped(): return lax.ppermute(value, axis, pairs)]
    ppermute x35 -> x36, starting transfers between devices: 27.6 us -> 27 us  [swapped(): return lax.ppermute(value, axis, pairs)]
    unnamed x65 -> x74, local copies, waits for them, and re-layouts: 6.29 us -> 6.13 us
    pallas_call x2 -> x4, Pallas kernels: 67.9 us -> 68 us  [the longest x2 37.7 us: cholesky_first(): pl.pallas_call(functools.partial(cholesky_first_kernel, fill), out_shape=...]
  transfers between devices with their start and end apart: 41 -> 42, of which waited for: 15 -> 17; matrix products, arithmetic and copies ran while one was open for 2% -> 2% of each run, Pallas kernels for 45% -> 49%
where the time goes in v3:
time: 226 us; the launch traced here: 222 us
  Pallas kernels  119 us (53%)
  waiting for transfers between devices  50.5 us (22%)
  starting transfers between devices  37.2 us (16%)
  local copies, waits for them, and re-layouts  11.6 us (5%)
  other arithmetic  2.59 us (1%)
    ppermute x36, waiting for transfers between devices, swapped(): return lax.ppermute(value, axis, pairs)  45.8 us
    pallas_call x2, Pallas kernels, cholesky_first(): pl.pallas_call(functools.partial(cholesky_first_kernel, fill), out_shape=...  37.7 us
    pallas_call x2, Pallas kernels, cholesky_second(): pl.pallas_call(cholesky_second_kernel, out_shape=(jax.ShapeDtypeStruct((o...  30.3 us
    ppermute x36, starting transfers between devices, swapped(): return lax.ppermute(value, axis, pairs)  27 us
    pallas_call x2, Pallas kernels, update_trailing(): pl.pallas_call(functools.partial(update_trailing_kernel, positions), out_...  13.2 us
    ppermute x6, starting transfers between devices, swapped_heavy(): return lax.ppermute(value, ('leaf', 'front'), pairs)  10.1 us
    pallas_call x1, Pallas kernels, panel_one(): pl.pallas_call(panel_one_kernel, out_shape=(jax.ShapeDtypeStruct((count +...  8.18 us
    pallas_call x1, Pallas kernels, panel_two(): pl.pallas_call(panel_two_kernel, out_shape=(jax.ShapeDtypeStruct((count +...  7.56 us
  transfers between devices with their start and end apart: 42, of which 17 were waited for; matrix products, arithmetic and copies ran while one was open for 2% of the time, Pallas kernels for 49%

profile of v3, /device:TPU:0, one launch (start us, length us, event | category | flops | bytes accessed | tf_op | source)
XLA Modules:
  0.0 222.3 jit_solution(10833431093632526310)
XLA Ops:
  0.7 1.4 copy.20.map_ref
  2.7 3.1 %pick_pivot.1.refs_0_ = bf16[256,1536]{1,0:T(8,128)(2,1)} custom-call(s32[2]{0:T(128)} %pad_add_fusion.ids_ref, s32[8,4,3]{2,1,0:T(4,128)} %copy.20.map_ref, bf16[3,256,3072]{2,1,0:T(8,128)(2,1)} %bitcast.35, bf16[4,256,512]{2,1,0:T(8,128)(2,1)} %bitcast.37), custom_call_target="tpu_custom_call" | custom-call | tf_op jit(solution)/shard_map/pick_pivot/pallas_call | solution.py:365
  5.8 3.0 %collective-permute-start = (bf16[256,1536]{1,0:T(8,128)(2,1)}, bf16[256,1536]{1,0:T(8,128)(2,1)S(1)}, u32[]{:S(2)}, u32[]{:S(2)}) collective-permute-start(bf16[256,1536]{1,0:T(8,128)(2,1)} %pick_pivot.1.refs_0_), channel_id=1, source_target_pairs={{0,4},{4,0},{8,12},{12,8},{16,20},{20,16},{24,28},{28,24},{1,5},{5... | collective-permute-start | bytes 2359304 | tf_op jit(solution)/shard_map/ppermute | solution.py:281
  8.9 1.5 collective-permute-start.1
  11.1 7.0 %pick_rest.1 = (bf16[3,256,512]{2,1,0:T(8,128)(2,1)}, bf16[3,256,512]{2,1,0:T(8,128)(2,1)}, bf16[3,256,512]{2,1,0:T(8,128)(2,1)}, bf16[3,256,768]{2,1,0:T(8,128)...) custom-call(s32[2]{0:T(128)} %pad_add_fusion.ids_ref, ...), custom_call_target="tpu_custom_call" | custom-call | bytes 20000000 | tf_op jit(solution)/shard_map/pick_rest/pallas_call | solution.py:413
  18.1 8.5 %collective-permute-done.refs_4_ = bf16[256,1536]{1,0:T(8,128)(2,1)S(1)} collective-permute-done((bf16[256,1536]{1,0:T(8,128)(2,1)}, bf16[256,1536]{1,0:T(8,128)(2,1)S(1)}, u32[]{:S(2)}, u32[]{:S(2)}) %collective-permute-start) | collective-permute-done | bytes 786464 | tf_op jit(solution)/shard_map/ppermute | solution.py:281
  26.6 1.5 collective-permute-done.1.refs_2_
  28.9 1.5 collective-permute-start.7
  32.3 6.5 %collective-permute-done.7.refs_7_ = bf16[128,1536]{1,0:T(8,128)(2,1)S(1)} collective-permute-done((bf16[128,1536]{1,0:T(8,128)(2,1)}, bf16[128,1536]{1,0:T(8,128)(2,1)S(1)}, u32[]{:S(2)}, u32[]{:S(2)}) %collective-permute-start.7) | collective-permute-done | bytes 393248 | tf_op jit(solution)/shard_map/ppermute | solution.py:281
  38.8 2.2 collective-permute-done.6.refs_6_
  43.0 20.0 %cholesky_first.2 = (f32[1024,512]{1,0:T(8,128)S(1)}, f32[2,256,256]{2,1,0:T(8,128)S(1)}, f32[512,512]{1,0:T(8,128)S(1)}) custom-call(s32[2]{0:T(128)S(1)} %copy-done.6, bf16[256,1536]{1,0:T(8,128)(2,1)S(1)} %copy-done.3, bf16[256,1536]{1,0:T(8,128)(2,1)S(1)} %collective-permute-done.3.refs_1_, bf16[256,1536]{1,0:T(8,128)(2,1)S(1)} %collective-permute-done.1.refs_2_, ...), custom_call_target="tpu_custom_call" | custom-call | flops 20000000000 | bytes 50000000 | tf_op jit(solution)/shard_map/cholesky_first/pallas_call | solution.py:246
  64.1 15.1 %cholesky_second.2 = (f32[512,512]{1,0:T(8,128)S(1)}, f32[2,256,256]{2,1,0:T(8,128)S(1)}) custom-call(f32[512,512]{1,0:T(8,128)S(1)} %get-tuple-element.55.rest_ref), custom_call_target="tpu_custom_call" | custom-call | flops 20000000000 | bytes 50000000 | tf_op jit(solution)/shard_map/cholesky_second/pallas_call | solution.py:264
  79.3 1.5 collective-permute-start.11
  80.7 3.2 %collective-permute-done.10.peer_ref = bf16[3,256,512]{2,1,0:T(8,128)(2,1)S(1)} collective-permute-done((bf16[3,256,512]{2,1,0:T(8,128)(2,1)S(1)}, bf16[3,256,512]{2,1,0:T(8,128)(2,1)S(1)}, u32[]{:S(2)}, u32[]{:S(2)}) %collective-permute-start.10) | collective-permute-done | bytes 786464 | tf_op jit(solution)/shard_map/ppermute | solution.py:281
  83.9 8.2 %panel_one.1 = (f32[4,256,512]{2,1,0:T(8,128)}, bf16[3,256,1024]{2,1,0:T(8,128)(2,1)S(1)}, bf16[256,1024]{1,0:T(8,128)(2,1)S(1)}, bf16[256,1024]{1,0:T(8,128)(2,1)S(1)}, bf16[256,1024]{1,0:T(8,128)(2,1)S(1)}) custom-call(s32[2]{0:T(128)S(1)} %copy-done.6, s32[4,4,3]{2,1,0:T(4,128)S(1)} %bitcast.34, f32[3,256,512]{2,1,0:T(8,128)S(1)} %get-tuple-element.98.mine_ref, ...), custom_call_target="tpu_custom_call" | custom-call | flops 1000000000 | bytes 1000000 | tf_op jit(solution)/shard_map/panel_one/pallas_call | solution.py:501
  92.1 1.1 copy-done.2
  93.2 2.4 %collective-permute-start.13 = (bf16[256,1024]{1,0:T(8,128)(2,1)S(1)}, bf16[256,1024]{1,0:T(8,128)(2,1)S(1)}, u32[]{:S(2)}, u32[]{:S(2)}) collective-permute-start(bf16[256,1024]{1,0:T(8,128)(2,1)S(1)} %get-tuple-element.66.refs_0_), channel_id=1, source_target_pairs={{0,2},{2,0},{5,7},{7,5},{8,10},{10,8},{13,15},{15,13},{16,18},{18,... | collective-permute-start | bytes 1572872 | tf_op jit(solution)/shard_map/ppermute | solution.py:292
  95.7 1.3 collective-permute-start.12
  97.0 3.0 %collective-permute-done.11.peer_ref = bf16[3,256,512]{2,1,0:T(8,128)(2,1)S(1)} collective-permute-done((bf16[3,256,512]{2,1,0:T(8,128)(2,1)S(1)}, bf16[3,256,512]{2,1,0:T(8,128)(2,1)S(1)}, u32[]{:S(2)}, u32[]{:S(2)}) %collective-permute-start.11) | collective-permute-done | bytes 786464 | tf_op jit(solution)/shard_map/ppermute | solution.py:281
  100.0 4.3 %collective-permute-done.13.refs_2_ = bf16[256,1024]{1,0:T(8,128)(2,1)S(1)} collective-permute-done((bf16[256,1024]{1,0:T(8,128)(2,1)S(1)}, bf16[256,1024]{1,0:T(8,128)(2,1)S(1)}, u32[]{:S(2)}, u32[]{:S(2)}) %collective-permute-start.13) | collective-permute-done | bytes 524320 | tf_op jit(solution)/shard_map/ppermute | solution.py:292
  104.3 1.3 collective-permute-start.14
  105.7 2.4 %collective-permute-start.25 = (bf16[256,1024]{1,0:T(8,128)(2,1)S(1)}, bf16[256,1024]{1,0:T(8,128)(2,1)}, u32[]{:S(2)}, u32[]{:S(2)}) collective-permute-start(bf16[256,1024]{1,0:T(8,128)(2,1)S(1)} %get-tuple-element.80.refs_4_), channel_id=1, source_target_pairs={{0,2},{2,0},{5,7},{7,5},{8,10},{10,8},{13,15},{15,13},{16,18},{18,... | collective-permute-start | bytes 1572872 | tf_op jit(solution)/shard_map/ppermute | solution.py:292
  108.1 1.6 collective-permute-start.22
  110.7 5.5 %update_separator.1 = (bf16[256,512]{1,0:T(8,128)(2,1)}, bf16[3,256,256]{2,1,0:T(8,128)(2,1)}, bf16[3,256,256]{2,1,0:T(8,128)(2,1)}) custom-call(s32[2]{0:T(128)} %pad_add_fusion.ids_ref, s32[4,4,3]{2,1,0:T(4,128)} %bitcast.31, bf16[3,256,512]{2,1,0:T(8,128)(2,1)} %get-tuple-element.62.keep_ref, bf16[3,256,512]{2,1,0:T(8,128)(2,1)} %copy-done.14, ...), custom_call_target="tpu_custom_call" | custom-call | flops 100000000 | bytes 100000 | tf_op jit(solution)/shard_map/update_separator/pallas_call | solution.py:627
  116.2 1.6 collective-permute-start.15
  118.8 5.6 %collective-permute-done.22.refs_2_ = bf16[256,1024]{1,0:T(8,128)(2,1)} collective-permute-done((bf16[256,1024]{1,0:T(8,128)(2,1)S(1)}, bf16[256,1024]{1,0:T(8,128)(2,1)}, u32[]{:S(2)}, u32[]{:S(2)}) %collective-permute-start.22) | collective-permute-done | bytes 524320 | tf_op jit(solution)/shard_map/ppermute | solution.py:281
  124.4 1.3 collective-permute-start.24
  125.7 1.3 collective-permute-start.26
  127.2 1.0 convert_add_fusion.refs_0_
  128.2 1.6 collective-permute-done.18.peer_ref
  129.8 1.7 collective-permute-start.19
  132.2 1.7 collective-permute-start.16
  134.8 6.6 %update_trailing.2 = bf16[3,256,768]{2,1,0:T(8,128)(2,1)} custom-call(s32[2]{0:T(128)} %pad_add_fusion.ids_ref, s32[4,4,3]{2,1,0:T(4,128)} %bitcast.32, bf16[3,256,768]{2,1,0:T(8,128)(2,1)} %get-tuple-element.75.keep_ref, bf16[3,256,768]{2,1,0:T(8,128)(2,1)} %copy-done.25, bf16[3,256,1024]{2,1,0:T(8,128)(2,1)} %copy-done.2, bf16[256,1024]{1,0:T(8,128)(2,1)} %copy-done.9, ...), custom_call_target="tpu_custom_call" | custom-call | flops 4000000000 | bytes 12000000 | tf_op jit(solution)/shard_map/update_trailing/pallas_call | solution.py:659
  141.5 1.1 collective-permute-done.19.refs_4_
  143.5 1.6 collective-permute-start.33
  147.4 2.7 %collective-permute-done.33.refs_6_ = f32[128,512]{1,0:T(8,128)S(1)} collective-permute-done((f32[128,512]{1,0:T(8,128)}, f32[128,512]{1,0:T(8,128)S(1)}, u32[]{:S(2)}, u32[]{:S(2)}) %collective-permute-start.33) | collective-permute-done | bytes 262176 | tf_op jit(solution)/shard_map/ppermute | solution.py:281
  150.0 2.4 %collective-permute-done.34.refs_7_ = f32[128,512]{1,0:T(8,128)S(1)} collective-permute-done((f32[128,512]{1,0:T(8,128)}, f32[128,512]{1,0:T(8,128)S(1)}, u32[]{:S(2)}, u32[]{:S(2)}) %collective-permute-start.34) | collective-permute-done | bytes 262176 | tf_op jit(solution)/shard_map/ppermute | solution.py:281
  153.1 1.6 collective-permute-start.28
  154.7 1.5 collective-permute-start.29
  156.2 1.6 collective-permute-start.38
  158.2 17.8 %cholesky_first.3 = (f32[1024,512]{1,0:T(8,128)S(1)}, f32[2,256,256]{2,1,0:T(8,128)S(1)}, f32[512,512]{1,0:T(8,128)S(1)}) custom-call(s32[2]{0:T(128)S(1)} %copy-done.7, f32[256,512]{1,0:T(8,128)S(1)} %convert_add_fusion.refs_0_, f32[256,512]{1,0:T(8,128)S(1)} %collective-permute-done.30.refs_1_, f32[256,512]{1,0:T(8,128)S(1)} %collective-permute-done.20.refs_2_, ...), custom_call_target="tpu_custom_call" | custom-call | flops 20000000000 | bytes 50000000 | tf_op jit(solution)/shard_map/cholesky_first/pallas_call | solution.py:246
  176.0 15.2 %cholesky_second.3 = (f32[512,512]{1,0:T(8,128)S(1)}, f32[2,256,256]{2,1,0:T(8,128)S(1)}) custom-call(f32[512,512]{1,0:T(8,128)S(1)} %get-tuple-element.85.rest_ref), custom_call_target="tpu_custom_call" | custom-call | flops 20000000000 | bytes 50000000 | tf_op jit(solution)/shard_map/cholesky_second/pallas_call | solution.py:264
  191.2 7.6 %panel_two.1 = (f32[4,256,256]{2,1,0:T(8,128)}, bf16[3,256,1024]{2,1,0:T(8,128)(2,1)S(1)}, bf16[256,1024]{1,0:T(8,128)(2,1)S(1)}) custom-call(s32[2]{0:T(128)S(1)} %copy-done.7, f32[768,256]{1,0:T(8,128)S(1)} %bitcast.29, bf16[768,256]{1,0:T(8,128)(2,1)S(1)} %collective-permute-done.27.x_ref, bf16[768,256]{1,0:T(8,128)(2,1)S(1)} %collective-permute-done.28.z_ref, ...), custom_call_target="tpu_custom_call" | custom-call | flops 1000000000 | bytes 1000000 | tf_op jit(solution)/shard_map/panel_two/pallas_call | solution.py:549
  198.8 1.1 copy-done.8
  201.7 6.6 %update_trailing.3.near_ref = bf16[3,256,768]{2,1,0:T(8,128)(2,1)} custom-call(s32[2]{0:T(128)} %pad_add_fusion.ids_ref, s32[4,4,3]{2,1,0:T(4,128)} %bitcast.33, bf16[3,256,768]{2,1,0:T(8,128)(2,1)} %get-tuple-element.90.keep_ref, bf16[3,256,768]{2,1,0:T(8,128)(2,1)} %copy-done.27, bf16[3,256,1024]{2,1,0:T(8,128)(2,1)} %copy-done.2, ...), custom_call_target="tpu_custom_call" | custom-call | flops 4000000000 | bytes 12000000 | tf_op jit(solution)/shard_map/update_trailing/pallas_call | solution.py:659
  208.3 4.6 %collective-permute-done.40.refs_2_ = bf16[256,1024]{1,0:T(8,128)(2,1)S(1)} collective-permute-done((bf16[256,1024]{1,0:T(8,128)(2,1)S(1)}, bf16[256,1024]{1,0:T(8,128)(2,1)S(1)}, u32[]{:S(2)}, u32[]{:S(2)}) %collective-permute-start.40) | collective-permute-done | bytes 524320 | tf_op jit(solution)/shard_map/ppermute | solution.py:281
  212.9 1.9 collective-permute-done.41.refs_3_
  215.6 6.3 %update_two.1 = bf16[3,256,768]{2,1,0:T(8,128)(2,1)} custom-call(s32[2]{0:T(128)} %pad_add_fusion.ids_ref, bf16[3,256,768]{2,1,0:T(8,128)(2,1)} %update_trailing.3.near_ref, bf16[3,256,768]{2,1,0:T(8,128)(2,1)} %copy-done.26, bf16[3,256,1024]{2,1,0:T(8,128)(2,1)} %copy-done.8, bf16[256,1024]{1,0:T(8,128)(2,1)} %copy-done.11, bf16[256,1024]{1,0:T(8,128)(2,1)} %copy-done.34, ...), custom_call_target="tpu_custom_call" | custom-call | flops 2000000000 | bytes 10000000 | tf_op jit(solution)/shard_map/update_two/pallas_call | solution.py:690
  (142 shorter events, 17.7 us)
Async XLA Ops:
  0.6 40.3 %copy-start = (s32[4,1,12,4]{2,3,1,0:T(4,128)S(1)}, s32[4,1,12,4]{2,3,1,0:T(4,128)}, u32[]{:S(2)}) copy-start(s32[4,1,12,4]{2,3,1,0:T(4,128)} %param.12) | copy-start | bytes 2308
  5.8 20.8 %collective-permute-start = (bf16[256,1536]{1,0:T(8,128)(2,1)}, bf16[256,1536]{1,0:T(8,128)(2,1)S(1)}, u32[]{:S(2)}, u32[]{:S(2)}) collective-permute-start(bf16[256,1536]{1,0:T(8,128)(2,1)} %pick_pivot.1.refs_0_), channel_id=1, source_target_pairs={{0,4},{4,0},{8,12},{12,8},{16,20},{20,16},{24,28},{28,24},{1,5},{5... | collective-permute-start | bytes 2359304 | tf_op jit(solution)/shard_map/ppermute | solution.py:281
  8.9 19.2 %collective-permute-start.1 = (bf16[256,1536]{1,0:T(8,128)(2,1)}, bf16[256,1536]{1,0:T(8,128)(2,1)S(1)}, u32[]{:S(2)}, u32[]{:S(2)}) collective-permute-start(bf16[256,1536]{1,0:T(8,128)(2,1)} %pick_pivot.1.refs_0_), channel_id=1, source_target_pairs={{0,2},{1,3},{2,0},{3,1},{4,6},{5,7},{6,4},{7,5},{8,10},{9,11},{10,... | collective-permute-start | bytes 2359304 | tf_op jit(solution)/shard_map/ppermute | solution.py:281
  18.1 24.9 %copy-start.6 = (s32[2]{0:T(128)S(1)}, s32[2]{0:T(128)}, u32[]{:S(2)}) copy-start(s32[2]{0:T(128)} %pad_add_fusion.ids_ref) | copy-start | bytes 28
  28.9 9.9 %collective-permute-start.7 = (bf16[128,1536]{1,0:T(8,128)(2,1)}, bf16[128,1536]{1,0:T(8,128)(2,1)S(1)}, u32[]{:S(2)}, u32[]{:S(2)}) collective-permute-start(bf16[128,1536]{1,0:T(8,128)(2,1)} %slice.32), channel_id=1, source_target_pairs={{0,2},{1,3},{2,0},{3,1},{4,6},{5,7},{6,4},{7,5},{8,10},{9,11},{10,... | collective-permute-start | bytes 1179656 | tf_op jit(solution)/shard_map/ppermute | solution.py:281
  31.2 9.7 %collective-permute-start.6 = (bf16[128,1536]{1,0:T(8,128)(2,1)}, bf16[128,1536]{1,0:T(8,128)(2,1)}, u32[]{:S(2)}, u32[]{:S(2)}) collective-permute-start(bf16[128,1536]{1,0:T(8,128)(2,1)} %slice.31), channel_id=1, source_target_pairs={{0,4},{4,0},{8,12},{12,8},{16,20},{20,16},{24,28},{28,24},{1,5},{5... | collective-permute-start | bytes 1179656 | tf_op jit(solution)/shard_map/ppermute | solution.py:281
  31.7 9.6 %collective-permute-start.3 = (bf16[256,1536]{1,0:T(8,128)(2,1)S(1)}, bf16[256,1536]{1,0:T(8,128)(2,1)S(1)}, u32[]{:S(2)}, u32[]{:S(2)}) collective-permute-start(bf16[256,1536]{1,0:T(8,128)(2,1)S(1)} %copy-done.3), channel_id=1, source_target_pairs={{0,1},{1,0},{2,3},{3,2},{4,5},{5,4},{6,7},{7,6},{8,9},{9,8},{10,11... | collective-permute-start | bytes 2359304 | tf_op jit(solution)/shard_map/ppermute | solution.py:281
  31.7 11.3 %collective-permute-start.5 = (bf16[256,1536]{1,0:T(8,128)(2,1)S(1)}, bf16[256,1536]{1,0:T(8,128)(2,1)}, u32[]{:S(2)}, u32[]{:S(2)}) collective-permute-start(bf16[256,1536]{1,0:T(8,128)(2,1)S(1)} %collective-permute-done.refs_4_), channel_id=1, source_target_pairs={{0,1},{1,0},{2,3},{3,2},{4,5},{5,4},{6,7},{7,6},{8,9},{9,8},{10,11... | collective-permute-start | bytes 2359304 | tf_op jit(solution)/shard_map/ppermute | solution.py:281
  32.3 10.8 %collective-permute-start.4 = (bf16[256,1536]{1,0:T(8,128)(2,1)S(1)}, bf16[256,1536]{1,0:T(8,128)(2,1)}, u32[]{:S(2)}, u32[]{:S(2)}) collective-permute-start(bf16[256,1536]{1,0:T(8,128)(2,1)S(1)} %collective-permute-done.1.refs_2_), channel_id=1, source_target_pairs={{0,1},{1,0},{2,3},{3,2},{4,5},{5,4},{6,7},{7,6},{8,9},{9,8},{10,11... | collective-permute-start | bytes 2359304 | tf_op jit(solution)/shard_map/ppermute | solution.py:281
  38.8 3.2 %collective-permute-start.9 = (bf16[128,1536]{1,0:T(8,128)(2,1)S(1)}, bf16[128,1536]{1,0:T(8,128)(2,1)}, u32[]{:S(2)}, u32[]{:S(2)}) collective-permute-start(bf16[128,1536]{1,0:T(8,128)(2,1)S(1)} %collective-permute-done.7.refs_7_), channel_id=1, source_target_pairs={{0,1},{1,0},{2,3},{3,2},{4,5},{5,4},{6,7},{7,6},{8,9},{9,8},{10,11... | collective-permute-start | bytes 1179656 | tf_op jit(solution)/shard_map/ppermute | solution.py:281
  40.9 2.1 collective-permute-start.8
  41.3 21.7 %copy-start.13 = (bf16[3,256,512]{2,1,0:T(8,128)(2,1)S(1)}, bf16[3,256,512]{2,1,0:T(8,128)(2,1)}, u32[]{:S(2)}) copy-start(bf16[3,256,512]{2,1,0:T(8,128)(2,1)} %get-tuple-element.50) | copy-start | bytes 2359300
  41.3 21.7 %collective-permute-start.2 = (bf16[3,256,512]{2,1,0:T(8,128)(2,1)}, bf16[3,256,512]{2,1,0:T(8,128)(2,1)S(1)}, u32[]{:S(2)}, u32[]{:S(2)}) collective-permute-start(bf16[3,256,512]{2,1,0:T(8,128)(2,1)} %get-tuple-element.53), channel_id=1, source_target_pairs={{0,4},{4,0},{8,12},{12,8},{16,20},{20,16},{24,28},{28,24},{1,5},{5... | collective-permute-start | bytes 2359304 | tf_op jit(solution)/shard_map/ppermute | solution.py:281
  63.5 20.4 %collective-permute-start.10 = (bf16[3,256,512]{2,1,0:T(8,128)(2,1)S(1)}, bf16[3,256,512]{2,1,0:T(8,128)(2,1)S(1)}, u32[]{:S(2)}, u32[]{:S(2)}) collective-permute-start(bf16[3,256,512]{2,1,0:T(8,128)(2,1)S(1)} %get-tuple-element.97), channel_id=1, source_target_pairs={{0,4},{4,0},{8,12},{12,8},{16,20},{20,16},{24,28},{28,24},{1,5},{5... | collective-permute-start | bytes 2359304 | tf_op jit(solution)/shard_map/ppermute | solution.py:281
  79.3 20.7 %collective-permute-start.11 = (bf16[3,256,512]{2,1,0:T(8,128)(2,1)S(1)}, bf16[3,256,512]{2,1,0:T(8,128)(2,1)S(1)}, u32[]{:S(2)}, u32[]{:S(2)}) collective-permute-start(bf16[3,256,512]{2,1,0:T(8,128)(2,1)S(1)} %copy-done.28), channel_id=1, source_target_pairs={{0,4},{4,0},{8,12},{12,8},{16,20},{20,16},{24,28},{28,24},{1,5},{5... | collective-permute-start | bytes 2359304 | tf_op jit(solution)/shard_map/ppermute | solution.py:281
  83.9 21.7 %copy-start.23 = (bf16[3,256,768]{2,1,0:T(8,128)(2,1)S(1)}, bf16[3,256,768]{2,1,0:T(8,128)(2,1)}, u32[]{:S(2)}) copy-start(bf16[3,256,768]{2,1,0:T(8,128)(2,1)} %get-tuple-element.73) | copy-start | bytes 3538948
  93.2 25.5 %copy-start.9 = (bf16[256,1024]{1,0:T(8,128)(2,1)}, bf16[256,1024]{1,0:T(8,128)(2,1)S(1)}, u32[]{:S(2)}) copy-start(bf16[256,1024]{1,0:T(8,128)(2,1)S(1)} %get-tuple-element.78.refs_0_) | copy-start | bytes 1572868
  93.2 31.2 %copy-start.10 = (bf16[256,1024]{1,0:T(8,128)(2,1)}, bf16[256,1024]{1,0:T(8,128)(2,1)S(1)}, u32[]{:S(2)}) copy-start(bf16[256,1024]{1,0:T(8,128)(2,1)S(1)} %get-tuple-element.80.refs_4_) | copy-start | bytes 1572868
  93.2 11.1 %collective-permute-start.13 = (bf16[256,1024]{1,0:T(8,128)(2,1)S(1)}, bf16[256,1024]{1,0:T(8,128)(2,1)S(1)}, u32[]{:S(2)}, u32[]{:S(2)}) collective-permute-start(bf16[256,1024]{1,0:T(8,128)(2,1)S(1)} %get-tuple-element.66.refs_0_), channel_id=1, source_target_pairs={{0,2},{2,0},{5,7},{7,5},{8,10},{10,8},{13,15},{15,13},{16,18},{18,... | collective-permute-start | bytes 1572872 | tf_op jit(solution)/shard_map/ppermute | solution.py:292
  95.7 14.1 %collective-permute-start.12 = (bf16[256,1024]{1,0:T(8,128)(2,1)S(1)}, bf16[256,1024]{1,0:T(8,128)(2,1)S(1)}, u32[]{:S(2)}, u32[]{:S(2)}) collective-permute-start(bf16[256,1024]{1,0:T(8,128)(2,1)S(1)} %get-tuple-element.66.refs_0_), channel_id=1, source_target_pairs={{0,1},{2,3},{5,4},{7,6},{8,9},{10,11},{13,12},{15,14},{16,17},{18,... | collective-permute-start | bytes 1572872 | tf_op jit(solution)/shard_map/ppermute | solution.py:292
  104.3 5.4 %collective-permute-start.14 = (bf16[256,1024]{1,0:T(8,128)(2,1)S(1)}, bf16[256,1024]{1,0:T(8,128)(2,1)S(1)}, u32[]{:S(2)}, u32[]{:S(2)}) collective-permute-start(bf16[256,1024]{1,0:T(8,128)(2,1)S(1)} %collective-permute-done.13.refs_2_), channel_id=1, source_target_pairs={{0,1},{2,3},{5,4},{7,6},{8,9},{10,11},{13,12},{15,14},{16,17},{18,... | collective-permute-start | bytes 1572872 | tf_op jit(solution)/shard_map/ppermute | solution.py:292
  105.6 24.2 %collective-permute-start.18 = (bf16[3,256,768]{2,1,0:T(8,128)(2,1)S(1)}, bf16[3,256,768]{2,1,0:T(8,128)(2,1)S(1)}, u32[]{:S(2)}, u32[]{:S(2)}) collective-permute-start(bf16[3,256,768]{2,1,0:T(8,128)(2,1)S(1)} %copy-done.23), channel_id=1, source_target_pairs={{0,4},{4,0},{8,12},{12,8},{16,20},{20,16},{24,28},{28,24},{1,5},{5... | collective-permute-start | bytes 3538952 | tf_op jit(solution)/shard_map/ppermute | solution.py:281
  105.7 13.1 %collective-permute-start.25 = (bf16[256,1024]{1,0:T(8,128)(2,1)S(1)}, bf16[256,1024]{1,0:T(8,128)(2,1)}, u32[]{:S(2)}, u32[]{:S(2)}) collective-permute-start(bf16[256,1024]{1,0:T(8,128)(2,1)S(1)} %get-tuple-element.80.refs_4_), channel_id=1, source_target_pairs={{0,2},{2,0},{5,7},{7,5},{8,10},{10,8},{13,15},{15,13},{16,18},{18,... | collective-permute-start | bytes 1572872 | tf_op jit(solution)/shard_map/ppermute | solution.py:292
  108.1 16.2 %collective-permute-start.22 = (bf16[256,1024]{1,0:T(8,128)(2,1)S(1)}, bf16[256,1024]{1,0:T(8,128)(2,1)}, u32[]{:S(2)}, u32[]{:S(2)}) collective-permute-start(bf16[256,1024]{1,0:T(8,128)(2,1)S(1)} %get-tuple-element.78.refs_0_), channel_id=1, source_target_pairs={{0,2},{1,3},{2,0},{3,1},{4,6},{5,7},{6,4},{7,5},{8,10},{9,11},{10,... | collective-permute-start | bytes 1572872 | tf_op jit(solution)/shard_map/ppermute | solution.py:281
  116.2 10.8 %collective-permute-start.15 = (bf16[256,512]{1,0:T(8,128)(2,1)}, bf16[256,512]{1,0:T(8,128)(2,1)S(1)}, u32[]{:S(2)}, u32[]{:S(2)}) collective-permute-start(bf16[256,512]{1,0:T(8,128)(2,1)} %get-tuple-element.70), channel_id=1, source_target_pairs={{0,8},{4,12},{8,0},{12,4},{16,24},{20,28},{24,16},{28,20},{1,9},{5... | collective-permute-start | bytes 786440 | tf_op jit(solution)/shard_map/ppermute | solution.py:281
  117.9 7.8 %collective-permute-start.17 = (bf16[256,256]{1,0:T(8,128)(2,1)S(1)}, bf16[256,256]{1,0:T(8,128)(2,1)S(1)}, u32[]{:S(2)}, u32[]{:S(2)}) collective-permute-start(bf16[256,256]{1,0:T(8,128)(2,1)S(1)} %slice_bitcast_fusion), channel_id=1, source_target_pairs={{0,8},{4,12},{8,0},{12,4},{16,24},{20,28},{24,16},{28,20},{1,9},{5... | collective-permute-start | bytes 393224 | tf_op jit(solution)/shard_map/ppermute | solution.py:281
  118.8 12.8 %collective-permute-start.21 = (bf16[256,1024]{1,0:T(8,128)(2,1)S(1)}, bf16[256,1024]{1,0:T(8,128)(2,1)S(1)}, u32[]{:S(2)}, u32[]{:S(2)}) collective-permute-start(bf16[256,1024]{1,0:T(8,128)(2,1)S(1)} %get-tuple-element.78.refs_0_), channel_id=1, source_target_pairs={{0,1},{1,0},{2,3},{3,2},{4,5},{5,4},{6,7},{7,6},{8,9},{9,8},{10,11... | collective-permute-start | bytes 1572872 | tf_op jit(solution)/shard_map/ppermute | solution.py:281
  124.4 7.8 %collective-permute-start.24 = (bf16[256,1024]{1,0:T(8,128)(2,1)S(1)}, bf16[256,1024]{1,0:T(8,128)(2,1)S(1)}, u32[]{:S(2)}, u32[]{:S(2)}) collective-permute-start(bf16[256,1024]{1,0:T(8,128)(2,1)S(1)} %get-tuple-element.80.refs_4_), channel_id=1, source_target_pairs={{0,1},{2,3},{5,4},{7,6},{8,9},{10,11},{13,12},{15,14},{16,17},{18,... | collective-permute-start | bytes 1572872 | tf_op jit(solution)/shard_map/ppermute | solution.py:292
  125.7 8.1 %collective-permute-start.26 = (bf16[256,1024]{1,0:T(8,128)(2,1)}, bf16[256,1024]{1,0:T(8,128)(2,1)S(1)}, u32[]{:S(2)}, u32[]{:S(2)}) collective-permute-start(bf16[256,1024]{1,0:T(8,128)(2,1)} %collective-permute-done.25.refs_6_), channel_id=1, source_target_pairs={{0,1},{2,3},{5,4},{7,6},{8,9},{10,11},{13,12},{15,14},{16,17},{18,... | collective-permute-start | bytes 1572872 | tf_op jit(solution)/shard_map/ppermute | solution.py:292
  127.1 6.8 %collective-permute-start.23 = (bf16[256,1024]{1,0:T(8,128)(2,1)}, bf16[256,1024]{1,0:T(8,128)(2,1)S(1)}, u32[]{:S(2)}, u32[]{:S(2)}) collective-permute-start(bf16[256,1024]{1,0:T(8,128)(2,1)} %collective-permute-done.22.refs_2_), channel_id=1, source_target_pairs={{0,1},{1,0},{2,3},{3,2},{4,5},{5,4},{6,7},{7,6},{8,9},{9,8},{10,11... | collective-permute-start | bytes 1572872 | tf_op jit(solution)/shard_map/ppermute | solution.py:281
  129.8 12.8 %collective-permute-start.19 = (f32[256,512]{1,0:T(8,128)S(1)}, f32[256,512]{1,0:T(8,128)S(1)}, u32[]{:S(2)}, u32[]{:S(2)}) collective-permute-start(f32[256,512]{1,0:T(8,128)S(1)} %convert_add_fusion.refs_0_), channel_id=1, source_target_pairs={{0,4},{4,0},{8,12},{12,8},{16,20},{20,16},{24,28},{28,24},{1,5},{5... | collective-permute-start | bytes 1572872 | tf_op jit(solution)/shard_map/ppermute | solution.py:281
  131.5 11.2 %collective-permute-start.20 = (f32[256,512]{1,0:T(8,128)S(1)}, f32[256,512]{1,0:T(8,128)S(1)}, u32[]{:S(2)}, u32[]{:S(2)}) collective-permute-start(f32[256,512]{1,0:T(8,128)S(1)} %convert_add_fusion.refs_0_), channel_id=1, source_target_pairs={{0,2},{1,3},{2,0},{3,1},{4,6},{5,7},{6,4},{7,5},{8,10},{9,11},{10,... | collective-permute-start | bytes 1572872 | tf_op jit(solution)/shard_map/ppermute | solution.py:281
  132.2 15.1 %collective-permute-start.16 = (bf16[3,256,256]{2,1,0:T(8,128)(2,1)}, bf16[3,256,256]{2,1,0:T(8,128)(2,1)S(1)}, u32[]{:S(2)}, u32[]{:S(2)}) collective-permute-start(bf16[3,256,256]{2,1,0:T(8,128)(2,1)} %get-tuple-element.71), channel_id=1, source_target_pairs={{0,8},{4,12},{8,0},{12,4},{16,24},{20,28},{24,16},{28,20},{1,9},{5... | collective-permute-start | bytes 1179656 | tf_op jit(solution)/shard_map/ppermute | solution.py:281
  143.5 6.6 %collective-permute-start.33 = (f32[128,512]{1,0:T(8,128)}, f32[128,512]{1,0:T(8,128)S(1)}, u32[]{:S(2)}, u32[]{:S(2)}) collective-permute-start(f32[128,512]{1,0:T(8,128)} %slice.38), channel_id=1, source_target_pairs={{0,4},{4,0},{8,12},{12,8},{16,20},{20,16},{24,28},{28,24},{1,5},{5... | collective-permute-start | bytes 786440 | tf_op jit(solution)/shard_map/ppermute | solution.py:281
  145.8 6.6 %collective-permute-start.34 = (f32[128,512]{1,0:T(8,128)}, f32[128,512]{1,0:T(8,128)S(1)}, u32[]{:S(2)}, u32[]{:S(2)}) collective-permute-start(f32[128,512]{1,0:T(8,128)} %slice.39), channel_id=1, source_target_pairs={{0,2},{1,3},{2,0},{3,1},{4,6},{5,7},{6,4},{7,5},{8,10},{9,11},{10,... | collective-permute-start | bytes 786440 | tf_op jit(solution)/shard_map/ppermute | solution.py:281
  146.7 6.0 %collective-permute-start.30 = (f32[256,512]{1,0:T(8,128)S(1)}, f32[256,512]{1,0:T(8,128)S(1)}, u32[]{:S(2)}, u32[]{:S(2)}) collective-permute-start(f32[256,512]{1,0:T(8,128)S(1)} %convert_add_fusion.refs_0_), channel_id=1, source_target_pairs={{0,1},{1,0},{2,3},{3,2},{4,5},{5,4},{6,7},{7,6},{8,9},{9,8},{10,11... | collective-permute-start | bytes 1572872 | tf_op jit(solution)/shard_map/ppermute | solution.py:281
  146.8 6.4 %collective-permute-start.31 = (f32[256,512]{1,0:T(8,128)S(1)}, f32[256,512]{1,0:T(8,128)S(1)}, u32[]{:S(2)}, u32[]{:S(2)}) collective-permute-start(f32[256,512]{1,0:T(8,128)S(1)} %collective-permute-done.20.refs_2_), channel_id=1, source_target_pairs={{0,1},{1,0},{2,3},{3,2},{4,5},{5,4},{6,7},{7,6},{8,9},{9,8},{10,11... | collective-permute-start | bytes 1572872 | tf_op jit(solution)/shard_map/ppermute | solution.py:281
  147.3 7.4 %collective-permute-start.32 = (f32[256,512]{1,0:T(8,128)S(1)}, f32[256,512]{1,0:T(8,128)S(1)}, u32[]{:S(2)}, u32[]{:S(2)}) collective-permute-start(f32[256,512]{1,0:T(8,128)S(1)} %collective-permute-done.19.refs_4_), channel_id=1, source_target_pairs={{0,1},{1,0},{2,3},{3,2},{4,5},{5,4},{6,7},{7,6},{8,9},{9,8},{10,11... | collective-permute-start | bytes 1572872 | tf_op jit(solution)/shard_map/ppermute | solution.py:281
  150.0 6.2 %collective-permute-start.35 = (f32[128,512]{1,0:T(8,128)S(1)}, f32[128,512]{1,0:T(8,128)S(1)}, u32[]{:S(2)}, u32[]{:S(2)}) collective-permute-start(f32[128,512]{1,0:T(8,128)S(1)} %collective-permute-done.33.refs_6_), channel_id=1, source_target_pairs={{0,1},{1,0},{2,3},{3,2},{4,5},{5,4},{6,7},{7,6},{8,9},{9,8},{10,11... | collective-permute-start | bytes 786440 | tf_op jit(solution)/shard_map/ppermute | solution.py:281
  152.4 5.4 %collective-permute-start.36 = (f32[128,512]{1,0:T(8,128)S(1)}, f32[128,512]{1,0:T(8,128)S(1)}, u32[]{:S(2)}, u32[]{:S(2)}) collective-permute-start(f32[128,512]{1,0:T(8,128)S(1)} %collective-permute-done.34.refs_7_), channel_id=1, source_target_pairs={{0,1},{1,0},{2,3},{3,2},{4,5},{5,4},{6,7},{7,6},{8,9},{9,8},{10,11... | collective-permute-start | bytes 786440 | tf_op jit(solution)/shard_map/ppermute | solution.py:281
  152.7 38.5 %collective-permute-start.27 = (bf16[768,256]{1,0:T(8,128)(2,1)S(1)}, bf16[768,256]{1,0:T(8,128)(2,1)S(1)}, u32[]{:S(2)}, u32[]{:S(2)}) collective-permute-start(bf16[768,256]{1,0:T(8,128)(2,1)S(1)} %bitcast_convert_fusion), channel_id=1, source_target_pairs={{0,4},{4,0},{8,12},{12,8},{16,20},{20,16},{24,28},{28,24},{1,5},{5... | collective-permute-start | bytes 1179656 | tf_op jit(solution)/shard_map/ppermute | solution.py:281
  153.1 38.0 %collective-permute-start.28 = (bf16[768,256]{1,0:T(8,128)(2,1)S(1)}, bf16[768,256]{1,0:T(8,128)(2,1)S(1)}, u32[]{:S(2)}, u32[]{:S(2)}) collective-permute-start(bf16[768,256]{1,0:T(8,128)(2,1)S(1)} %bitcast_convert_fusion), channel_id=1, source_target_pairs={{0,8},{4,12},{8,0},{12,4},{16,24},{20,28},{24,16},{28,20},{1,9},{5... | collective-permute-start | bytes 1179656 | tf_op jit(solution)/shard_map/ppermute | solution.py:281
  154.7 36.5 %collective-permute-start.29 = (bf16[768,256]{1,0:T(8,128)(2,1)S(1)}, bf16[768,256]{1,0:T(8,128)(2,1)S(1)}, u32[]{:S(2)}, u32[]{:S(2)}) collective-permute-start(bf16[768,256]{1,0:T(8,128)(2,1)S(1)} %bitcast_convert_fusion), channel_id=1, source_target_pairs={{0,12},{4,8},{8,4},{12,0},{16,28},{20,24},{24,20},{28,16},{1,13},{... | collective-permute-start | bytes 1179656 | tf_op jit(solution)/shard_map/ppermute | solution.py:281
  156.2 56.6 %collective-permute-start.38 = (bf16[3,256,768]{2,1,0:T(8,128)(2,1)S(1)}, bf16[3,256,768]{2,1,0:T(8,128)(2,1)S(1)}, u32[]{:S(2)}, u32[]{:S(2)}) collective-permute-start(bf16[3,256,768]{2,1,0:T(8,128)(2,1)S(1)} %copy-done.24), channel_id=1, source_target_pairs={{0,8},{4,12},{8,0},{12,4},{16,24},{20,28},{24,16},{28,20},{1,9},{5... | collective-permute-start | bytes 3538952 | tf_op jit(solution)/shard_map/ppermute | solution.py:281
  157.8 42.8 %collective-permute-start.37 = (bf16[3,256,768]{2,1,0:T(8,128)(2,1)S(1)}, bf16[3,256,768]{2,1,0:T(8,128)(2,1)S(1)}, u32[]{:S(2)}, u32[]{:S(2)}) collective-permute-start(bf16[3,256,768]{2,1,0:T(8,128)(2,1)S(1)} %copy-done.22), channel_id=1, source_target_pairs={{0,4},{4,0},{8,12},{12,8},{16,20},{20,16},{24,28},{28,24},{1,5},{5... | collective-permute-start | bytes 3538952 | tf_op jit(solution)/shard_map/ppermute | solution.py:281
  199.9 12.9 %collective-permute-start.40 = (bf16[256,1024]{1,0:T(8,128)(2,1)S(1)}, bf16[256,1024]{1,0:T(8,128)(2,1)S(1)}, u32[]{:S(2)}, u32[]{:S(2)}) collective-permute-start(bf16[256,1024]{1,0:T(8,128)(2,1)S(1)} %get-tuple-element.95.refs_0_), channel_id=1, source_target_pairs={{0,2},{1,3},{2,0},{3,1},{4,6},{5,7},{6,4},{7,5},{8,10},{9,11},{10,... | collective-permute-start | bytes 1572872 | tf_op jit(solution)/shard_map/ppermute | solution.py:281
  200.6 12.3 %collective-permute-start.39 = (bf16[256,1024]{1,0:T(8,128)(2,1)S(1)}, bf16[256,1024]{1,0:T(8,128)(2,1)S(1)}, u32[]{:S(2)}, u32[]{:S(2)}) collective-permute-start(bf16[256,1024]{1,0:T(8,128)(2,1)S(1)} %get-tuple-element.95.refs_0_), channel_id=1, source_target_pairs={{0,1},{1,0},{2,3},{3,2},{4,5},{5,4},{6,7},{7,6},{8,9},{9,8},{10,11... | collective-permute-start | bytes 1572872 | tf_op jit(solution)/shard_map/ppermute | solution.py:281
  212.8 2.0 collective-permute-start.41
  (30 other events, 198.8 us)
